TPU v7x, 32 devices: a whole 2x2x4 slice. The times are simulated.
32 devices in a mesh: groups: 2 (over y), ed: 4 (over z), dp: 2 (over x), tp: 2 (over core).
Axes of the slice: x: 2, y: 2, z: 4, core: 2. Of those that a mesh axis runs over, the one named last changes fastest.
Arguments:
- tokens: bfloat16 [1024, 2048], P(('groups', 'ed')), parts along dimension 0, may hold values from -6 to 6
- expert_ids: int32 [1024, 2], P(('groups', 'ed')), parts along dimension 0, may hold values from 0 to 7, all different within a row; in each aligned block of 128 rows (0 to 127, 128 to 255, ...) at most 48 rows name the same one
- gates: bfloat16 [1024, 2], P(('groups', 'ed')), parts along dimension 0, may hold values from 0.099609375 to 1
- out_grad: bfloat16 [1024, 2048], P(('groups', 'ed')), parts along dimension 0, may hold values from -6 to 6
- gate_weight: bfloat16 [2048, 57344], P(None, ('ed', 'dp', 'tp')), may hold values from -0.125 to 0.125
- up_weight: bfloat16 [2048, 57344], P(None, ('ed', 'dp', 'tp')), may hold values from -0.125 to 0.125
- down_weight: bfloat16 [57344, 2048], P(('ed', 'dp', 'tp')), may hold values from -0.0625 to 0.0625
Outputs:
- layer_out: bfloat16 [1024, 2048], P(('groups', 'ed')), parts along dimension 0
- token_grad: bfloat16 [1024, 2048], P(('groups', 'ed')), parts along dimension 0
- gate_grad: float32 [1024, 2], P(('groups', 'ed')), parts along dimension 0
- gate_weight_grad: bfloat16 [4096, 57344], P('groups', ('ed', 'dp', 'tp')), parts along dimension 0
- up_weight_grad: bfloat16 [4096, 57344], P('groups', ('ed', 'dp', 'tp')), parts along dimension 0
- down_weight_grad: bfloat16 [114688, 2048], P(('groups', 'ed', 'dp', 'tp')), parts along dimension 0
There are 2 independent parts, one for each index of `groups`. A program takes and returns all parts, laid end to end along the dimension named above; an argument that names none is the same for every part. Nothing has to cross between parts.
Inputs may be any that keep to these rules, and one draw needn't show every extreme that they name: `expert_ids`: each row names 2 different experts. Among the 128 rows of one index of ed (aligned blocks of rows) no expert is named by more than 48 rows, and in every draw some expert is named by exactly 48 rows of some block.
All inputs are finite; a program needn't handle non-finite values.
Results may differ from a plain program's by a relative error of at most 0.0058.
Values may be sent and summed in bfloat16 or wider, within the bound.
No kernel may reach another device: no remote copies, remote signals or barrier semaphores. Data moves between devices by JAX's collectives and lax.ppermute only.
A program may use at most 192 MiB of HBM per device.

v0:
```python
import jax
import jax.numpy as jnp
from jax import lax
from jax.sharding import PartitionSpec as P

FF = 7168
EXPERTS = 8
CAP = 48


def contract_last(left_mat, right_mat):
    return lax.dot_general(
        left_mat, right_mat, (((1,), (1,)), ((), ())), preferred_element_type=jnp.float32
    )


def contract_first(left_mat, right_mat):
    return lax.dot_general(
        left_mat, right_mat, (((0,), (0,)), ((), ())), preferred_element_type=jnp.float32
    )


def expert_rows(rows_in, rows_grad, scale_col, gate_cols, up_cols, down_rows):
    pre_gate = jnp.dot(rows_in, gate_cols, preferred_element_type=jnp.float32)
    pre_up = jnp.dot(rows_in, up_cols, preferred_element_type=jnp.float32)
    logistic = jax.nn.sigmoid(pre_gate)
    silu_gate = pre_gate * logistic
    hidden = (silu_gate * pre_up).astype(jnp.bfloat16)
    partial_out = jnp.dot(hidden, down_rows, preferred_element_type=jnp.float32)
    back_rows = contract_last(rows_grad, down_rows)
    scale_two = scale_col[:, None]
    hidden_grad = scale_two * back_rows
    gate_pre_grad = (hidden_grad * pre_up * logistic * (1.0 + pre_gate * (1.0 - logistic))).astype(
        jnp.bfloat16
    )
    up_pre_grad = (hidden_grad * silu_gate).astype(jnp.bfloat16)
    partial_input = contract_last(gate_pre_grad, gate_cols) + contract_last(up_pre_grad, up_cols)
    out_scaled = (scale_two * rows_grad.astype(jnp.float32)).astype(jnp.bfloat16)
    grad_gate = contract_first(rows_in, gate_pre_grad)
    grad_up = contract_first(rows_in, up_pre_grad)
    grad_down = contract_first(hidden, out_scaled)
    return (partial_out, partial_input, grad_gate, grad_up, grad_down)


def router_rows(placed_full, matches, gate_slot):
    gate_token = jnp.einsum("ect,ec->et", placed_full, gate_slot, precision=lax.Precision.HIGHEST)
    return jnp.einsum(
        "etk,et->kt", matches.astype(jnp.float32), gate_token, precision=lax.Precision.HIGHEST
    )


def on_device(tokens, expert_ids, gates, out_grad, gate_weight, up_weight, down_weight):
    ed_count = lax.axis_size("ed")
    rep_count = lax.axis_size(("dp", "tp"))
    rep_index = lax.axis_index(("dp", "tp"))
    model_width = tokens.shape[1]
    hidden_dev = gate_weight.shape[1]
    owners = jnp.arange(ed_count, dtype=jnp.int32)
    dest_expert = (owners * rep_count + rep_index) * hidden_dev // FF
    expert_axis = jnp.arange(EXPERTS, dtype=jnp.int32)
    matches = expert_ids[None, :, :] == expert_axis[:, None, None]
    chosen = jnp.any(matches, axis=2).astype(jnp.int32)
    slot_of = jnp.cumsum(chosen, axis=1) - 1
    placed = (slot_of[:, None, :] == jnp.arange(CAP, dtype=jnp.int32)[None, :, None]) & (
        chosen[:, None, :] > 0
    )
    placed_low = placed.astype(jnp.bfloat16)
    placed_full = placed.astype(jnp.float32)
    weight_tok = jnp.sum(jnp.where(matches, gates[None, :, :], jnp.zeros((), jnp.bfloat16)), axis=2)
    send_rows = jnp.einsum(
        "ect,td->ecd", placed_low, tokens, preferred_element_type=jnp.float32
    ).astype(jnp.bfloat16)
    send_grads = jnp.einsum(
        "ect,td->ecd", placed_low, out_grad, preferred_element_type=jnp.float32
    ).astype(jnp.bfloat16)
    send_scale = jnp.einsum(
        "ect,et->ec", placed_low, weight_tok, preferred_element_type=jnp.float32
    ).astype(jnp.bfloat16)
    weighted = placed_full * send_scale.astype(jnp.float32)[:, :, None]
    exp_rows, exp_grads, exp_scale = (
        lax.all_to_all(
            jnp.take(send_rows, dest_expert, axis=0), "ed", split_axis=0, concat_axis=0, tiled=True
        ),
        lax.all_to_all(
            jnp.take(send_grads, dest_expert, axis=0), "ed", split_axis=0, concat_axis=0, tiled=True
        ),
        lax.all_to_all(
            jnp.take(send_scale, dest_expert, axis=0), "ed", split_axis=0, concat_axis=0, tiled=True
        ),
    )
    partial_out, partial_input, grad_gate, grad_up, grad_down = expert_rows(
        exp_rows.reshape(-1, model_width),
        exp_grads.reshape(-1, model_width),
        exp_scale.reshape(-1).astype(jnp.float32),
        gate_weight,
        up_weight,
        down_weight,
    )
    out_slots = partial_out.reshape(ed_count, CAP, model_width)
    input_slots = partial_input.reshape(ed_count, CAP, model_width)
    back_out, back_input = (
        lax.all_to_all(out_slots, "ed", split_axis=0, concat_axis=0, tiled=True),
        lax.all_to_all(input_slots, "ed", split_axis=0, concat_axis=0, tiled=True),
    )
    owner_map = (dest_expert[None, :] == expert_axis[:, None]).astype(jnp.float32)
    expert_out = jnp.einsum("ej,jcd->ecd", owner_map, back_out, precision=lax.Precision.HIGHEST)
    expert_input = jnp.einsum("ej,jcd->ecd", owner_map, back_input, precision=lax.Precision.HIGHEST)
    layer_full = jnp.einsum("ect,ecd->td", weighted, expert_out, precision=lax.Precision.HIGHEST)
    input_full = jnp.einsum(
        "ect,ecd->td", placed_full, expert_input, precision=lax.Precision.HIGHEST
    )
    gate_slot = jnp.sum(expert_out * send_grads.astype(jnp.float32), axis=2)
    gate_full = router_rows(placed_full, matches, gate_slot)
    layer_piece, input_piece, gate_piece = (
        lax.psum_scatter(layer_full, ("dp", "tp"), scatter_dimension=1, tiled=True),
        lax.psum_scatter(input_full, ("dp", "tp"), scatter_dimension=1, tiled=True),
        lax.psum_scatter(gate_full, ("dp", "tp"), scatter_dimension=1, tiled=True),
    )
    layer_all, input_all, gate_all = (
        lax.all_gather(layer_piece, ("dp", "tp"), axis=1, tiled=True),
        lax.all_gather(input_piece, ("dp", "tp"), axis=1, tiled=True),
        lax.all_gather(gate_piece, ("dp", "tp"), axis=1, tiled=True),
    )
    gate_grad = gate_all.T
    return (
        layer_all.astype(jnp.bfloat16),
        input_all.astype(jnp.bfloat16),
        gate_grad,
        grad_gate.astype(jnp.bfloat16),
        grad_up.astype(jnp.bfloat16),
        grad_down.astype(jnp.bfloat16),
    )


def solution(mesh):
    in_specs = (
        P(("groups", "ed"), None),
        P(("groups", "ed"), None),
        P(("groups", "ed"), None),
        P(("groups", "ed"), None),
        P(None, ("ed", "dp", "tp")),
        P(None, ("ed", "dp", "tp")),
        P(("ed", "dp", "tp"), None),
    )
    out_specs = (
        P(("groups", "ed"), None),
        P(("groups", "ed"), None),
        P(("groups", "ed"), None),
        P("groups", ("ed", "dp", "tp")),
        P("groups", ("ed", "dp", "tp")),
        P(("groups", "ed", "dp", "tp"), None),
    )
    return jax.shard_map(
        on_device, mesh=mesh, in_specs=in_specs, out_specs=out_specs, check_vma=False
    )
```

profile of v0, /device:TPU:0, one launch (start us, length us, event | category | flops | bytes accessed | tf_op | source)
XLA Modules:
  0.0 295.0 jit_solution(6763657128608919633)
XLA Ops:
  10.4 6.3 %all-to-all-start.2 = ((bf16[4,1,48]{2,1,0:T(2,128)(2,1)}), bf16[4,1,48]{2,1,0:T(2,128)(2,1)S(1)}, u32[]{:S(2)}, u32[]{:S(2)}) async-start(bf16[4,1,48]{2,1,0:T(2,128)(2,1)} %copy.47), calls=%async_computation.3 | async-start | bytes 4096 | tf_op jit(solution)/shard_map/all_to_all | solution.py:87
  17.3 2.0 copy.49
  19.4 1.7 convolution_convert_fusion.4
  21.1 2.0 gather_fusion.2
  23.1 2.0 gather_fusion.1
  26.4 5.1 %all-to-all-start = ((bf16[4,48,2048]{2,1,0:T(8,128)(2,1)}), bf16[4,48,2048]{2,1,0:T(8,128)(2,1)S(1)}, u32[]{:S(2)}, u32[]{:S(2)}) async-start(bf16[4,48,2048]{2,1,0:T(8,128)(2,1)} %get-tuple-element.15), calls=%async_computation | async-start | bytes 1572864 | tf_op jit(solution)/shard_map/all_to_all | solution.py:81
  31.6 19.4 %all-to-all-done = bf16[4,48,2048]{2,1,0:T(8,128)(2,1)S(1)} async-done(((bf16[4,48,2048]{2,1,0:T(8,128)(2,1)}), bf16[4,48,2048]{2,1,0:T(8,128)(2,1)S(1)}, u32[]{:S(2)}, u32[]{:S(2)}) %all-to-all-start) | async-done | bytes 786464 | tf_op jit(solution)/shard_map/all_to_all | solution.py:81
  51.1 4.0 %all-to-all-start.3 = ((bf16[4,48,2048]{2,1,0:T(8,128)(2,1)}), bf16[4,48,2048]{2,1,0:T(8,128)(2,1)S(1)}, u32[]{:S(2)}, u32[]{:S(2)}) async-start(bf16[4,48,2048]{2,1,0:T(8,128)(2,1)} %get-tuple-element.14), calls=%async_computation.4 | async-start | bytes 1572864 | tf_op jit(solution)/shard_map/all_to_all | solution.py:84
  55.1 9.7 %fusion.44 = f32[192,3584]{1,0:T(8,128)} fusion(bf16[192,2048]{1,0:T(8,128)(2,1)S(1)} %bitcast.62, bf16[2048,3584]{1,0:T(8,128)(2,1)} %param.14), kind=kOutput, calls=%fused_computation.66 | convolution fusion | flops 2818572288 | bytes 18219008 | tf_op jit(solution)/shard_map/dot_general | solution.py:25
  64.8 9.7 %fusion.43 = f32[192,3584]{1,0:T(8,128)} fusion(bf16[192,2048]{1,0:T(8,128)(2,1)S(1)} %bitcast.63, bf16[2048,3584]{1,0:T(8,128)(2,1)} %param.13), kind=kOutput, calls=%fused_computation.65 | convolution fusion | flops 2818572288 | bytes 18219008 | tf_op jit(solution)/shard_map/dot_general | solution.py:24
  74.7 17.1 %multiply_convert_fusion = (bf16[192,3584]{1,0:T(8,128)(2,1)}, bf16[192,3584]{1,0:T(8,128)(2,1)}, bf16[192,3584]{1,0:T(8,128)(2,1)}) fusion(f32[192,3584]{1,0:T(8,128)} %fusion.43, f32[192,3584]{1,0:T(8,128)} %fusion.44, bf16[192,2048]{1,0:T(8,128)(2,1)S(1)} %bitcast.66, bf16[3584,2048]{1,0:T(8,128)(2,1)} %param.15, f32[192]{0:T(256)S(1)} %reshape.149), kind=kOutput, calls=%fused_computation.14 | convolution fusion | flops 2829582336 | bytes 25101056 | tf_op jit(solution)/shard_map/dot_general | solution.py:12
  91.8 8.6 %fusion.46 = f32[192,2048]{1,0:T(8,128)S(1)} fusion(bf16[192,3584]{1,0:T(8,128)(2,1)} %get-tuple-element.10, bf16[2048,3584]{1,0:T(8,128)(2,1)} %param.13), kind=kOutput, calls=%fused_computation.68 | convolution fusion | flops 2818572288 | bytes 17629184 | tf_op jit(solution)/shard_map/dot_general | solution.py:12
  100.4 11.2 %convolution_add_fusion = f32[192,2048]{1,0:T(8,128)} fusion(f32[192,2048]{1,0:T(8,128)S(1)} %fusion.46, bf16[192,3584]{1,0:T(8,128)(2,1)S(1)} %copy-done.4, bf16[2048,3584]{1,0:T(8,128)(2,1)} %param.14), kind=kOutput, calls=%fused_computation.19 | convolution fusion | flops 2818965504 | bytes 19202048 | tf_op jit(solution)/shard_map/dot_general | solution.py:12
  111.6 5.1 %all-to-all-start.4 = ((f32[4,48,2048]{2,1,0:T(8,128)}), f32[4,48,2048]{2,1,0:T(8,128)}, u32[]{:S(2)}, u32[]{:S(2)}) async-start(f32[4,48,2048]{2,1,0:T(8,128)} %bitcast.69), calls=%async_computation.5 | async-start | bytes 3145728 | tf_op jit(solution)/shard_map/all_to_all | solution.py:103
  116.7 9.8 %fusion.45 = f32[192,2048]{1,0:T(8,128)} fusion(bf16[192,3584]{1,0:T(8,128)(2,1)} %get-tuple-element.11, bf16[3584,2048]{1,0:T(8,128)(2,1)} %param.15), kind=kOutput, calls=%fused_computation.67 | convolution fusion | flops 2818572288 | bytes 17629184 | tf_op jit(solution)/shard_map/dot_general | solution.py:29
  126.5 26.2 %all-to-all-done.4 = f32[4,48,2048]{2,1,0:T(8,128)} async-done(((f32[4,48,2048]{2,1,0:T(8,128)}), f32[4,48,2048]{2,1,0:T(8,128)}, u32[]{:S(2)}, u32[]{:S(2)}) %all-to-all-start.4) | async-done | bytes 1572896 | tf_op jit(solution)/shard_map/all_to_all | solution.py:103
  152.7 4.3 %all-to-all-start.1 = ((f32[4,48,2048]{2,1,0:T(8,128)}), f32[4,48,2048]{2,1,0:T(8,128)}, u32[]{:S(2)}, u32[]{:S(2)}) async-start(f32[4,48,2048]{2,1,0:T(8,128)} %bitcast.68), calls=%async_computation.1 | async-start | bytes 3145728 | tf_op jit(solution)/shard_map/all_to_all | solution.py:102
  157.2 4.3 %fusion.11 = f32[8,48,2048]{2,0,1:T(8,128)S(1)} fusion(f32[4,48,2048]{2,1,0:T(8,128)} %all-to-all-done.4, s32[4]{0:T(128)S(1)} %and_select_fusion.1), kind=kOutput, calls=%fused_computation.22 | convolution fusion | flops 37748768 | bytes 4718608 | tf_op jit(solution)/shard_map/ej,jcd->ecd/dot_general | solution.py:107
  161.4 4.2 %fusion.8 = f32[128,2048]{1,0:T(8,128)} fusion(f32[8,48,2048]{2,0,1:T(8,128)S(1)} %fusion.11, s32[8,128]{1,0:T(8,128)S(1)} %broadcast_add_fusion, pred[8,128]{1,0:T(8,128)(4,1)S(1)} %get-tuple-element.12), kind=kOutput, calls=%fused_computation.21 | convolution fusion | flops 1208057856 | bytes 4199424 | tf_op jit(solution)/shard_map/ect,ecd->td/dot_general | solution.py:109
  166.0 27.7 %all-to-all-done.1 = f32[4,48,2048]{2,1,0:T(8,128)} async-done(((f32[4,48,2048]{2,1,0:T(8,128)}), f32[4,48,2048]{2,1,0:T(8,128)}, u32[]{:S(2)}, u32[]{:S(2)}) %all-to-all-start.1) | async-done | bytes 1572896 | tf_op jit(solution)/shard_map/all_to_all | solution.py:102
  193.6 4.5 %multiply_reduce_fusion = (f32[8,48]{0,1:T(8,128)S(1)}, f32[8,48,2048]{2,0,1:T(8,128)S(1)}) fusion(bf16[8,48,2048]{2,0,1:T(8,128)(2,1)S(1)} %convolution_convert_fusion.3, f32[4,48,2048]{2,1,0:T(8,128)} %all-to-all-done.1, s32[4]{0:T(128)S(1)} %and_select_fusion.1), kind=kOutput, calls=%fused_computation.11 | convolution fusion | flops 40107680 | bytes 6293008 | tf_op jit(solution)/shard_map/ej,jcd->ecd/dot_general | solution.py:106
  198.1 4.9 %fusion.5 = f32[128,2048]{1,0:T(8,128)} fusion(f32[8,48,2048]{2,0,1:T(8,128)S(1)} %get-tuple-element.17, f32[8,48]{1,0:T(8,128)S(1)} %get-tuple-element.7, s32[8,128]{1,0:T(8,128)S(1)} %broadcast_add_fusion, pred[8,128]{1,0:T(8,128)(4,1)S(1)} %get-tuple-element.12), kind=kOutput, calls=%fused_computation.20 | convolution fusion | flops 1208107008 | bytes 4200960 | tf_op jit(solution)/shard_map/ect,ecd->td/dot_general | solution.py:108
  205.1 9.0 %convolution_convert_fusion.1 = bf16[2048,3584]{1,0:T(8,128)(2,1)} fusion(bf16[192,2048]{1,0:T(8,128)(2,1)S(1)} %bitcast.64, bf16[192,3584]{1,0:T(8,128)(2,1)} %get-tuple-element.9), kind=kOutput, calls=%fused_computation.4 | convolution fusion | flops 2825912320 | bytes 16842752 | tf_op jit(solution)/shard_map/dot_general | solution.py:18
  214.1 13.1 %reduce-scatter.6.cloned.1.call-done = f32[128,512]{1,0:T(8,128)} async-done(((f32[128,2048]{1,0:T(8,128)}), f32[128,512]{1,0:T(8,128)}) %reduce-scatter.6.cloned.1.call-update) | async-done | bytes 262160 | tf_op jit(solution)/shard_map/reduce_scatter | solution.py:115
  227.2 7.6 %convolution_convert_fusion.2 = bf16[2048,3584]{1,0:T(8,128)(2,1)} fusion(bf16[192,2048]{1,0:T(8,128)(2,1)S(1)} %bitcast.65, bf16[192,3584]{1,0:T(8,128)(2,1)S(1)} %copy-done.3), kind=kOutput, calls=%fused_computation.5 | convolution fusion | flops 2825912320 | bytes 16842752 | tf_op jit(solution)/shard_map/dot_general | solution.py:18
  234.8 7.6 %convolution_convert_fusion = bf16[3584,2048]{1,0:T(8,128)(2,1)} fusion(bf16[192,3584]{1,0:T(8,128)(2,1)S(1)} %copy-done.2, bf16[192,2048]{1,0:T(8,128)(2,1)S(1)} %bitcast.67, f32[192]{0:T(256)S(1)} %reshape.149), kind=kOutput, calls=%fused_computation.3 | convolution fusion | flops 2827091968 | bytes 16843520 | tf_op jit(solution)/shard_map/dot_general | solution.py:18
  242.5 7.1 %reduce-scatter.10.cloned.1.call-done = f32[32,2]{1,0:T(8,128)} async-done(((f32[128,2]{1,0:T(8,128)}), f32[32,2]{1,0:T(8,128)}) %reduce-scatter.10.cloned.1.call-update) | async-done | bytes 272
  250.4 5.1 %all-gather = f32[4,32,2]{1,2,0:T(2,128)S(1)} all-gather(f32[1,32,2]{1,2,0:T(2,128)S(1)} %bitcast.74), channel_id=1, replica_groups=mesh['groups'=2,'ed'=4,'dp'=2,'tp'=2] {'dp','tp'}, dimensions={0}, use_global_device_ids=true | all-gather | bytes 1280 | tf_op jit(solution)/shard_map/all_gather | solution.py:122
  256.1 11.8 %all-gather.6.cloned.1.call-done = f32[128,2048]{1,0:T(8,128)} async-done(((f32[128,512]{1,0:T(8,128)}), f32[128,2048]{1,0:T(8,128)}) %all-gather.6.cloned.1.call-update) | async-done | bytes 1048592 | tf_op jit(solution)/shard_map/all_gather | solution.py:121
  267.9 2.1 convert_element_type.83
  270.0 16.2 %all-gather.4.cloned.1.call-done = f32[128,2048]{1,0:T(8,128)} async-done(((f32[128,512]{1,0:T(8,128)}), f32[128,2048]{1,0:T(8,128)}) %all-gather.4.cloned.1.call-update) | async-done | bytes 1048592 | tf_op jit(solution)/shard_map/all_gather | solution.py:120
  286.1 2.1 convert_element_type.77
  (55 shorter events, 9.1 us)
Async XLA Ops:
  7.2 9.6 %copy-start = (bf16[128,2048]{1,0:T(8,128)(2,1)S(1)}, bf16[128,2048]{1,0:T(8,128)(2,1)}, u32[]{:S(2)}) copy-start(bf16[128,2048]{1,0:T(8,128)(2,1)} %param.12) | copy-start | bytes 1572868
  9.0 10.4 %copy-start.5 = (bf16[128,2048]{1,0:T(8,128)(2,1)S(1)}, bf16[128,2048]{1,0:T(8,128)(2,1)}, u32[]{:S(2)}) copy-start(bf16[128,2048]{1,0:T(8,128)(2,1)} %param.9) | copy-start | bytes 1572868
  10.4 16.1 %all-to-all-start.2 = ((bf16[4,1,48]{2,1,0:T(2,128)(2,1)}), bf16[4,1,48]{2,1,0:T(2,128)(2,1)S(1)}, u32[]{:S(2)}, u32[]{:S(2)}) async-start(bf16[4,1,48]{2,1,0:T(2,128)(2,1)} %copy.47), calls=%async_computation.3 | async-start | bytes 4096 | tf_op jit(solution)/shard_map/all_to_all | solution.py:87
  26.4 24.6 %all-to-all-start = ((bf16[4,48,2048]{2,1,0:T(8,128)(2,1)}), bf16[4,48,2048]{2,1,0:T(8,128)(2,1)S(1)}, u32[]{:S(2)}, u32[]{:S(2)}) async-start(bf16[4,48,2048]{2,1,0:T(8,128)(2,1)} %get-tuple-element.15), calls=%async_computation | async-start | bytes 1572864 | tf_op jit(solution)/shard_map/all_to_all | solution.py:81
  51.1 23.6 %all-to-all-start.3 = ((bf16[4,48,2048]{2,1,0:T(8,128)(2,1)}), bf16[4,48,2048]{2,1,0:T(8,128)(2,1)S(1)}, u32[]{:S(2)}, u32[]{:S(2)}) async-start(bf16[4,48,2048]{2,1,0:T(8,128)(2,1)} %get-tuple-element.14), calls=%async_computation.4 | async-start | bytes 1572864 | tf_op jit(solution)/shard_map/all_to_all | solution.py:84
  91.8 8.6 %copy-start.4 = (bf16[192,3584]{1,0:T(8,128)(2,1)S(1)}, bf16[192,3584]{1,0:T(8,128)(2,1)}, u32[]{:S(2)}) copy-start(bf16[192,3584]{1,0:T(8,128)(2,1)} %get-tuple-element.9) | copy-start | bytes 4128772
  111.6 41.1 %all-to-all-start.4 = ((f32[4,48,2048]{2,1,0:T(8,128)}), f32[4,48,2048]{2,1,0:T(8,128)}, u32[]{:S(2)}, u32[]{:S(2)}) async-start(f32[4,48,2048]{2,1,0:T(8,128)} %bitcast.69), calls=%async_computation.5 | async-start | bytes 3145728 | tf_op jit(solution)/shard_map/all_to_all | solution.py:103
  152.7 40.9 %all-to-all-start.1 = ((f32[4,48,2048]{2,1,0:T(8,128)}), f32[4,48,2048]{2,1,0:T(8,128)}, u32[]{:S(2)}, u32[]{:S(2)}) async-start(f32[4,48,2048]{2,1,0:T(8,128)} %bitcast.68), calls=%async_computation.1 | async-start | bytes 3145728 | tf_op jit(solution)/shard_map/all_to_all | solution.py:102
  157.1 47.1 %reduce-scatter.8.cloned.1.call-start = ((), (), s32[]{:S(2)}) async-start(), calls=%async_computation.10 | async-start | bytes 1310720 | tf_op jit(solution)/shard_map/reduce_scatter | solution.py:116
  165.7 61.5 %reduce-scatter.6.cloned.1.call-start = ((), (), s32[]{:S(2)}) async-start(), calls=%async_computation.8 | async-start | bytes 1310720 | tf_op jit(solution)/shard_map/reduce_scatter | solution.py:115
  198.1 5.2 %copy-start.6 = (s32[128,2]{0,1:T(2,128)S(1)}, s32[128,2]{0,1:T(2,128)}, u32[]{:S(2)}) copy-start(s32[128,2]{0,1:T(2,128)} %param.10) | copy-start | bytes 3076
  203.0 46.6 %reduce-scatter.10.cloned.1.call-start = ((), (), s32[]{:S(2)}) async-start(), calls=%async_computation.12 | async-start | bytes 81920
  204.2 63.7 %all-gather.6.cloned.1.call-start = ((), (), s32[]{:S(2)}) async-start(), calls=%async_computation.11 | async-start | bytes 1310720 | tf_op jit(solution)/shard_map/all_gather | solution.py:121
  204.7 22.5 %copy-start.3 = (bf16[192,3584]{1,0:T(8,128)(2,1)S(1)}, bf16[192,3584]{1,0:T(8,128)(2,1)}, u32[]{:S(2)}) copy-start(bf16[192,3584]{1,0:T(8,128)(2,1)} %get-tuple-element.10) | copy-start | bytes 4128772
  204.8 81.4 %all-gather.4.cloned.1.call-start = ((), (), s32[]{:S(2)}) async-start(), calls=%async_computation.9 | async-start | bytes 1310720 | tf_op jit(solution)/shard_map/all_gather | solution.py:120
  227.2 7.6 %copy-start.2 = (bf16[192,3584]{1,0:T(8,128)(2,1)S(1)}, bf16[192,3584]{1,0:T(8,128)(2,1)}, u32[]{:S(2)}) copy-start(bf16[192,3584]{1,0:T(8,128)(2,1)} %get-tuple-element.11) | copy-start | bytes 4128772
  234.8 53.4 %copy-start.1 = (bf16[128,2048]{1,0:T(8,128)(2,1)S(1)}, bf16[128,2048]{1,0:T(8,128)(2,1)}, u32[]{:S(2)}) copy-start(bf16[128,2048]{1,0:T(8,128)(2,1)} %param.12) | copy-start | bytes 1572868
Sparse Core Ops, SparseCore 0:
  165.8 26.2 reduce-scatter.7
  203.2 23.9 reduce-scatter.5
  230.2 19.3 reduce-scatter.9
  251.1 16.7 all-gather.5
  269.4 16.7 all-gather.3
where the time goes:
time: 299 us; the launch traced here: 295 us
  waiting for transfers between devices  122 us (41%)
  matrix products  111 us (37%)
  starting transfers between devices  25.6 us (9%)
  between operations  14.2 us (5%)
  local copies, waits for them, and re-layouts  9.55 us (3%)
  other arithmetic  7.48 us (3%)
  blocking collectives  5.06 us (2%)
    dot_general x3, matrix products, contract_last(): lax.dot_general(left_mat, right_mat, (((1,), (1,)), ((), ())), preferred_...  36.9 us
    all_to_all x1, waiting for transfers between devices, on_device(): lax.all_to_all(out_slots, 'ed', split_axis=0, concat_axis=0, tiled=True)  27.7 us
    all_to_all x1, waiting for transfers between devices, on_device(): lax.all_to_all(input_slots, 'ed', split_axis=0, concat_axis=0, tiled=True)  26.2 us
    dot_general x3, matrix products, contract_first(): lax.dot_general(left_mat, right_mat, (((0,), (0,)), ((), ())), preferred_...  24.3 us
    all_to_all x1, waiting for transfers between devices, on_device(): lax.all_to_all(jnp.take(send_rows, dest_expert, axis=0), 'ed', split_axis...  19.4 us
    all_gather x1, waiting for transfers between devices, on_device(): lax.all_gather(layer_piece, ('dp', 'tp'), axis=1, tiled=True)  16.2 us
    reduce_scatter x1, waiting for transfers between devices, on_device(): lax.psum_scatter(layer_full, ('dp', 'tp'), scatter_dimension=1, tiled=True)  13.1 us
    all_gather x1, waiting for transfers between devices, on_device(): lax.all_gather(input_piece, ('dp', 'tp'), axis=1, tiled=True)  11.8 us
  transfers between devices with their start and end apart: 10, of which 8 were waited for; matrix products, arithmetic and copies ran while one was open for 29% of the time, Pallas kernels for 0%

commit v1 on v0

v1 whole, which is shorter than its diff:
```python
import functools

import jax
import jax.numpy as jnp
from jax import lax
from jax.experimental import pallas as pl
from jax.experimental.pallas import tpu as pltpu
from jax.sharding import PartitionSpec as P

FF = 7168
CAP = 48
LANES = 128
F32 = jnp.float32
BF16 = jnp.bfloat16
VMEM_LIMIT = 56 * 1024 * 1024


def dot(left, right, left_dim=1, right_dim=0):
    return lax.dot_general(
        left, right, (((left_dim,), (right_dim,)), ((), ())), preferred_element_type=F32
    )


def params():
    return pltpu.CompilerParams(vmem_limit_bytes=VMEM_LIMIT)


def whole(shape):
    return pl.BlockSpec(shape, lambda *_: (0,) * len(shape))


def tile_of(size, most):
    for tile in (1024, 512, 256, 128):
        if tile <= most and size % tile == 0:
            return tile
    return size


def cost(flops, nbytes):
    return pl.CostEstimate(flops=int(flops), bytes_accessed=int(nbytes), transcendentals=0)


def shift(value, axis, step):
    count = lax.axis_size(axis)
    return lax.ppermute(value, axis, [(j, (j + step) % count) for j in range(count)])


def pick_body(n, half, scal, ids, gates, tokens, grads, *outs):
    tok_outs, grad_outs, coef_own, first, second, weighted = (
        outs[:n], outs[n:2 * n], outs[2 * n], outs[2 * n + 1], outs[2 * n + 2], outs[2 * n + 3],
    )
    rows = ids.shape[0]
    eye = (
        lax.broadcasted_iota(jnp.int32, (rows, rows), 0)
        == lax.broadcasted_iota(jnp.int32, (rows, rows), 1)
    ).astype(BF16)
    upper = (
        lax.broadcasted_iota(jnp.int32, (rows, rows), 0)
        <= lax.broadcasted_iota(jnp.int32, (rows, rows), 1)
    ).astype(BF16)
    ids_row = dot(ids[...].astype(F32).astype(BF16), eye, 0, 0)
    gates_row = dot(gates[...], eye, 0, 0)
    at = pl.multiple_of(scal[0] * half, half)
    slot_index = lax.broadcasted_iota(jnp.int32, (CAP, rows), 0).astype(F32)
    for s in range(n):
        expert = scal[1 + s].astype(F32)
        hit0 = (ids_row[0:1] == expert).astype(F32)
        hit1 = (ids_row[1:2] == expert).astype(F32)
        chosen = hit0 + hit1
        place = dot(jnp.broadcast_to(chosen, (8, rows)).astype(BF16), upper)[0:1] - 1.0
        here = (place == slot_index).astype(F32)
        placed0 = here * hit0
        placed1 = here * hit1
        weight = placed0 * gates_row[0:1] + placed1 * gates_row[1:2]
        placed = (placed0 + placed1).astype(BF16)
        span = pl.ds(s * CAP, CAP)
        first[span, :] = placed0.astype(BF16)
        second[span, :] = placed1.astype(BF16)
        weighted[span, :] = weight.astype(BF16)
        coef = jnp.broadcast_to(jnp.sum(weight, axis=1, keepdims=True), (CAP, LANES)).astype(BF16)
        if s == 0:
            tok_outs[0][...] = dot(placed, tokens[...]).astype(BF16)
            grad_outs[0][...] = dot(placed, grads[...]).astype(BF16)
            coef_own[...] = coef
        else:
            tok_outs[s][...] = dot(placed, tokens[:, pl.ds(at, half)]).astype(BF16)
            grad_outs[s][:, 0:half] = dot(placed, grads[:, pl.ds(at, half)]).astype(BF16)
            grad_outs[s][:, half:] = coef


def pick(n, scal, ids, gates, tokens, grads):
    rows, width = tokens.shape
    half = width // 2
    slots = n * CAP
    out = (
        [jax.ShapeDtypeStruct((CAP, width), BF16)]
        + [jax.ShapeDtypeStruct((CAP, half), BF16)] * (n - 1)
        + [jax.ShapeDtypeStruct((CAP, width), BF16)]
        + [jax.ShapeDtypeStruct((CAP, half + LANES), BF16)] * (n - 1)
        + [jax.ShapeDtypeStruct((CAP, LANES), BF16)]
        + [jax.ShapeDtypeStruct((slots, rows), BF16)] * 3
    )
    got = pl.pallas_call(
        functools.partial(pick_body, n, half),
        out_shape=out,
        grid_spec=pltpu.PrefetchScalarGridSpec(
            num_scalar_prefetch=1,
            grid=(1,),
            in_specs=[whole(v.shape) for v in (ids, gates, tokens, grads)],
            out_specs=[whole(v.shape) for v in out],
        ),
        compiler_params=params(),
        cost_estimate=cost(4 * slots * rows * width, 4 * rows * width * 2),
        name="pick",
    )(scal, ids, gates, tokens, grads)
    return got[:n], got[n:2 * n], got[2 * n], got[2 * n + 1:]


def gather_rows(n, half, scal, own, direct, other, held):
    mine = pl.multiple_of(scal[0] * half, half)
    theirs = pl.multiple_of((1 - scal[0]) * half, half)
    held[0:CAP, :] = own[...]
    for s in range(1, n):
        span = pl.ds(s * CAP, CAP)
        held[span, pl.ds(mine, half)] = direct[s - 1][:, 0:half]
        held[span, pl.ds(theirs, half)] = other[s - 1][:, 0:half]


def forward_body(n, half, scal, own, *refs):
    direct, other = refs[:n - 1], refs[n - 1:2 * n - 2]
    gate_w, up_w, rows_out, hidden, act, slope = refs[2 * n - 2:]

    @pl.when(pl.program_id(0) == 0)
    def _():
        gather_rows(n, half, scal, own, direct, other, rows_out)

    rows = rows_out[...]
    pre_gate = dot(rows, gate_w[...])
    pre_up = dot(rows, up_w[...])
    logistic = jax.nn.sigmoid(pre_gate)
    silu = pre_gate * logistic
    hidden[...] = (silu * pre_up).astype(BF16)
    act[...] = silu
    slope[...] = pre_up * logistic * (1.0 + pre_gate * (1.0 - logistic))


def forward(n, scal, own, direct, other, gate_w, up_w):
    width, hid = gate_w.shape
    slots = n * CAP
    tile = tile_of(hid, 512)
    column = lambda i, *_: (0, i)
    out = [
        jax.ShapeDtypeStruct((slots, width), BF16),
        jax.ShapeDtypeStruct((slots, hid), BF16),
        jax.ShapeDtypeStruct((slots, hid), F32),
        jax.ShapeDtypeStruct((slots, hid), F32),
    ]
    return pl.pallas_call(
        functools.partial(forward_body, n, width // 2),
        out_shape=out,
        grid_spec=pltpu.PrefetchScalarGridSpec(
            num_scalar_prefetch=1,
            grid=(hid // tile,),
            in_specs=[whole(v.shape) for v in (own, *direct, *other)]
            + [pl.BlockSpec((width, tile), column)] * 2,
            out_specs=[whole((slots, width))] + [pl.BlockSpec((slots, tile), column)] * 3,
        ),
        compiler_params=params(),
        cost_estimate=cost(4 * slots * width * hid, 4 * width * hid + 10 * slots * hid),
        name="forward",
    )(scal, own, *direct, *other, gate_w, up_w)


def middle_body(n, half, scal, own, coef_own, *refs):
    direct, other = refs[:n - 1], refs[n - 1:2 * n - 2]
    (hidden, act, slope, down, scaled, gate_grad, up_grad, send, keep, router,
     held, total, coef) = refs[2 * n - 2:]
    step = pl.program_id(0)

    @pl.when(step == 0)
    def _():
        gather_rows(n, half, scal, own, direct, other, held)
        coef[0:CAP, :] = coef_own[...].astype(F32)
        for s in range(1, n):
            coef[pl.ds(s * CAP, CAP), :] = direct[s - 1][:, half:].astype(F32)
        scaled[...] = (coef[:, 0:1] * held[...].astype(F32)).astype(BF16)
        router[...] = jnp.zeros_like(router)

    rows = hidden[...]
    back = dot(held[...], down[...], 1, 1)
    out = dot(rows, down[...])

    @pl.when(step == 0)
    def _():
        total[...] = out

    @pl.when(step > 0)
    def _():
        total[...] += out

    router[...] += jnp.broadcast_to(
        jnp.sum(rows.astype(F32) * back, axis=1, keepdims=True), router.shape
    )
    grad = coef[:, 0:1] * back
    gate_grad[...] = (grad * slope[...]).astype(BF16)
    up_grad[...] = (grad * act[...]).astype(BF16)

    @pl.when(step == pl.num_programs(0) - 1)
    def _():
        mine = pl.multiple_of(scal[0] * half, half)
        theirs = pl.multiple_of((1 - scal[0]) * half, half)
        send[...] = total[:, pl.ds(theirs, half)].astype(BF16)
        keep[...] = total[:, pl.ds(mine, half)]


def middle(n, scal, own, coef_own, direct, other, hidden, act, slope, down):
    hid, width = down.shape
    half = width // 2
    slots = n * CAP
    tile = tile_of(hid, 512)
    column = pl.BlockSpec((slots, tile), lambda i, *_: (0, i))
    out = [
        jax.ShapeDtypeStruct((slots, width), BF16),
        jax.ShapeDtypeStruct((slots, hid), BF16),
        jax.ShapeDtypeStruct((slots, hid), BF16),
        jax.ShapeDtypeStruct((slots, half), BF16),
        jax.ShapeDtypeStruct((slots, half), F32),
        jax.ShapeDtypeStruct((slots, LANES), F32),
    ]
    return pl.pallas_call(
        functools.partial(middle_body, n, half),
        out_shape=out,
        grid_spec=pltpu.PrefetchScalarGridSpec(
            num_scalar_prefetch=1,
            grid=(hid // tile,),
            in_specs=[whole(v.shape) for v in (own, coef_own, *direct, *other)]
            + [column] * 3
            + [pl.BlockSpec((tile, width), lambda i, *_: (i, 0))],
            out_specs=[whole((slots, width)), column, column]
            + [whole((slots, half)), whole((slots, half)), whole((slots, LANES))],
            scratch_shapes=[
                pltpu.VMEM((slots, width), BF16),
                pltpu.VMEM((slots, width), F32),
                pltpu.VMEM((slots, LANES), F32),
            ],
        ),
        compiler_params=params(),
        cost_estimate=cost(4 * slots * width * hid, 2 * width * hid + 14 * slots * hid),
        name="middle",
    )(scal, own, coef_own, *direct, *other, hidden, act, slope, down)


def backward_body(scal, gate_grad, up_grad, gate_w, up_w, out):
    out[...] = (
        dot(gate_grad[...], gate_w[...], 1, 1) + dot(up_grad[...], up_w[...], 1, 1)
    ).astype(out.dtype)


def backward(mine, kind, scal, gate_grad, up_grad, gate_w, up_w):
    width, hid = gate_w.shape
    half = width // 2
    slots = gate_grad.shape[0]
    tile = tile_of(half, 256)
    tiles = half // tile
    if mine:
        row = lambda i, scal: (scal[0] * tiles + i, 0)
    else:
        row = lambda i, scal: ((1 - scal[0]) * tiles + i, 0)
    return pl.pallas_call(
        backward_body,
        out_shape=jax.ShapeDtypeStruct((slots, half), kind),
        grid_spec=pltpu.PrefetchScalarGridSpec(
            num_scalar_prefetch=1,
            grid=(tiles,),
            in_specs=[whole((slots, hid))] * 2 + [pl.BlockSpec((tile, hid), row)] * 2,
            out_specs=pl.BlockSpec((slots, tile), lambda i, *_: (0, i)),
        ),
        compiler_params=params(),
        cost_estimate=cost(4 * slots * half * hid, 4 * half * hid),
        name="backward_keep" if mine else "backward_send",
    )(scal, gate_grad, up_grad, gate_w, up_w)


def columns_grad_body(rows, grad, out, flipped):
    @pl.when(pl.program_id(0) == 0)
    def _():
        flipped[...] = rows[...].T

    out[...] = dot(flipped[...], grad[...]).astype(BF16)


def columns_grad(rows, grad):
    slots, width = rows.shape
    hid = grad.shape[1]
    tile = tile_of(hid, 512)
    column = lambda i: (0, i)
    return pl.pallas_call(
        columns_grad_body,
        out_shape=jax.ShapeDtypeStruct((width, hid), BF16),
        grid=(hid // tile,),
        in_specs=[whole((slots, width)), pl.BlockSpec((slots, tile), column)],
        out_specs=pl.BlockSpec((width, tile), column),
        scratch_shapes=[pltpu.VMEM((width, slots), BF16)],
        compiler_params=params(),
        cost_estimate=cost(2 * slots * width * hid, 2 * width * hid),
        name="columns_grad",
    )(rows, grad)


def rows_grad_body(hidden, scaled, out):
    out[...] = dot(hidden[...], scaled[...], 0, 0).astype(BF16)


def rows_grad(hidden, scaled):
    slots, hid = hidden.shape
    width = scaled.shape[1]
    tile = tile_of(hid, 512)
    return pl.pallas_call(
        rows_grad_body,
        out_shape=jax.ShapeDtypeStruct((hid, width), BF16),
        grid=(hid // tile,),
        in_specs=[pl.BlockSpec((slots, tile), lambda i: (0, i)), whole((slots, width))],
        out_specs=pl.BlockSpec((tile, width), lambda i: (i, 0)),
        compiler_params=params(),
        cost_estimate=cost(2 * slots * width * hid, 2 * width * hid),
        name="rows_grad",
    )(hidden, scaled)


def three_parts(value):
    high = value.astype(BF16)
    rest = value - high.astype(F32)
    mid = rest.astype(BF16)
    return high, mid, (rest - mid.astype(F32)).astype(BF16)


def merge_body(n, keep, got, *refs):
    outs = refs[-n:]
    half = keep.shape[1]
    for s in range(n):
        span = pl.ds(s * CAP, CAP)
        outs[s][:, 0:half] = (keep[span, :] + got[span, :].astype(F32)).astype(BF16)
        if len(refs) > n:
            high, mid, low = three_parts(refs[0][span, :])
            lane = lax.broadcasted_iota(jnp.int32, (CAP, LANES), 1)
            outs[s][:, half:] = jnp.where(
                lane == 0, high, jnp.where(lane == 1, mid, jnp.where(lane == 2, low, jnp.zeros_like(low)))
            )


def merge(n, keep, got, router=None):
    half = keep.shape[1]
    wide = half + (0 if router is None else LANES)
    args = (keep, got) if router is None else (keep, got, router)
    return pl.pallas_call(
        functools.partial(merge_body, n),
        out_shape=[jax.ShapeDtypeStruct((CAP, wide), BF16)] * n,
        compiler_params=params(),
        cost_estimate=cost(0, 8 * keep.size),
        name="merge",
    )(*args)


def combine_body(n, weights, *refs):
    chunks, out = refs[:n], refs[-1]
    half = chunks[0].shape[1]
    total = dot(weights[0:CAP, :], chunks[0][...], 0, 0)
    for s in range(1, n):
        total += dot(weights[pl.ds(s * CAP, CAP), :], chunks[s][...], 0, 0)
    out[...] = total.astype(BF16)


def combine(n, weights, chunks):
    half = chunks[0].shape[1]
    return pl.pallas_call(
        functools.partial(combine_body, n),
        out_shape=jax.ShapeDtypeStruct((weights.shape[1], half), BF16),
        compiler_params=params(),
        cost_estimate=cost(2 * weights.size * half, 2 * n * CAP * half),
        name="combine",
    )(weights, *chunks)


def combine_router_body(n, half, first, second, *refs):
    chunks, out = refs[:n], refs[-1]
    rows = first.shape[1]
    total = jnp.zeros((rows, half), F32)
    score0 = jnp.zeros((rows, LANES), F32)
    score1 = jnp.zeros((rows, LANES), F32)
    for s in range(n):
        span = pl.ds(s * CAP, CAP)
        placed0, placed1 = first[span, :], second[span, :]
        total += dot(placed0 + placed1, chunks[s][:, 0:half], 0, 0)
        score0 += dot(placed0, chunks[s][:, half:], 0, 0)
        score1 += dot(placed1, chunks[s][:, half:], 0, 0)
    out[:, 0:half] = total.astype(BF16)
    out[:, half:] = spread_scores(
        jnp.sum(score0, axis=1, keepdims=True), jnp.sum(score1, axis=1, keepdims=True)
    )


def spread_scores(score0, score1):
    rows = score0.shape[0]
    lane = lax.broadcasted_iota(jnp.int32, (rows, LANES), 1)
    out = jnp.zeros((rows, LANES), F32)
    for k, score in enumerate((score0, score1)):
        for p, part in enumerate(three_parts(score)):
            out = jnp.where(lane == 3 * k + p, part.astype(F32), out)
    return out.astype(BF16)


def joined_scores(packed):
    values = packed.astype(F32)
    score0 = values[:, 0:1] + values[:, 1:2] + values[:, 2:3]
    score1 = values[:, 3:4] + values[:, 4:5] + values[:, 5:6]
    return score0, score1


def combine_router(n, first, second, chunks):
    wide = chunks[0].shape[1]
    rows = first.shape[1]
    return pl.pallas_call(
        functools.partial(combine_router_body, n, wide - LANES),
        out_shape=jax.ShapeDtypeStruct((rows, wide), BF16),
        compiler_params=params(),
        cost_estimate=cost(2 * first.size * wide, 2 * n * CAP * wide),
        name="combine_router",
    )(first, second, *chunks)


def add_body(half, *refs):
    pieces, out = refs[:-1], refs[-1]
    total = pieces[0][:, 0:half].astype(F32)
    for piece in pieces[1:]:
        total += piece[:, 0:half].astype(F32)
    out[:, 0:half] = total.astype(BF16)
    if out.shape[1] > half:
        score0, score1 = joined_scores(pieces[0][:, half:])
        for piece in pieces[1:]:
            more0, more1 = joined_scores(piece[:, half:])
            score0, score1 = score0 + more0, score1 + more1
        out[:, half:] = spread_scores(score0, score1)


def add_pieces(half, pieces):
    return pl.pallas_call(
        functools.partial(add_body, half),
        out_shape=jax.ShapeDtypeStruct(pieces[0].shape, BF16),
        compiler_params=params(),
        cost_estimate=cost(0, 6 * pieces[0].size),
        name="add_pieces",
    )(*pieces)


def finish_body(half, scal, own, other, out, *score):
    mine = pl.multiple_of(scal[0] * half, half)
    theirs = pl.multiple_of((1 - scal[0]) * half, half)
    out[:, pl.ds(mine, half)] = own[:, 0:half]
    out[:, pl.ds(theirs, half)] = other[:, 0:half]
    if score:
        own0, own1 = joined_scores(own[:, half:])
        other0, other1 = joined_scores(other[:, half:])
        lane = lax.broadcasted_iota(jnp.int32, score[0].shape, 1)
        score[0][...] = jnp.where(lane == 0, own0 + other0, own1 + other1)


def finish(half, scal, own, other):
    rows, wide = own.shape
    out = [jax.ShapeDtypeStruct((rows, 2 * half), BF16)]
    if wide > half:
        out.append(jax.ShapeDtypeStruct((rows, 2), F32))
    return pl.pallas_call(
        functools.partial(finish_body, half),
        out_shape=out,
        grid_spec=pltpu.PrefetchScalarGridSpec(
            num_scalar_prefetch=1,
            grid=(1,),
            in_specs=[whole(v.shape) for v in (own, other)],
            out_specs=[whole(v.shape) for v in out],
        ),
        compiler_params=params(),
        cost_estimate=cost(0, 4 * rows * wide),
        name="finish",
    )(scal, own, other)


def over_dp(half, value):
    count = lax.axis_size("dp")
    if count == 2:
        return add_pieces(half, [value, shift(value, "dp", 1)])
    gathered = lax.all_gather(value, "dp", axis=0, tiled=False)
    return add_pieces(half, [gathered[j] for j in range(count)])


def on_device(tokens, expert_ids, gates, out_grad, gate_weight, up_weight, down_weight):
    n = lax.axis_size("ed")
    reps = lax.axis_size(("dp", "tp"))
    me = lax.axis_index("ed")
    rep = lax.axis_index(("dp", "tp"))
    width = tokens.shape[1]
    half = width // 2
    hid = gate_weight.shape[1]
    owners = (me + jnp.arange(n, dtype=jnp.int32)) % n
    experts = (owners * reps + rep) * hid // FF
    scal = jnp.concatenate([lax.axis_index("tp").reshape(1), experts]).astype(jnp.int32)

    toks, grads, coef_own, (first, second, weighted) = pick(
        n, scal, expert_ids, gates, tokens, out_grad
    )
    tok_z = [shift(toks[s], "ed", s) for s in range(1, n)]
    grad_z = [shift(grads[s], "ed", s) for s in range(1, n)]
    tok_c = [shift(v, "tp", 1) for v in tok_z]
    rows, hidden, act, slope = forward(n, scal, toks[0], tok_z, tok_c, gate_weight, up_weight)
    grad_c = [shift(v, "tp", 1) for v in grad_z]
    scaled, gate_pre, up_pre, out_send, out_keep, router = middle(
        n, scal, grads[0], coef_own, grad_z, grad_c, hidden, act, slope, down_weight
    )
    out_got = shift(out_send, "tp", 1)
    in_send = backward(False, BF16, scal, gate_pre, up_pre, gate_weight, up_weight)
    out_chunks = merge(n, out_keep, out_got)
    out_back = [out_chunks[0]] + [shift(out_chunks[s], "ed", -s) for s in range(1, n)]
    in_got = shift(in_send, "tp", 1)
    in_keep = backward(True, F32, scal, gate_pre, up_pre, gate_weight, up_weight)
    in_chunks = merge(n, in_keep, in_got, router)
    in_back = [in_chunks[0]] + [shift(in_chunks[s], "ed", -s) for s in range(1, n)]
    down_grad = rows_grad(hidden, scaled)
    gate_w_grad = columns_grad(rows, gate_pre)
    up_w_grad = columns_grad(rows, up_pre)
    out_half = over_dp(half, combine(n, weighted, out_back))
    layer_out, = finish(half, scal, out_half, shift(out_half, "tp", 1))
    in_half = over_dp(half, combine_router(n, first, second, in_back))
    token_grad, gate_grad = finish(half, scal, in_half, shift(in_half, "tp", 1))
    return layer_out, token_grad, gate_grad, gate_w_grad, up_w_grad, down_grad


def solution(mesh):
    token_spec = P(("groups", "ed"), None)
    in_specs = (
        token_spec,
        token_spec,
        token_spec,
        token_spec,
        P(None, ("ed", "dp", "tp")),
        P(None, ("ed", "dp", "tp")),
        P(("ed", "dp", "tp"), None),
    )
    out_specs = (
        token_spec,
        token_spec,
        token_spec,
        P("groups", ("ed", "dp", "tp")),
        P("groups", ("ed", "dp", "tp")),
        P(("groups", "ed", "dp", "tp"), None),
    )
    return jax.shard_map(
        on_device, mesh=mesh, in_specs=in_specs, out_specs=out_specs, check_vma=False
    )
```

time: 299 us -> 164 us (0.55); the launches traced: 295 us -> 163 us
  matrix products: 111 us -> 0 us
  Pallas kernels: 0 us -> 107 us
  waiting for transfers between devices: 122 us -> 20.6 us
  between operations: 14.2 us -> 0.86 us
  other arithmetic: 7.48 us -> 0.64 us
  blocking collectives: 5.06 us -> 0 us
    dot_general x17 -> x0, matrix products: 111 us -> none  [the longest x3 36.9 us: contract_last(): lax.dot_general(left_mat, right_mat, (((1,), (1,)), ((), ())), preferred_...]
    pallas_call x0 -> x16, Pallas kernels: none -> 107 us  [the longest x2 21.2 us: backward(): pl.pallas_call(backward_body, out_shape=jax.ShapeDtypeStruct((slots, half...]
    all_to_all x5 -> x0, waiting for transfers between devices: 73.5 us -> none  [the longest x1 27.7 us: on_device(): lax.all_to_all(out_slots, 'ed', split_axis=0, concat_axis=0, tiled=True)]
    all_gather x2 -> x0, waiting for transfers between devices: 27.9 us -> none  [the longest x1 16.2 us: on_device(): lax.all_gather(layer_piece, ('dp', 'tp'), axis=1, tiled=True)]
    all_to_all x5 -> x0, starting transfers between devices: 24.9 us -> none  [the longest x1 6.32 us: on_device(): lax.all_to_all(jnp.take(send_scale, dest_expert, axis=0), 'ed', split_axi...]
    ppermute x0 -> x24, starting transfers between devices: none -> 23.4 us  [shift(): lax.ppermute(value, axis, [(j, (j + step) % count) for j in range(count)])]
    ppermute x0 -> x24, waiting for transfers between devices: none -> 20.6 us  [shift(): lax.ppermute(value, axis, [(j, (j + step) % count) for j in range(count)])]
    reduce_scatter x2 -> x0, waiting for transfers between devices: 13.1 us -> none  [the longest x1 13.1 us: on_device(): lax.psum_scatter(layer_full, ('dp', 'tp'), scatter_dimension=1, tiled=True)]
  transfers between devices with their start and end apart: 10 -> 24, of which waited for: 8 -> 5; matrix products, arithmetic and copies ran while one was open for 29% -> 0% of each run, Pallas kernels for 0% -> 44%
where the time goes in v1:
time: 164 us; the launch traced here: 163 us
  Pallas kernels  107 us (65%)
  starting transfers between devices  23.4 us (14%)
  waiting for transfers between devices  20.6 us (13%)
  local copies, waits for them, and re-layouts  11.3 us (7%)
    ppermute x24, starting transfers between devices, shift(): lax.ppermute(value, axis, [(j, (j + step) % count) for j in range(count)])  23.4 us
    pallas_call x2, Pallas kernels, backward(): pl.pallas_call(backward_body, out_shape=jax.ShapeDtypeStruct((slots, half...  21.2 us
    ppermute x24, waiting for transfers between devices, shift(): lax.ppermute(value, axis, [(j, (j + step) % count) for j in range(count)])  20.6 us
    pallas_call x2, Pallas kernels, columns_grad(): pl.pallas_call(columns_grad_body, out_shape=jax.ShapeDtypeStruct((width,...  19.8 us
    pallas_call x1, Pallas kernels, middle(): pl.pallas_call(functools.partial(middle_body, n, half), out_shape=out, gr...  17.4 us
    pallas_call x1, Pallas kernels, forward(): pl.pallas_call(functools.partial(forward_body, n, width // 2), out_shape=...  16.8 us
    unnamed x53, local copies, waits for them, and re-layouts  11.3 us
    pallas_call x1, Pallas kernels, rows_grad(): pl.pallas_call(rows_grad_body, out_shape=jax.ShapeDtypeStruct((hid, width...  9.72 us
  transfers between devices with their start and end apart: 24, of which 5 were waited for; matrix products, arithmetic and copies ran while one was open for 0% of the time, Pallas kernels for 44%

profile of v1, /device:TPU:0, one launch (start us, length us, event | category | flops | bytes accessed | tf_op | source)
XLA Modules:
  0.0 163.4 jit_solution(13430108174626061868)
XLA Ops:
  0.6 1.4 copy.14.gates
  2.0 1.4 copy.13.ids
  4.1 3.8 %pick.1 = (bf16[48,2048]{1,0:T(8,128)(2,1)}, bf16[48,1024]{1,0:T(8,128)(2,1)}, bf16[48,1024]{1,0:T(8,128)(2,1)}, bf16[48,1024]{1,0:T(8,128)(2,1)}, bf16[48,2048]...) custom-call(s32[5]{0:T(128)} %pad_add_fusion.scal, ...), custom_call_target="tpu_custom_call" | custom-call | flops 201326592 | bytes 2097152 | tf_op jit(solution)/shard_map/pick/pallas_call | solution.py:103
  7.9 3.1 %collective-permute-start.6 = (bf16[48,1024]{1,0:T(8,128)(2,1)}, bf16[48,1024]{1,0:T(8,128)(2,1)S(1)}, u32[]{:S(2)}, u32[]{:S(2)}) collective-permute-start(bf16[48,1024]{1,0:T(8,128)(2,1)} %get-tuple-element.45), channel_id=1, source_target_pairs={{0,4},{4,8},{8,12},{12,0},{1,5},{5,9},{9,13},{13,1},{2,6},{6,10},{... | collective-permute-start | bytes 294920 | tf_op jit(solution)/shard_map/ppermute | solution.py:45
  10.9 1.6 collective-permute-start
  12.5 1.1 collective-permute-start.7
  13.6 2.9 %collective-permute-start.8 = (bf16[48,1024]{1,0:T(8,128)(2,1)}, bf16[48,1024]{1,0:T(8,128)(2,1)S(1)}, u32[]{:S(2)}, u32[]{:S(2)}) collective-permute-start(bf16[48,1024]{1,0:T(8,128)(2,1)} %get-tuple-element.47), channel_id=1, source_target_pairs={{0,12},{4,0},{8,4},{12,8},{1,13},{5,1},{9,5},{13,9},{2,14},{6,2},{... | collective-permute-start | bytes 294920 | tf_op jit(solution)/shard_map/ppermute | solution.py:45
  17.0 1.9 %collective-permute-start.2 = (bf16[48,1152]{1,0:T(8,128)(2,1)}, bf16[48,1152]{1,0:T(8,128)(2,1)S(1)}, u32[]{:S(2)}, u32[]{:S(2)}) collective-permute-start(bf16[48,1152]{1,0:T(8,128)(2,1)} %get-tuple-element.43), channel_id=1, source_target_pairs={{0,12},{4,0},{8,4},{12,8},{1,13},{5,1},{9,5},{13,9},{2,14},{6,2},{... | collective-permute-start | bytes 331784 | tf_op jit(solution)/shard_map/ppermute | solution.py:45
  18.9 5.4 %collective-permute-done.7.refs_1_ = bf16[48,1024]{1,0:T(8,128)(2,1)S(1)} collective-permute-done((bf16[48,1024]{1,0:T(8,128)(2,1)}, bf16[48,1024]{1,0:T(8,128)(2,1)S(1)}, u32[]{:S(2)}, u32[]{:S(2)}) %collective-permute-start.7) | collective-permute-done | bytes 98336 | tf_op jit(solution)/shard_map/ppermute | solution.py:45
  24.9 4.7 %collective-permute-done.1.refs_1_ = bf16[48,1152]{1,0:T(8,128)(2,1)S(1)} collective-permute-done((bf16[48,1152]{1,0:T(8,128)(2,1)}, bf16[48,1152]{1,0:T(8,128)(2,1)S(1)}, u32[]{:S(2)}, u32[]{:S(2)}) %collective-permute-start.1) | collective-permute-done | bytes 110624 | tf_op jit(solution)/shard_map/ppermute | solution.py:45
  30.8 16.8 %forward.1 = (bf16[192,2048]{1,0:T(8,128)(2,1)}, bf16[192,3584]{1,0:T(8,128)(2,1)}, f32[192,3584]{1,0:T(8,128)}, f32[192,3584]{1,0:T(8,128)}) custom-call(s32[5]{0:T(128)} %pad_add_fusion.scal, bf16[48,2048]{1,0:T(8,128)(2,1)} %get-tuple-element.44.own, bf16[48,1024]{1,0:T(8,128)(2,1)} %copy-done.18, bf16[48,1024]{1,0:T(8,128)(2,1)} %copy-done.19, ...), custom_call_target="tpu_custom_call" | custom-call | flops 5637144576 | bytes 36241408 | tf_op jit(solution)/shard_map/forward/pallas_call | solution.py:158
  48.4 17.4 %middle.1 = (bf16[192,2048]{1,0:T(8,128)(2,1)}, bf16[192,3584]{1,0:T(8,128)(2,1)}, bf16[192,3584]{1,0:T(8,128)(2,1)}, bf16[192,1024]{1,0:T(8,128)(2,1)}, f32[192,1024]{1,0:T(8,128)}, /*index=5*/f32[192,128]{1,0:T(8,128)}) custom-call(s32[5]{0:T(128)} %pad_add_fusion.scal, bf16[48,2048]{1,0:T(8,128)(2,1)} %get-tuple-element.39.own, ...), custom_call_target="tpu_custom_call" | custom-call | flops 5637144576 | bytes 24313856 | tf_op jit(solution)/shard_map/middle/pallas_call | solution.py:230
  65.8 10.6 %backward_send.1 = bf16[192,1024]{1,0:T(8,128)(2,1)} custom-call(s32[5]{0:T(128)} %pad_add_fusion.scal, bf16[192,3584]{1,0:T(8,128)(2,1)} %get-tuple-element.59.gate_grad.grad, bf16[192,3584]{1,0:T(8,128)(2,1)} %get-tuple-element.60.up_grad.grad, bf16[2048,3584]{1,0:T(8,128)(2,1)} %gate_w.3, bf16[2048,3584]{1,0:T(8,128)(2,1)} %up_w.3), custom_call_target="tpu_custom_call" | custom-call | flops 2818572288 | bytes 14680064 | tf_op jit(solution)/shard_map/backward_send/pallas_call | solution.py:269
  76.9 10.6 %backward_keep.1.keep = f32[192,1024]{1,0:T(8,128)} custom-call(s32[5]{0:T(128)} %pad_add_fusion.scal, bf16[192,3584]{1,0:T(8,128)(2,1)} %get-tuple-element.59.gate_grad.grad, bf16[192,3584]{1,0:T(8,128)(2,1)} %get-tuple-element.60.up_grad.grad, bf16[2048,3584]{1,0:T(8,128)(2,1)} %gate_w.3, bf16[2048,3584]{1,0:T(8,128)(2,1)} %up_w.3), custom_call_target="tpu_custom_call" | custom-call | flops 2818572288 | bytes 14680064 | tf_op jit(solution)/shard_map/backward_keep/pallas_call | solution.py:269
  88.3 2.1 %merge.3 = (bf16[48,1152]{1,0:T(8,128)(2,1)}, bf16[48,1152]{1,0:T(8,128)(2,1)}, bf16[48,1152]{1,0:T(8,128)(2,1)}, bf16[48,1152]{1,0:T(8,128)(2,1)}) custom-call(f32[192,1024]{1,0:T(8,128)} %backward_keep.1.keep, bf16[192,1024]{1,0:T(8,128)(2,1)} %copy-done.1, f32[192,128]{1,0:T(8,128)} %get-tuple-element.61.refs_0_), custom_call_target="tpu_custom_call" | custom-call | bytes 1572864 | tf_op jit(solution)/shard_map/merge/pallas_call | solution.py:355
  90.3 4.0 %collective-permute-start.19 = (bf16[48,1152]{1,0:T(8,128)(2,1)}, bf16[48,1152]{1,0:T(8,128)(2,1)S(1)}, u32[]{:S(2)}, u32[]{:S(2)}) collective-permute-start(bf16[48,1152]{1,0:T(8,128)(2,1)} %get-tuple-element.63), channel_id=1, source_target_pairs={{0,12},{4,0},{8,4},{12,8},{1,13},{5,1},{9,5},{13,9},{2,14},{6,2},{... | collective-permute-start | bytes 331784 | tf_op jit(solution)/shard_map/ppermute | solution.py:45
  94.8 3.2 %collective-permute-done.19.refs_1_ = bf16[48,1152]{1,0:T(8,128)(2,1)S(1)} collective-permute-done((bf16[48,1152]{1,0:T(8,128)(2,1)}, bf16[48,1152]{1,0:T(8,128)(2,1)S(1)}, u32[]{:S(2)}, u32[]{:S(2)}) %collective-permute-start.19) | collective-permute-done | bytes 110624 | tf_op jit(solution)/shard_map/ppermute | solution.py:45
  98.0 7.1 %collective-permute-done.20.refs_2_ = bf16[48,1152]{1,0:T(8,128)(2,1)S(1)} collective-permute-done((bf16[48,1152]{1,0:T(8,128)(2,1)}, bf16[48,1152]{1,0:T(8,128)(2,1)S(1)}, u32[]{:S(2)}, u32[]{:S(2)}) %collective-permute-start.20) | collective-permute-done | bytes 110624 | tf_op jit(solution)/shard_map/ppermute | solution.py:45
  105.8 2.5 %combine_router.1.refs_0_ = bf16[128,1152]{1,0:T(8,128)(2,1)} custom-call(bf16[192,128]{1,0:T(8,128)(2,1)} %get-tuple-element.57.first, bf16[192,128]{1,0:T(8,128)(2,1)} %get-tuple-element.58.second, bf16[48,1152]{1,0:T(8,128)(2,1)} %get-tuple-element.62.refs_0_, bf16[48,1152]{1,0:T(8,128)(2,1)} %copy-done.12, bf16[48,1152]{1,0:T(8,128)(2,1)} %copy-done.13, ...), custom_call_target="tpu_custom_call" | custom-call | flops 56623104 | bytes 442368 | tf_op jit(solution)/shard_map/combine_router/pallas_call | solution.py:422
  108.3 1.5 collective-permute-start.22
  110.5 2.0 %merge.2 = (bf16[48,1024]{1,0:T(8,128)(2,1)}, bf16[48,1024]{1,0:T(8,128)(2,1)}, bf16[48,1024]{1,0:T(8,128)(2,1)}, bf16[48,1024]{1,0:T(8,128)(2,1)}) custom-call(f32[192,1024]{1,0:T(8,128)} %get-tuple-element.51.keep, bf16[192,1024]{1,0:T(8,128)(2,1)} %copy-done), custom_call_target="tpu_custom_call" | custom-call | bytes 1572864 | tf_op jit(solution)/shard_map/merge/pallas_call | solution.py:355
  113.4 1.0 collective-permute-start.14
  114.4 2.0 %collective-permute-start.15 = (bf16[48,1024]{1,0:T(8,128)(2,1)}, bf16[48,1024]{1,0:T(8,128)(2,1)S(1)}, u32[]{:S(2)}, u32[]{:S(2)}) collective-permute-start(bf16[48,1024]{1,0:T(8,128)(2,1)} %get-tuple-element.56), channel_id=1, source_target_pairs={{0,4},{4,8},{8,12},{12,0},{1,5},{5,9},{9,13},{13,1},{2,6},{6,10},{... | collective-permute-start | bytes 294920 | tf_op jit(solution)/shard_map/ppermute | solution.py:45
  116.4 9.9 %columns_grad.3 = bf16[2048,3584]{1,0:T(8,128)(2,1)} custom-call(bf16[192,2048]{1,0:T(8,128)(2,1)} %get-tuple-element.68.rows, bf16[192,3584]{1,0:T(8,128)(2,1)} %get-tuple-element.60.up_grad.grad), custom_call_target="tpu_custom_call" | custom-call | flops 2818572288 | bytes 14680064 | tf_op jit(solution)/shard_map/columns_grad/pallas_call | solution.py:297
  127.0 2.2 %combine.1.refs_0_ = bf16[128,1024]{1,0:T(8,128)(2,1)} custom-call(bf16[192,128]{1,0:T(8,128)(2,1)} %get-tuple-element.38.weights, bf16[48,1024]{1,0:T(8,128)(2,1)} %get-tuple-element.53.refs_0_, bf16[48,1024]{1,0:T(8,128)(2,1)} %copy-done.15, bf16[48,1024]{1,0:T(8,128)(2,1)} %copy-done.16, bf16[48,1024]{1,0:T(8,128)(2,1)} %copy-done.17), custom_call_target="tpu_custom_call" | custom-call | flops 50331648 | bytes 393216 | tf_op jit(solution)/shard_map/combine/pallas_call | solution.py:375
  130.5 2.1 %add_pieces.3.own = bf16[128,1152]{1,0:T(8,128)(2,1)} custom-call(bf16[128,1152]{1,0:T(8,128)(2,1)} %combine_router.1.refs_0_, bf16[128,1152]{1,0:T(8,128)(2,1)} %copy-done.2), custom_call_target="tpu_custom_call" | custom-call | bytes 884736 | tf_op jit(solution)/shard_map/add_pieces/pallas_call | solution.py:446
  132.6 9.9 %columns_grad.2 = bf16[2048,3584]{1,0:T(8,128)(2,1)} custom-call(bf16[192,2048]{1,0:T(8,128)(2,1)} %get-tuple-element.68.rows, bf16[192,3584]{1,0:T(8,128)(2,1)} %get-tuple-element.59.gate_grad.grad), custom_call_target="tpu_custom_call" | custom-call | flops 2818572288 | bytes 14680064 | tf_op jit(solution)/shard_map/columns_grad/pallas_call | solution.py:297
  143.3 1.8 %add_pieces.2.own = bf16[128,1024]{1,0:T(8,128)(2,1)} custom-call(bf16[128,1024]{1,0:T(8,128)(2,1)} %combine.1.refs_0_, bf16[128,1024]{1,0:T(8,128)(2,1)} %copy-done.4), custom_call_target="tpu_custom_call" | custom-call | bytes 786432 | tf_op jit(solution)/shard_map/add_pieces/pallas_call | solution.py:446
  145.6 9.7 %rows_grad.1 = bf16[3584,2048]{1,0:T(8,128)(2,1)} custom-call(bf16[192,3584]{1,0:T(8,128)(2,1)} %get-tuple-element.48.refs_6_.hidden, bf16[192,2048]{1,0:T(8,128)(2,1)} %get-tuple-element.69.scaled), custom_call_target="tpu_custom_call" | custom-call | flops 2818572288 | bytes 14680064 | tf_op jit(solution)/shard_map/rows_grad/pallas_call | solution.py:318
  156.0 2.5 %finish.2 = bf16[128,2048]{1,0:T(8,128)(2,1)} custom-call(s32[5]{0:T(128)} %pad_add_fusion.scal, bf16[128,1024]{1,0:T(8,128)(2,1)} %add_pieces.2.own, bf16[128,1024]{1,0:T(8,128)(2,1)} %copy-done.5), custom_call_target="tpu_custom_call" | custom-call | bytes 524288 | tf_op jit(solution)/shard_map/finish/pallas_call | solution.py:472
  159.2 2.7 %finish.3 = (bf16[128,2048]{1,0:T(8,128)(2,1)}, f32[128,2]{1,0:T(8,128)}) custom-call(s32[5]{0:T(128)} %pad_add_fusion.scal, bf16[128,1152]{1,0:T(8,128)(2,1)} %add_pieces.3.own, bf16[128,1152]{1,0:T(8,128)(2,1)} %copy-done.3), custom_call_target="tpu_custom_call" | custom-call | bytes 589824 | tf_op jit(solution)/shard_map/finish/pallas_call | solution.py:472
  161.9 1.5 copy.15
  (87 shorter events, 12.5 us)
Async XLA Ops:
  7.9 9.1 %collective-permute-start.6 = (bf16[48,1024]{1,0:T(8,128)(2,1)}, bf16[48,1024]{1,0:T(8,128)(2,1)S(1)}, u32[]{:S(2)}, u32[]{:S(2)}) collective-permute-start(bf16[48,1024]{1,0:T(8,128)(2,1)} %get-tuple-element.45), channel_id=1, source_target_pairs={{0,4},{4,8},{8,12},{12,0},{1,5},{5,9},{9,13},{13,1},{2,6},{6,10},{... | collective-permute-start | bytes 294920 | tf_op jit(solution)/shard_map/ppermute | solution.py:45
  10.9 13.8 %collective-permute-start = (bf16[48,1152]{1,0:T(8,128)(2,1)}, bf16[48,1152]{1,0:T(8,128)(2,1)S(1)}, u32[]{:S(2)}, u32[]{:S(2)}) collective-permute-start(bf16[48,1152]{1,0:T(8,128)(2,1)} %get-tuple-element.41), channel_id=1, source_target_pairs={{0,4},{4,8},{8,12},{12,0},{1,5},{5,9},{9,13},{13,1},{2,6},{6,10},{... | collective-permute-start | bytes 331784 | tf_op jit(solution)/shard_map/ppermute | solution.py:45
  12.5 11.7 %collective-permute-start.7 = (bf16[48,1024]{1,0:T(8,128)(2,1)}, bf16[48,1024]{1,0:T(8,128)(2,1)S(1)}, u32[]{:S(2)}, u32[]{:S(2)}) collective-permute-start(bf16[48,1024]{1,0:T(8,128)(2,1)} %get-tuple-element.46), channel_id=1, source_target_pairs={{0,8},{4,12},{8,0},{12,4},{1,9},{5,13},{9,1},{13,5},{2,10},{6,14},... | collective-permute-start | bytes 294920 | tf_op jit(solution)/shard_map/ppermute | solution.py:45
  13.6 10.7 %collective-permute-start.8 = (bf16[48,1024]{1,0:T(8,128)(2,1)}, bf16[48,1024]{1,0:T(8,128)(2,1)S(1)}, u32[]{:S(2)}, u32[]{:S(2)}) collective-permute-start(bf16[48,1024]{1,0:T(8,128)(2,1)} %get-tuple-element.47), channel_id=1, source_target_pairs={{0,12},{4,0},{8,4},{12,8},{1,13},{5,1},{9,5},{13,9},{2,14},{6,2},{... | collective-permute-start | bytes 294920 | tf_op jit(solution)/shard_map/ppermute | solution.py:45
  16.5 13.1 %collective-permute-start.1 = (bf16[48,1152]{1,0:T(8,128)(2,1)}, bf16[48,1152]{1,0:T(8,128)(2,1)S(1)}, u32[]{:S(2)}, u32[]{:S(2)}) collective-permute-start(bf16[48,1152]{1,0:T(8,128)(2,1)} %get-tuple-element.42), channel_id=1, source_target_pairs={{0,8},{4,12},{8,0},{12,4},{1,9},{5,13},{9,1},{13,5},{2,10},{6,14},... | collective-permute-start | bytes 331784 | tf_op jit(solution)/shard_map/ppermute | solution.py:45
  17.0 13.2 %copy-start.18 = (bf16[48,1024]{1,0:T(8,128)(2,1)}, bf16[48,1024]{1,0:T(8,128)(2,1)S(1)}, u32[]{:S(2)}) copy-start(bf16[48,1024]{1,0:T(8,128)(2,1)S(1)} %collective-permute-done.6.refs_0_) | copy-start | bytes 294916
  17.0 12.5 %collective-permute-start.2 = (bf16[48,1152]{1,0:T(8,128)(2,1)}, bf16[48,1152]{1,0:T(8,128)(2,1)S(1)}, u32[]{:S(2)}, u32[]{:S(2)}) collective-permute-start(bf16[48,1152]{1,0:T(8,128)(2,1)} %get-tuple-element.43), channel_id=1, source_target_pairs={{0,12},{4,0},{8,4},{12,8},{1,13},{5,1},{9,5},{13,9},{2,14},{6,2},{... | collective-permute-start | bytes 331784 | tf_op jit(solution)/shard_map/ppermute | solution.py:45
  24.3 5.9 %copy-start.19 = (bf16[48,1024]{1,0:T(8,128)(2,1)}, bf16[48,1024]{1,0:T(8,128)(2,1)S(1)}, u32[]{:S(2)}) copy-start(bf16[48,1024]{1,0:T(8,128)(2,1)S(1)} %collective-permute-done.7.refs_1_) | copy-start | bytes 294916
  24.3 5.8 %collective-permute-start.9 = (bf16[48,1024]{1,0:T(8,128)(2,1)S(1)}, bf16[48,1024]{1,0:T(8,128)(2,1)S(1)}, u32[]{:S(2)}, u32[]{:S(2)}) collective-permute-start(bf16[48,1024]{1,0:T(8,128)(2,1)S(1)} %collective-permute-done.6.refs_0_), channel_id=1, source_target_pairs={{0,1},{1,0},{2,3},{3,2},{4,5},{5,4},{6,7},{7,6},{8,9},{9,8},{10,11... | collective-permute-start | bytes 294920 | tf_op jit(solution)/shard_map/ppermute | solution.py:45
  24.3 5.9 %copy-start.20 = (bf16[48,1024]{1,0:T(8,128)(2,1)}, bf16[48,1024]{1,0:T(8,128)(2,1)S(1)}, u32[]{:S(2)}) copy-start(bf16[48,1024]{1,0:T(8,128)(2,1)S(1)} %collective-permute-done.8.refs_2_) | copy-start | bytes 294916
  24.3 5.9 %collective-permute-start.10 = (bf16[48,1024]{1,0:T(8,128)(2,1)S(1)}, bf16[48,1024]{1,0:T(8,128)(2,1)S(1)}, u32[]{:S(2)}, u32[]{:S(2)}) collective-permute-start(bf16[48,1024]{1,0:T(8,128)(2,1)S(1)} %collective-permute-done.7.refs_1_), channel_id=1, source_target_pairs={{0,1},{1,0},{2,3},{3,2},{4,5},{5,4},{6,7},{7,6},{8,9},{9,8},{10,11... | collective-permute-start | bytes 294920 | tf_op jit(solution)/shard_map/ppermute | solution.py:45
  24.8 22.8 %copy-start.6 = (bf16[48,1152]{1,0:T(8,128)(2,1)}, bf16[48,1152]{1,0:T(8,128)(2,1)S(1)}, u32[]{:S(2)}) copy-start(bf16[48,1152]{1,0:T(8,128)(2,1)S(1)} %collective-permute-done.refs_0_) | copy-start | bytes 331780
  24.8 5.4 %collective-permute-start.11 = (bf16[48,1024]{1,0:T(8,128)(2,1)S(1)}, bf16[48,1024]{1,0:T(8,128)(2,1)S(1)}, u32[]{:S(2)}, u32[]{:S(2)}) collective-permute-start(bf16[48,1024]{1,0:T(8,128)(2,1)S(1)} %collective-permute-done.8.refs_2_), channel_id=1, source_target_pairs={{0,1},{1,0},{2,3},{3,2},{4,5},{5,4},{6,7},{7,6},{8,9},{9,8},{10,11... | collective-permute-start | bytes 294920 | tf_op jit(solution)/shard_map/ppermute | solution.py:45
  29.5 18.1 %copy-start.7 = (bf16[48,1152]{1,0:T(8,128)(2,1)}, bf16[48,1152]{1,0:T(8,128)(2,1)S(1)}, u32[]{:S(2)}) copy-start(bf16[48,1152]{1,0:T(8,128)(2,1)S(1)} %collective-permute-done.1.refs_1_) | copy-start | bytes 331780
  29.5 18.1 %collective-permute-start.3 = (bf16[48,1152]{1,0:T(8,128)(2,1)S(1)}, bf16[48,1152]{1,0:T(8,128)(2,1)S(1)}, u32[]{:S(2)}, u32[]{:S(2)}) collective-permute-start(bf16[48,1152]{1,0:T(8,128)(2,1)S(1)} %collective-permute-done.refs_0_), channel_id=1, source_target_pairs={{0,1},{1,0},{2,3},{3,2},{4,5},{5,4},{6,7},{7,6},{8,9},{9,8},{10,11... | collective-permute-start | bytes 331784 | tf_op jit(solution)/shard_map/ppermute | solution.py:45
  29.6 18.1 %copy-start.8 = (bf16[48,1152]{1,0:T(8,128)(2,1)}, bf16[48,1152]{1,0:T(8,128)(2,1)S(1)}, u32[]{:S(2)}) copy-start(bf16[48,1152]{1,0:T(8,128)(2,1)S(1)} %collective-permute-done.2.refs_2_) | copy-start | bytes 331780
  29.6 18.1 %collective-permute-start.4 = (bf16[48,1152]{1,0:T(8,128)(2,1)S(1)}, bf16[48,1152]{1,0:T(8,128)(2,1)S(1)}, u32[]{:S(2)}, u32[]{:S(2)}) collective-permute-start(bf16[48,1152]{1,0:T(8,128)(2,1)S(1)} %collective-permute-done.1.refs_1_), channel_id=1, source_target_pairs={{0,1},{1,0},{2,3},{3,2},{4,5},{5,4},{6,7},{7,6},{8,9},{9,8},{10,11... | collective-permute-start | bytes 331784 | tf_op jit(solution)/shard_map/ppermute | solution.py:45
  30.1 17.6 %collective-permute-start.5 = (bf16[48,1152]{1,0:T(8,128)(2,1)S(1)}, bf16[48,1152]{1,0:T(8,128)(2,1)S(1)}, u32[]{:S(2)}, u32[]{:S(2)}) collective-permute-start(bf16[48,1152]{1,0:T(8,128)(2,1)S(1)} %collective-permute-done.2.refs_2_), channel_id=1, source_target_pairs={{0,1},{1,0},{2,3},{3,2},{4,5},{5,4},{6,7},{7,6},{8,9},{9,8},{10,11... | collective-permute-start | bytes 331784 | tf_op jit(solution)/shard_map/ppermute | solution.py:45
  65.8 11.1 %copy-start.24 = (bf16[192,1024]{1,0:T(8,128)(2,1)S(1)}, bf16[192,1024]{1,0:T(8,128)(2,1)}, u32[]{:S(2)}) copy-start(bf16[192,1024]{1,0:T(8,128)(2,1)} %get-tuple-element.52) | copy-start | bytes 1179652
  76.4 11.1 %collective-permute-start.18 = (bf16[192,1024]{1,0:T(8,128)(2,1)}, bf16[192,1024]{1,0:T(8,128)(2,1)S(1)}, u32[]{:S(2)}, u32[]{:S(2)}) collective-permute-start(bf16[192,1024]{1,0:T(8,128)(2,1)} %backward_send.1), channel_id=1, source_target_pairs={{0,1},{1,0},{2,3},{3,2},{4,5},{5,4},{6,7},{7,6},{8,9},{9,8},{10,11... | collective-permute-start | bytes 1179656 | tf_op jit(solution)/shard_map/ppermute | solution.py:45
  76.9 32.9 %collective-permute-start.12 = (bf16[192,1024]{1,0:T(8,128)(2,1)S(1)}, bf16[192,1024]{1,0:T(8,128)(2,1)S(1)}, u32[]{:S(2)}, u32[]{:S(2)}) collective-permute-start(bf16[192,1024]{1,0:T(8,128)(2,1)S(1)} %copy-done.24), channel_id=1, source_target_pairs={{0,1},{1,0},{2,3},{3,2},{4,5},{5,4},{6,7},{7,6},{8,9},{9,8},{10,11... | collective-permute-start | bytes 1179656 | tf_op jit(solution)/shard_map/ppermute | solution.py:45
  90.3 7.7 %collective-permute-start.19 = (bf16[48,1152]{1,0:T(8,128)(2,1)}, bf16[48,1152]{1,0:T(8,128)(2,1)S(1)}, u32[]{:S(2)}, u32[]{:S(2)}) collective-permute-start(bf16[48,1152]{1,0:T(8,128)(2,1)} %get-tuple-element.63), channel_id=1, source_target_pairs={{0,12},{4,0},{8,4},{12,8},{1,13},{5,1},{9,5},{13,9},{2,14},{6,2},{... | collective-permute-start | bytes 331784 | tf_op jit(solution)/shard_map/ppermute | solution.py:45
  94.3 10.8 %collective-permute-start.20 = (bf16[48,1152]{1,0:T(8,128)(2,1)}, bf16[48,1152]{1,0:T(8,128)(2,1)S(1)}, u32[]{:S(2)}, u32[]{:S(2)}) collective-permute-start(bf16[48,1152]{1,0:T(8,128)(2,1)} %get-tuple-element.64), channel_id=1, source_target_pairs={{0,8},{4,12},{8,0},{12,4},{1,9},{5,13},{9,1},{13,5},{2,10},{6,14},... | collective-permute-start | bytes 331784 | tf_op jit(solution)/shard_map/ppermute | solution.py:45
  94.5 10.6 %collective-permute-start.21 = (bf16[48,1152]{1,0:T(8,128)(2,1)}, bf16[48,1152]{1,0:T(8,128)(2,1)S(1)}, u32[]{:S(2)}, u32[]{:S(2)}) collective-permute-start(bf16[48,1152]{1,0:T(8,128)(2,1)} %get-tuple-element.65), channel_id=1, source_target_pairs={{0,4},{4,8},{8,12},{12,0},{1,5},{5,9},{9,13},{13,1},{2,6},{6,10},{... | collective-permute-start | bytes 331784 | tf_op jit(solution)/shard_map/ppermute | solution.py:45
  98.0 7.1 %copy-start.12 = (bf16[48,1152]{1,0:T(8,128)(2,1)}, bf16[48,1152]{1,0:T(8,128)(2,1)S(1)}, u32[]{:S(2)}) copy-start(bf16[48,1152]{1,0:T(8,128)(2,1)S(1)} %collective-permute-done.19.refs_1_) | copy-start | bytes 331780
  108.3 21.6 %collective-permute-start.22 = (bf16[128,1152]{1,0:T(8,128)(2,1)}, bf16[128,1152]{1,0:T(8,128)(2,1)S(1)}, u32[]{:S(2)}, u32[]{:S(2)}) collective-permute-start(bf16[128,1152]{1,0:T(8,128)(2,1)} %combine_router.1.refs_0_), channel_id=1, source_target_pairs={{0,2},{2,0},{1,3},{3,1},{4,6},{6,4},{5,7},{7,5},{8,10},{10,8},{9,1... | collective-permute-start | bytes 884744 | tf_op jit(solution)/shard_map/ppermute | solution.py:45
  112.5 13.9 %collective-permute-start.13 = (bf16[48,1024]{1,0:T(8,128)(2,1)}, bf16[48,1024]{1,0:T(8,128)(2,1)S(1)}, u32[]{:S(2)}, u32[]{:S(2)}) collective-permute-start(bf16[48,1024]{1,0:T(8,128)(2,1)} %get-tuple-element.54), channel_id=1, source_target_pairs={{0,12},{4,0},{8,4},{12,8},{1,13},{5,1},{9,5},{13,9},{2,14},{6,2},{... | collective-permute-start | bytes 294920 | tf_op jit(solution)/shard_map/ppermute | solution.py:45
  113.4 12.9 %collective-permute-start.14 = (bf16[48,1024]{1,0:T(8,128)(2,1)}, bf16[48,1024]{1,0:T(8,128)(2,1)S(1)}, u32[]{:S(2)}, u32[]{:S(2)}) collective-permute-start(bf16[48,1024]{1,0:T(8,128)(2,1)} %get-tuple-element.55), channel_id=1, source_target_pairs={{0,8},{4,12},{8,0},{12,4},{1,9},{5,13},{9,1},{13,5},{2,10},{6,14},... | collective-permute-start | bytes 294920 | tf_op jit(solution)/shard_map/ppermute | solution.py:45
  114.4 12.0 %collective-permute-start.15 = (bf16[48,1024]{1,0:T(8,128)(2,1)}, bf16[48,1024]{1,0:T(8,128)(2,1)S(1)}, u32[]{:S(2)}, u32[]{:S(2)}) collective-permute-start(bf16[48,1024]{1,0:T(8,128)(2,1)} %get-tuple-element.56), channel_id=1, source_target_pairs={{0,4},{4,8},{8,12},{12,0},{1,5},{5,9},{9,13},{13,1},{2,6},{6,10},{... | collective-permute-start | bytes 294920 | tf_op jit(solution)/shard_map/ppermute | solution.py:45
  129.3 13.3 %collective-permute-start.16 = (bf16[128,1024]{1,0:T(8,128)(2,1)}, bf16[128,1024]{1,0:T(8,128)(2,1)S(1)}, u32[]{:S(2)}, u32[]{:S(2)}) collective-permute-start(bf16[128,1024]{1,0:T(8,128)(2,1)} %combine.1.refs_0_), channel_id=1, source_target_pairs={{0,2},{2,0},{1,3},{3,1},{4,6},{6,4},{5,7},{7,5},{8,10},{10,8},{9,1... | collective-permute-start | bytes 786440 | tf_op jit(solution)/shard_map/ppermute | solution.py:45
  132.6 25.9 %collective-permute-start.23 = (bf16[128,1152]{1,0:T(8,128)(2,1)}, bf16[128,1152]{1,0:T(8,128)(2,1)S(1)}, u32[]{:S(2)}, u32[]{:S(2)}) collective-permute-start(bf16[128,1152]{1,0:T(8,128)(2,1)} %add_pieces.3.own), channel_id=1, source_target_pairs={{0,1},{1,0},{2,3},{3,2},{4,5},{5,4},{6,7},{7,6},{8,9},{9,8},{10,11... | collective-permute-start | bytes 884744 | tf_op jit(solution)/shard_map/ppermute | solution.py:45
  145.0 10.2 %collective-permute-start.17 = (bf16[128,1024]{1,0:T(8,128)(2,1)}, bf16[128,1024]{1,0:T(8,128)(2,1)S(1)}, u32[]{:S(2)}, u32[]{:S(2)}) collective-permute-start(bf16[128,1024]{1,0:T(8,128)(2,1)} %add_pieces.2.own), channel_id=1, source_target_pairs={{0,1},{1,0},{2,3},{3,2},{4,5},{5,4},{6,7},{7,6},{8,9},{9,8},{10,11... | collective-permute-start | bytes 786440 | tf_op jit(solution)/shard_map/ppermute | solution.py:45
  (17 other events, 11.6 us)

commit v2 on v0

v2 whole, which is shorter than its diff:
```python
import functools

import jax
import jax.numpy as jnp
from jax import lax
from jax.experimental import pallas as pl
from jax.experimental.pallas import tpu as pltpu
from jax.sharding import PartitionSpec as P

FF = 7168
CAP = 48
LANES = 128
F32 = jnp.float32
BF16 = jnp.bfloat16


def dot(left, right, left_dim=1, right_dim=0):
    return lax.dot_general(
        left, right, (((left_dim,), (right_dim,)), ((), ())), preferred_element_type=F32
    )


def params(megabytes=6, slots=0):
    scale = 1 if slots <= 256 else 4
    return pltpu.CompilerParams(vmem_limit_bytes=megabytes * scale * 1024 * 1024)


def tile_of(size, most):
    for tile in (1024, 512, 256):
        if tile <= most and size % tile == 0:
            return tile
    return size


def padded(slots):
    return -(-slots // 256) * 256


IN_VMEM = pl.BlockSpec(memory_space=pltpu.VMEM)
ANYWHERE = pl.BlockSpec(memory_space=pl.ANY)


def own_half(half):
    return pl.multiple_of(lax.axis_index("tp") * half, half)


def other_half(half):
    return pl.multiple_of((1 - lax.axis_index("tp")) * half, half)


def cost(flops, nbytes):
    return pl.CostEstimate(flops=int(flops), bytes_accessed=int(nbytes), transcendentals=0)


def shift(value, axis, step):
    count = lax.axis_size(axis)
    return lax.ppermute(value, axis, [(j, (j + step) % count) for j in range(count)])


def pick_tokens_body(n, hid, reps, ids, gates, tokens, *outs):
    toks, (first, second, weighted) = outs[:n], outs[n:]
    rows, width = tokens.shape
    half = width // 2
    upper = (
        lax.broadcasted_iota(jnp.int32, (rows, rows), 0)
        <= lax.broadcasted_iota(jnp.int32, (rows, rows), 1)
    ).astype(BF16)
    me, rep = lax.axis_index("ed"), lax.axis_index("dp") * 2 + lax.axis_index("tp")
    slot_index = lax.broadcasted_iota(jnp.int32, (CAP, rows), 0).astype(F32)
    gate0, gate1 = gates[0:1, :].astype(F32), gates[1:2, :].astype(F32)
    ids0, ids1 = ids[0:1, :], ids[1:2, :]
    for s in range(n):
        owner = lax.rem(me + s, n)
        expert = ((owner * reps + rep) * hid) // FF
        hit0 = jnp.where(ids0 == expert, 1.0, 0.0)
        hit1 = jnp.where(ids1 == expert, 1.0, 0.0)
        chosen = jnp.broadcast_to(hit0 + hit1, (8, rows)).astype(BF16)
        place = dot(chosen, upper)[0:1] - 1.0
        here = jnp.where(place == slot_index, 1.0, 0.0)
        placed0, placed1 = here * hit0, here * hit1
        placed = (placed0 + placed1).astype(BF16)
        span = pl.ds(s * CAP, CAP)
        first[span, :] = placed0.astype(BF16)
        second[span, :] = placed1.astype(BF16)
        weighted[span, :] = (placed0 * gate0 + placed1 * gate1).astype(BF16)
        if s == 0:
            toks[0][...] = dot(placed, tokens[...]).astype(BF16)
        else:
            toks[s][...] = dot(placed, tokens[:, pl.ds(own_half(half), half)]).astype(BF16)


def pick_tokens(n, hid, ids, gates, tokens):
    rows, width = tokens.shape
    slots = n * CAP
    out = (
        [jax.ShapeDtypeStruct((CAP, width), BF16)]
        + [jax.ShapeDtypeStruct((CAP, width // 2), BF16)] * (n - 1)
        + [jax.ShapeDtypeStruct((slots, rows), BF16)] * 3
    )
    got = pl.pallas_call(
        functools.partial(pick_tokens_body, n, hid, lax.axis_size(("dp", "tp"))),
        out_shape=out,
        compiler_params=params(),
        cost_estimate=cost(2 * slots * rows * width, 4 * rows * width),
        name="pick_tokens",
    )(ids, gates, tokens)
    return got[:n], got[n:]


def pick_grads_body(n, after, first, second, weighted, grads, *outs):
    half = grads.shape[1] // 2
    for s in range(n):
        span = pl.ds(s * CAP, CAP)
        placed = first[span, :] + second[span, :]
        coef = jnp.sum(weighted[span, :].astype(F32), axis=1, keepdims=True)
        coef = jnp.broadcast_to(coef, (CAP, LANES)).astype(BF16)
        if s == 0:
            outs[0][...] = dot(placed, grads[...]).astype(BF16)
            outs[n][...] = coef
        else:
            outs[s][:, 0:half] = dot(placed, grads[:, pl.ds(own_half(half), half)]).astype(BF16)
            outs[s][:, half:] = coef


def pick_grads(after, n, placing, grads):
    rows, width = grads.shape
    out = (
        [jax.ShapeDtypeStruct((CAP, width), BF16)]
        + [jax.ShapeDtypeStruct((CAP, width // 2 + LANES), BF16)] * (n - 1)
        + [jax.ShapeDtypeStruct((CAP, LANES), BF16)]
    )
    got = pl.pallas_call(
        functools.partial(pick_grads_body, n),
        out_shape=out,
        in_specs=[ANYWHERE] + [IN_VMEM] * 4,
        out_specs=[IN_VMEM] * (n + 1),
        compiler_params=params(),
        cost_estimate=cost(2 * n * CAP * rows * width, 4 * rows * width),
        name="pick_grads",
    )(after, *placing, grads)
    return got[:n], got[n]


def load_body(after, weight, held, done, sems):
    rows = weight.shape[0] // sems.shape[0]
    copies = [
        pltpu.make_async_copy(weight.at[pl.ds(j * rows, rows)], held.at[pl.ds(j * rows, rows)], sems.at[j])
        for j in range(sems.shape[0])
    ]
    for copy in copies:
        copy.start()
    done[...] = jnp.zeros_like(done)
    for copy in copies:
        copy.wait()


def load(after, weight):
    return pl.pallas_call(
        load_body,
        out_shape=[pltpu.VMEM(weight.shape, BF16), jax.ShapeDtypeStruct((8, LANES), F32)],
        in_specs=[ANYWHERE] * 2,
        out_specs=[IN_VMEM] * 2,
        scratch_shapes=[pltpu.SemaphoreType.DMA((4,))],
        compiler_params=params(1),
        cost_estimate=cost(0, 2 * weight.size),
        name="load",
    )(after, weight)


def stack_body(after, *refs):
    pieces, out = refs[:-1], refs[-1]
    for s, piece in enumerate(pieces):
        out[s * CAP:(s + 1) * CAP, :] = piece[...]


def stack(after, pieces):
    wide = pieces[0].shape[1]
    return pl.pallas_call(
        stack_body,
        out_shape=jax.ShapeDtypeStruct((len(pieces) * CAP, wide), BF16),
        in_specs=[ANYWHERE] + [IN_VMEM] * len(pieces),
        out_specs=IN_VMEM,
        compiler_params=params(),
        cost_estimate=cost(0, 4 * len(pieces) * CAP * wide),
        name="stack",
    )(after, *pieces)


def gather_rows(half, own, direct, other, held):
    held[0:CAP, :] = own[...]
    held[CAP:held.shape[0], pl.ds(own_half(half), half)] = direct[:, 0:half]
    held[CAP:held.shape[0], pl.ds(other_half(half), half)] = other[:, 0:half]


def clear_padding(slots, ref):
    if ref.shape[0] > slots:
        ref[slots:, :] = jnp.zeros((ref.shape[0] - slots, ref.shape[1]), ref.dtype)


def forward_body(slots, own, direct, other, gate_w, up_w, rows_out, hidden, act, slope):
    width, hid = gate_w.shape
    gather_rows(width // 2, own, direct, other, rows_out.at[pl.ds(0, slots)])
    clear_padding(slots, rows_out)
    clear_padding(slots, hidden)
    rows = rows_out[0:slots, :]
    tile = tile_of(hid, 512)
    for at in range(0, hid, tile):
        span = slice(at, at + tile)
        pre_gate = dot(rows, gate_w[:, span])
        pre_up = dot(rows, up_w[:, span])
        logistic = jax.nn.sigmoid(pre_gate)
        silu = pre_gate * logistic
        hidden[0:slots, span] = (silu * pre_up).astype(BF16)
        act[:, span] = silu.astype(BF16)
        slope[:, span] = (pre_up * logistic * (1.0 + pre_gate * (1.0 - logistic))).astype(BF16)


def forward(n, own, direct, other, gate_w, up_w):
    width, hid = gate_w.shape
    slots = n * CAP
    return pl.pallas_call(
        functools.partial(forward_body, slots),
        out_shape=[
            pltpu.VMEM((padded(slots), width), BF16),
            pltpu.VMEM((padded(slots), hid), BF16),
            pltpu.VMEM((slots, hid), BF16),
            pltpu.VMEM((slots, hid), BF16),
        ],
        in_specs=[IN_VMEM] * 5,
        out_specs=[IN_VMEM] * 4,
        compiler_params=params(6, slots),
        cost_estimate=cost(4 * slots * width * hid, 2 * slots * width),
        name="forward",
    )(own, direct, other, gate_w, up_w)


def streamed(down, buffers, sems, tile, columns):
    def copy(step):
        return pltpu.make_async_copy(
            down.at[pl.ds(step * tile, tile), columns],
            buffers.at[step % buffers.shape[0]],
            sems.at[step % buffers.shape[0]],
        )

    return copy


def expert_out_body(mine, slots, hidden, down, out, buffers, sems):
    hid, width = down.shape
    half = width // 2
    tile = buffers.shape[1]
    start = own_half(half) if mine else other_half(half)
    copy = streamed(down, buffers, sems, tile, pl.ds(start, half))
    steps = hid // tile
    depth = buffers.shape[0]
    for step in range(min(depth, steps)):
        copy(step).start()
    total = None
    for step in range(steps):
        copy(step).wait()
        part = dot(hidden[0:slots, step * tile:(step + 1) * tile], buffers[step % depth])
        total = part if total is None else total + part
        if step + depth < steps:
            copy(step + depth).start()
    out[...] = total.astype(out.dtype)


def expert_out(mine, kind, slots, hidden, down):
    hid, width = down.shape
    half = width // 2
    tile = tile_of(hid, 512)
    return pl.pallas_call(
        functools.partial(expert_out_body, mine, slots),
        out_shape=jax.ShapeDtypeStruct((slots, half), kind),
        in_specs=[IN_VMEM, ANYWHERE],
        out_specs=IN_VMEM,
        scratch_shapes=[pltpu.VMEM((4, tile, half), BF16), pltpu.SemaphoreType.DMA((4,))],
        compiler_params=params(8, slots),
        cost_estimate=cost(2 * slots * half * hid, 2 * half * hid),
        name="out_keep" if mine else "out_send",
    )(hidden, down)


def back_body(after, own, coef_own, direct, other, hidden, act, slope, down, scaled, gate_grad,
              up_grad, router, held, coef, buffers, sems):
    hid, width = down.shape
    half = width // 2
    slots = held.shape[0]
    depth, tile = buffers.shape[0:2]
    steps = hid // tile
    copy = streamed(down, buffers, sems, tile, slice(None))
    for step in range(min(depth, steps)):
        copy(step).start()
    gather_rows(half, own, direct, other, held)
    coef[0:CAP, :] = coef_own[...].astype(F32)
    coef[CAP:, :] = direct[:, half:].astype(F32)
    scale = coef[:, 0:1]
    scaled[0:slots, :] = (scale * held[...].astype(F32)).astype(BF16)
    for ref in (scaled, gate_grad, up_grad):
        clear_padding(slots, ref)
    score = None
    for step in range(steps):
        span = slice(step * tile, (step + 1) * tile)
        copy(step).wait()
        back = dot(held[...], buffers[step % depth], 1, 1)
        if step + depth < steps:
            copy(step + depth).start()
        part = jnp.sum(hidden[0:slots, span].astype(F32) * back, axis=1, keepdims=True)
        score = part if score is None else score + part
        grad = scale * back
        gate_grad[0:slots, span] = (grad * slope[:, span].astype(F32)).astype(BF16)
        up_grad[0:slots, span] = (grad * act[:, span].astype(F32)).astype(BF16)
    router[...] = jnp.broadcast_to(score, router.shape)


def back(after, n, own, coef_own, direct, other, hidden, act, slope, down):
    hid, width = down.shape
    slots = n * CAP
    tile = tile_of(hid, 256)
    return pl.pallas_call(
        back_body,
        out_shape=[
            pltpu.VMEM((padded(slots), width), BF16),
            pltpu.VMEM((padded(slots), hid), BF16),
            pltpu.VMEM((padded(slots), hid), BF16),
            jax.ShapeDtypeStruct((slots, LANES), F32),
        ],
        in_specs=[ANYWHERE] + [IN_VMEM] * 7 + [ANYWHERE],
        out_specs=[IN_VMEM] * 4,
        scratch_shapes=[
            pltpu.VMEM((slots, width), BF16),
            pltpu.VMEM((slots, LANES), F32),
            pltpu.VMEM((4, tile, width), BF16),
            pltpu.SemaphoreType.DMA((4,)),
        ],
        compiler_params=params(8, slots),
        cost_estimate=cost(2 * slots * width * hid, 2 * width * hid),
        name="back",
    )(after, own, coef_own, direct, other, hidden, act, slope, down)


def input_body(mine, gate_grad, up_grad, gate_w, up_w, out):
    slots, half = out.shape
    start = own_half(half) if mine else other_half(half)
    tile = tile_of(half, 256)
    for at in range(0, half, tile):
        span = pl.ds(start + at, tile)
        value = dot(gate_grad[0:slots, :], gate_w[span, :], 1, 1)
        value += dot(up_grad[0:slots, :], up_w[span, :], 1, 1)
        out[:, at:at + tile] = value.astype(out.dtype)


def input_part(mine, kind, slots, gate_grad, up_grad, gate_w, up_w):
    width, hid = gate_w.shape
    return pl.pallas_call(
        functools.partial(input_body, mine),
        out_shape=jax.ShapeDtypeStruct((slots, width // 2), kind),
        in_specs=[IN_VMEM] * 4,
        out_specs=IN_VMEM,
        compiler_params=params(6, slots),
        cost_estimate=cost(2 * slots * width * hid, 2 * slots * width),
        name="input_keep" if mine else "input_send",
    )(gate_grad, up_grad, gate_w, up_w)


def weight_grad_body(left, right, out, buffers, sems):
    depth, tile, columns = buffers.shape
    steps = out.shape[0] // tile
    piece = tile_of(columns, 512)

    def copy(step):
        slot = step % depth
        return pltpu.make_async_copy(
            buffers.at[slot], out.at[pl.ds(step * tile, tile), :], sems.at[slot]
        )

    for step in range(steps):
        flipped = left[:, step * tile:(step + 1) * tile].T
        if step >= depth:
            copy(step - depth).wait()
        for at in range(0, columns, piece):
            value = dot(flipped, right[:, at:at + piece])
            buffers[step % depth, :, at:at + piece] = value.astype(BF16)
        copy(step).start()
    for step in range(max(0, steps - depth), steps):
        copy(step).wait()


def weight_grad(left, right, name):
    slots, rows = left.shape
    columns = right.shape[1]
    tile = tile_of(rows, 256)
    return pl.pallas_call(
        weight_grad_body,
        out_shape=pltpu.HBM((rows, columns), BF16),
        in_specs=[IN_VMEM] * 2,
        out_specs=ANYWHERE,
        scratch_shapes=[pltpu.VMEM((4, tile, columns), BF16), pltpu.SemaphoreType.DMA((4,))],
        compiler_params=params(12, slots),
        cost_estimate=cost(2 * slots * rows * columns, 2 * rows * columns),
        name=name,
    )(left, right)


def three_parts(value):
    high = value.astype(BF16)
    rest = value - high.astype(F32)
    mid = rest.astype(BF16)
    return high, mid, (rest - mid.astype(F32)).astype(BF16)


def write_chunks(n, total, got, router, outs):
    half = total.shape[1]
    for s in range(n):
        span = slice(s * CAP, (s + 1) * CAP)
        outs[s][:, 0:half] = (total[span, :] + got[span, :].astype(F32)).astype(BF16)
        if router is not None:
            high, mid, low = three_parts(router[span, :])
            lane = lax.broadcasted_iota(jnp.int32, (CAP, LANES), 1)
            outs[s][:, half:] = jnp.where(
                lane == 0, high, jnp.where(lane == 1, mid, jnp.where(lane == 2, low, jnp.zeros_like(low)))
            )


def merge_body(n, keep, got, *refs):
    write_chunks(n, keep[...], got, refs[0] if len(refs) > n else None, refs[-n:])


def merge(n, keep, got, *router):
    wide = keep.shape[1] + LANES * len(router)
    return pl.pallas_call(
        functools.partial(merge_body, n),
        out_shape=[jax.ShapeDtypeStruct((CAP, wide), BF16)] * n,
        compiler_params=params(),
        cost_estimate=cost(0, 8 * keep.size),
        name="merge",
    )(keep, got, *router)


def combine_body(n, weights, *refs):
    chunks, out = refs[:n], refs[-1]
    half = chunks[0].shape[1]
    total = dot(weights[0:CAP, :], chunks[0][...], 0, 0)
    for s in range(1, n):
        total += dot(weights[pl.ds(s * CAP, CAP), :], chunks[s][...], 0, 0)
    out[...] = total.astype(BF16)


def combine(n, weights, chunks):
    half = chunks[0].shape[1]
    return pl.pallas_call(
        functools.partial(combine_body, n),
        out_shape=jax.ShapeDtypeStruct((weights.shape[1], half), BF16),
        compiler_params=params(),
        cost_estimate=cost(2 * weights.size * half, 2 * n * CAP * half),
        name="combine",
    )(weights, *chunks)


def combine_router_body(n, half, first, second, *refs):
    chunks, out = refs[:n], refs[-1]
    rows = first.shape[1]
    total = jnp.zeros((rows, half), F32)
    score0 = jnp.zeros((rows, LANES), F32)
    score1 = jnp.zeros((rows, LANES), F32)
    for s in range(n):
        span = pl.ds(s * CAP, CAP)
        placed0, placed1 = first[span, :], second[span, :]
        total += dot(placed0 + placed1, chunks[s][:, 0:half], 0, 0)
        score0 += dot(placed0, chunks[s][:, half:], 0, 0)
        score1 += dot(placed1, chunks[s][:, half:], 0, 0)
    out[:, 0:half] = total.astype(BF16)
    out[:, half:] = spread_scores(
        jnp.sum(score0, axis=1, keepdims=True), jnp.sum(score1, axis=1, keepdims=True)
    )


def spread_scores(score0, score1):
    rows = score0.shape[0]
    lane = lax.broadcasted_iota(jnp.int32, (rows, LANES), 1)
    out = jnp.zeros((rows, LANES), F32)
    for k, score in enumerate((score0, score1)):
        for p, part in enumerate(three_parts(score)):
            out = jnp.where(lane == 3 * k + p, part.astype(F32), out)
    return out.astype(BF16)


def joined_scores(packed):
    values = packed.astype(F32)
    score0 = values[:, 0:1] + values[:, 1:2] + values[:, 2:3]
    score1 = values[:, 3:4] + values[:, 4:5] + values[:, 5:6]
    return score0, score1


def combine_router(n, first, second, chunks):
    wide = chunks[0].shape[1]
    rows = first.shape[1]
    return pl.pallas_call(
        functools.partial(combine_router_body, n, wide - LANES),
        out_shape=jax.ShapeDtypeStruct((rows, wide), BF16),
        compiler_params=params(),
        cost_estimate=cost(2 * first.size * wide, 2 * n * CAP * wide),
        name="combine_router",
    )(first, second, *chunks)


def finish_body(half, count, *refs):
    own, other, out = refs[:count], refs[count:2 * count], refs[2 * count]
    for pieces, start in ((own, own_half(half)), (other, other_half(half))):
        total = pieces[0][:, 0:half].astype(F32)
        for piece in pieces[1:]:
            total += piece[:, 0:half].astype(F32)
        out[:, pl.ds(start, half)] = total.astype(BF16)
    if len(refs) > 2 * count + 1:
        scores = [[joined_scores(piece[:, half:]) for piece in pieces] for pieces in (own, other)]
        sums = [[sum(part[k] for part in parts) for k in range(2)] for parts in scores]
        lane = lax.broadcasted_iota(jnp.int32, refs[-1].shape, 1)
        refs[-1][...] = jnp.where(
            lane == 0, sums[0][0] + sums[1][0], sums[0][1] + sums[1][1]
        )


def finish(half, own, other):
    rows, wide = own[0].shape
    out = [jax.ShapeDtypeStruct((rows, 2 * half), BF16)]
    if wide > half:
        out.append(jax.ShapeDtypeStruct((rows, 2), F32))
    return pl.pallas_call(
        functools.partial(finish_body, half, len(own)),
        out_shape=out,
        compiler_params=params(),
        cost_estimate=cost(0, 4 * rows * wide),
        name="finish",
    )(*own, *other)


def over_chips(half, value):
    count = lax.axis_size("dp")
    if count == 2:
        own = [value, shift(value, "dp", 1)]
    else:
        gathered = lax.all_gather(value, "dp", axis=0, tiled=False)
        own = [gathered[j] for j in range(count)]
    return finish(half, own, [shift(piece, "tp", 1) for piece in own])


def on_device(tokens, expert_ids, gates, out_grad, gate_weight, up_weight, down_weight):
    ids, gates, tokens, out_grad, gate_weight, up_weight, down_weight = (
        pltpu.with_memory_space_constraint(v, pltpu.HBM)
        for v in (expert_ids.T, gates.T, tokens, out_grad, gate_weight, up_weight, down_weight)
    )
    n = lax.axis_size("ed")
    slots = n * CAP
    half = tokens.shape[1] // 2
    hid = gate_weight.shape[1]

    toks, placing = pick_tokens(n, hid, ids, gates, tokens)
    tok_z = [shift(toks[s], "ed", s) for s in range(1, n)]
    gate_held, gate_done = load(toks[0], gate_weight)
    grads, coef_own = pick_grads(gate_done, n, placing, out_grad)
    grad_z = [shift(grads[s], "ed", s) for s in range(1, n)]
    up_held, up_done = load(grads[0], up_weight)
    tok_all = stack(up_done, tok_z)
    rows, hidden, act, slope = forward(
        n, toks[0], tok_all, shift(tok_all, "tp", 1), gate_held, up_held
    )
    out_part = expert_out(False, BF16, slots, hidden, down_weight)
    out_got = shift(out_part, "tp", 1)
    out_keep = expert_out(True, F32, slots, hidden, down_weight)
    out_chunks = merge(n, out_keep, out_got)
    out_back = [out_chunks[0]] + [shift(out_chunks[s], "ed", -s) for s in range(1, n)]
    grad_all = stack(hidden, grad_z)
    scaled, gate_pre, up_pre, router = back(
        out_chunks[0], n, grads[0], coef_own, grad_all, shift(grad_all, "tp", 1),
        hidden, act, slope, down_weight,
    )
    in_part = input_part(False, BF16, slots, gate_pre, up_pre, gate_held, up_held)
    in_got = shift(in_part, "tp", 1)
    in_keep = input_part(True, F32, slots, gate_pre, up_pre, gate_held, up_held)
    in_chunks = merge(n, in_keep, in_got, router)
    in_back = [in_chunks[0]] + [shift(in_chunks[s], "ed", -s) for s in range(1, n)]
    down_grad = weight_grad(hidden, scaled, "down_grad")
    gate_w_grad = weight_grad(rows, gate_pre, "gate_grad")
    up_w_grad = weight_grad(rows, up_pre, "up_grad")
    first, second, weighted = placing
    layer_out, = over_chips(half, combine(n, weighted, out_back))
    token_grad, gate_grad = over_chips(half, combine_router(n, first, second, in_back))
    return layer_out, token_grad, gate_grad, gate_w_grad, up_w_grad, down_grad


def solution(mesh):
    token_spec = P(("groups", "ed"), None)
    in_specs = (
        token_spec,
        token_spec,
        token_spec,
        token_spec,
        P(None, ("ed", "dp", "tp")),
        P(None, ("ed", "dp", "tp")),
        P(("ed", "dp", "tp"), None),
    )
    out_specs = (
        token_spec,
        token_spec,
        token_spec,
        P("groups", ("ed", "dp", "tp")),
        P("groups", ("ed", "dp", "tp")),
        P(("groups", "ed", "dp", "tp"), None),
    )
    return jax.shard_map(
        on_device, mesh=mesh, in_specs=in_specs, out_specs=out_specs, check_vma=False
    )
```

time: 299 us -> 104 us (0.35); the launches traced: 295 us -> 104 us
  waiting for transfers between devices: 122 us -> 6.18 us
  matrix products: 111 us -> 0 us
  Pallas kernels: 0 us -> 73.4 us
  between operations: 14.2 us -> 0.99 us
  local copies, waits for them, and re-layouts: 9.55 us -> 0.66 us
  other arithmetic: 7.48 us -> 0.01 us
  blocking collectives: 5.06 us -> 0 us
  starting transfers between devices: 25.6 us -> 22.6 us
    dot_general x17 -> x0, matrix products: 111 us -> none  [the longest x3 36.9 us: contract_last(): lax.dot_general(left_mat, right_mat, (((1,), (1,)), ((), ())), preferred_...]
    all_to_all x5 -> x0, waiting for transfers between devices: 73.5 us -> none  [the longest x1 27.7 us: on_device(): lax.all_to_all(out_slots, 'ed', split_axis=0, concat_axis=0, tiled=True)]
    pallas_call x0 -> x21, Pallas kernels: none -> 73.4 us  [the longest x3 19 us: weight_grad(): pl.pallas_call(weight_grad_body, out_shape=pltpu.HBM((rows, columns), BF1...]
    all_gather x2 -> x0, waiting for transfers between devices: 27.9 us -> none  [the longest x1 16.2 us: on_device(): lax.all_gather(layer_piece, ('dp', 'tp'), axis=1, tiled=True)]
    all_to_all x5 -> x0, starting transfers between devices: 24.9 us -> none  [the longest x1 6.32 us: on_device(): lax.all_to_all(jnp.take(send_scale, dest_expert, axis=0), 'ed', split_axi...]
    ppermute x0 -> x22, starting transfers between devices: none -> 22.6 us  [shift(): lax.ppermute(value, axis, [(j, (j + step) % count) for j in range(count)])]
    reduce_scatter x2 -> x0, waiting for transfers between devices: 13.1 us -> none  [the longest x1 13.1 us: on_device(): lax.psum_scatter(layer_full, ('dp', 'tp'), scatter_dimension=1, tiled=True)]
    unnamed x6 -> x0, waiting for transfers between devices: 7.7 us -> none
  transfers between devices with their start and end apart: 10 -> 22, of which waited for: 8 -> 2; matrix products, arithmetic and copies ran while one was open for 29% -> 0% of each run, Pallas kernels for 0% -> 51%
where the time goes in v2:
time: 104 us
  Pallas kernels  73.4 us (71%)
  starting transfers between devices  22.6 us (22%)
  waiting for transfers between devices  6.18 us (6%)
    ppermute x22, starting transfers between devices, shift(): lax.ppermute(value, axis, [(j, (j + step) % count) for j in range(count)])  22.6 us
    pallas_call x3, Pallas kernels, weight_grad(): pl.pallas_call(weight_grad_body, out_shape=pltpu.HBM((rows, columns), BF1...  19 us
    pallas_call x1, Pallas kernels, back(): pl.pallas_call(back_body, out_shape=[pltpu.VMEM((padded(slots), width), B...  12.8 us
    pallas_call x2, Pallas kernels, load(): pl.pallas_call(load_body, out_shape=[pltpu.VMEM(weight.shape, BF16), jax....  10.6 us
    pallas_call x2, Pallas kernels, input_part(): pl.pallas_call(functools.partial(input_body, mine), out_shape=jax.ShapeDt...  9.02 us
    pallas_call x2, Pallas kernels, expert_out(): pl.pallas_call(functools.partial(expert_out_body, mine, slots), out_shape...  8.88 us
    pallas_call x1, Pallas kernels, forward(): pl.pallas_call(functools.partial(forward_body, slots), out_shape=[pltpu.V...  6.38 us
    ppermute x22, waiting for transfers between devices, shift(): lax.ppermute(value, axis, [(j, (j + step) % count) for j in range(count)])  6.18 us
  transfers between devices with their start and end apart: 22, of which 2 were waited for; matrix products, arithmetic and copies ran while one was open for 0% of the time, Pallas kernels for 51%

profile of v2, /device:TPU:0, one launch (start us, length us, event | category | flops | bytes accessed | tf_op | source)
XLA Modules:
  0.0 103.8 jit_solution(12986768766548379470)
XLA Ops:
  0.6 1.9 %pick_tokens.1 = (bf16[48,2048]{1,0:T(8,128)(2,1)S(1)}, bf16[48,1024]{1,0:T(8,128)(2,1)S(1)}, bf16[48,1024]{1,0:T(8,128)(2,1)S(1)}, bf16[48,1024]{1,0:T(8,128)(2...) custom-call(s32[2,128]{1,0:T(2,128)} %bitcast.4, ...), custom_call_target="tpu_custom_call" | custom-call | flops 100663296 | bytes 1048576 | tf_op jit(solution)/shard_map/pick_tokens/pallas_call | solution.py:100
  2.6 3.1 %collective-permute-start = (bf16[48,1024]{1,0:T(8,128)(2,1)S(1)}, bf16[48,1024]{1,0:T(8,128)(2,1)S(1)}, u32[]{:S(2)}, u32[]{:S(2)}) collective-permute-start(bf16[48,1024]{1,0:T(8,128)(2,1)S(1)} %get-tuple-element.47), channel_id=1, source_target_pairs={{0,4},{4,8},{8,12},{12,0},{1,5},{5,9},{9,13},{13,1},{2,6},{6,10},{... | collective-permute-start | bytes 294920 | tf_op jit(solution)/shard_map/ppermute | solution.py:57
  5.6 2.6 %collective-permute-start.1 = (bf16[48,1024]{1,0:T(8,128)(2,1)S(1)}, bf16[48,1024]{1,0:T(8,128)(2,1)S(1)}, u32[]{:S(2)}, u32[]{:S(2)}) collective-permute-start(bf16[48,1024]{1,0:T(8,128)(2,1)S(1)} %get-tuple-element.48), channel_id=1, source_target_pairs={{0,8},{4,12},{8,0},{12,4},{1,9},{5,13},{9,1},{13,5},{2,10},{6,14},... | collective-permute-start | bytes 294920 | tf_op jit(solution)/shard_map/ppermute | solution.py:57
  8.2 1.3 %collective-permute-start.2 = (bf16[48,1024]{1,0:T(8,128)(2,1)S(1)}, bf16[48,1024]{1,0:T(8,128)(2,1)S(1)}, u32[]{:S(2)}, u32[]{:S(2)}) collective-permute-start(bf16[48,1024]{1,0:T(8,128)(2,1)S(1)} %get-tuple-element.49), channel_id=1, source_target_pairs={{0,12},{4,0},{8,4},{12,8},{1,13},{5,1},{9,5},{13,9},{2,14},{6,2},{... | collective-permute-start | bytes 294920 | tf_op jit(solution)/shard_map/ppermute | solution.py:57
  9.6 5.3 %load.2 = (bf16[2048,3584]{1,0:T(8,128)(2,1)S(1)}, f32[8,128]{1,0:T(8,128)S(1)}) custom-call(bf16[48,2048]{1,0:T(8,128)(2,1)S(1)} %get-tuple-element.41.after.own, bf16[2048,3584]{1,0:T(8,128)(2,1)} %weight.2), custom_call_target="tpu_custom_call" | custom-call | bytes 14680064 | tf_op jit(solution)/shard_map/load/pallas_call | solution.py:158
  14.9 1.4 %pick_grads.1 = (bf16[48,2048]{1,0:T(8,128)(2,1)S(1)}, bf16[48,1152]{1,0:T(8,128)(2,1)S(1)}, bf16[48,1152]{1,0:T(8,128)(2,1)S(1)}, bf16[48,1152]{1,0:T(8,128)(2,1)S(1)}, bf16[48,128]{1,0:T(8,128)(2,1)S(1)}) custom-call(f32[8,128]{1,0:T(8,128)S(1)} %get-tuple-element.42.after, bf16[192,128]{1,0:T(8,128)(2,1)S(1)} %get-tuple-element.43.first, ...), custom_call_target="tpu_custom_call" | custom-call | flops 100663296 | bytes 1048576 | tf_op jit(solution)/shard_map/pick_grads/pallas_call | solution.py:132
  16.2 5.3 %load.3 = (bf16[2048,3584]{1,0:T(8,128)(2,1)S(1)}, f32[8,128]{1,0:T(8,128)S(1)}) custom-call(bf16[48,2048]{1,0:T(8,128)(2,1)S(1)} %get-tuple-element.45.after.own, bf16[2048,3584]{1,0:T(8,128)(2,1)} %weight.3), custom_call_target="tpu_custom_call" | custom-call | bytes 14680064 | tf_op jit(solution)/shard_map/load/pallas_call | solution.py:158
  21.7 0.7 collective-permute-start.11
  22.7 2.8 %collective-permute-start.13 = (bf16[48,1152]{1,0:T(8,128)(2,1)S(1)}, bf16[48,1152]{1,0:T(8,128)(2,1)S(1)}, u32[]{:S(2)}, u32[]{:S(2)}) collective-permute-start(bf16[48,1152]{1,0:T(8,128)(2,1)S(1)} %get-tuple-element.60), channel_id=1, source_target_pairs={{0,12},{4,0},{8,4},{12,8},{1,13},{5,1},{9,5},{13,9},{2,14},{6,2},{... | collective-permute-start | bytes 331784 | tf_op jit(solution)/shard_map/ppermute | solution.py:57
  25.6 6.4 %forward.1 = (bf16[256,2048]{1,0:T(8,128)(2,1)S(1)}, bf16[256,3584]{1,0:T(8,128)(2,1)S(1)}, bf16[192,3584]{1,0:T(8,128)(2,1)S(1)}, bf16[192,3584]{1,0:T(8,128)(2,1)S(1)}) custom-call(bf16[48,2048]{1,0:T(8,128)(2,1)S(1)} %get-tuple-element.41.after.own, bf16[144,1024]{1,0:T(8,128)(2,1)S(1)} %stack.2.direct, ...), custom_call_target="tpu_custom_call" | custom-call | flops 5637144576 | bytes 786432 | tf_op jit(solution)/shard_map/forward/pallas_call | solution.py:221
  32.0 4.0 %out_send.1 = bf16[192,1024]{1,0:T(8,128)(2,1)S(1)} custom-call(bf16[256,3584]{1,0:T(8,128)(2,1)S(1)} %get-tuple-element.52.hidden.after.left, bf16[3584,2048]{1,0:T(8,128)(2,1)} %down.5), custom_call_target="tpu_custom_call" | custom-call | flops 1409286144 | bytes 7340032 | tf_op jit(solution)/shard_map/out_send/pallas_call | solution.py:272
  36.2 0.5 collective-permute-start.14
  36.7 4.8 %out_keep.1.keep = f32[192,1024]{1,0:T(8,128)S(1)} custom-call(bf16[256,3584]{1,0:T(8,128)(2,1)S(1)} %get-tuple-element.52.hidden.after.left, bf16[3584,2048]{1,0:T(8,128)(2,1)} %down.5), custom_call_target="tpu_custom_call" | custom-call | flops 1409286144 | bytes 7340032 | tf_op jit(solution)/shard_map/out_keep/pallas_call | solution.py:272
  41.7 12.8 %back.1 = (bf16[256,2048]{1,0:T(8,128)(2,1)S(1)}, bf16[256,3584]{1,0:T(8,128)(2,1)S(1)}, bf16[256,3584]{1,0:T(8,128)(2,1)S(1)}, f32[192,128]{1,0:T(8,128)S(1)}) custom-call(bf16[48,1024]{1,0:T(8,128)(2,1)S(1)} %get-tuple-element.53.refs_0_.after, bf16[48,2048]{1,0:T(8,128)(2,1)S(1)} %get-tuple-element.45.after.own, ...), custom_call_target="tpu_custom_call" | custom-call | flops 2818572288 | bytes 14680064 | tf_op jit(solution)/shard_map/back/pallas_call | solution.py:320
  54.6 4.5 %input_send.1 = bf16[192,1024]{1,0:T(8,128)(2,1)S(1)} custom-call(bf16[256,3584]{1,0:T(8,128)(2,1)S(1)} %get-tuple-element.63.gate_grad.right, bf16[256,3584]{1,0:T(8,128)(2,1)S(1)} %get-tuple-element.64.up_grad.right, bf16[2048,3584]{1,0:T(8,128)(2,1)S(1)} %get-tuple-element.50.gate_w, bf16[2048,3584]{1,0:T(8,128)(2,1)S(1)} %bitcast.3), custom_call_target="tpu_custom_call" | custom-call | flops 2818572288 | bytes 786432 | tf_op jit(solution)/shard_map/input_send/pallas_call | solution.py:355
  59.2 1.3 %collective-permute-start.5 = (bf16[48,1024]{1,0:T(8,128)(2,1)S(1)}, bf16[48,1024]{1,0:T(8,128)(2,1)S(1)}, u32[]{:S(2)}, u32[]{:S(2)}) collective-permute-start(bf16[48,1024]{1,0:T(8,128)(2,1)S(1)} %get-tuple-element.54), channel_id=1, source_target_pairs={{0,12},{4,0},{8,4},{12,8},{1,13},{5,1},{9,5},{13,9},{2,14},{6,2},{... | collective-permute-start | bytes 294920 | tf_op jit(solution)/shard_map/ppermute | solution.py:57
  60.5 4.5 %input_keep.1.keep = f32[192,1024]{1,0:T(8,128)S(1)} custom-call(bf16[256,3584]{1,0:T(8,128)(2,1)S(1)} %get-tuple-element.63.gate_grad.right, bf16[256,3584]{1,0:T(8,128)(2,1)S(1)} %get-tuple-element.64.up_grad.right, bf16[2048,3584]{1,0:T(8,128)(2,1)S(1)} %get-tuple-element.50.gate_w, bf16[2048,3584]{1,0:T(8,128)(2,1)S(1)} %bitcast.3), custom_call_target="tpu_custom_call" | custom-call | flops 2818572288 | bytes 786432 | tf_op jit(solution)/shard_map/input_keep/pallas_call | solution.py:355
  65.0 0.9 collective-permute-start.6
  65.9 2.0 %collective-permute-start.7 = (bf16[48,1024]{1,0:T(8,128)(2,1)S(1)}, bf16[48,1024]{1,0:T(8,128)(2,1)S(1)}, u32[]{:S(2)}, u32[]{:S(2)}) collective-permute-start(bf16[48,1024]{1,0:T(8,128)(2,1)S(1)} %get-tuple-element.56), channel_id=1, source_target_pairs={{0,4},{4,8},{8,12},{12,0},{1,5},{5,9},{9,13},{13,1},{2,6},{6,10},{... | collective-permute-start | bytes 294920 | tf_op jit(solution)/shard_map/ppermute | solution.py:57
  68.0 1.9 %collective-permute-start.16 = (bf16[48,1152]{1,0:T(8,128)(2,1)S(1)}, bf16[48,1152]{1,0:T(8,128)(2,1)S(1)}, u32[]{:S(2)}, u32[]{:S(2)}) collective-permute-start(bf16[48,1152]{1,0:T(8,128)(2,1)S(1)} %get-tuple-element.67), channel_id=1, source_target_pairs={{0,12},{4,0},{8,4},{12,8},{1,13},{5,1},{9,5},{13,9},{2,14},{6,2},{... | collective-permute-start | bytes 331784 | tf_op jit(solution)/shard_map/ppermute | solution.py:57
  70.2 0.8 collective-permute-start.18
  71.0 6.0 %up_grad.1 = bf16[2048,3584]{1,0:T(8,128)(2,1)} custom-call(bf16[256,2048]{1,0:T(8,128)(2,1)S(1)} %get-tuple-element.72.left, bf16[256,3584]{1,0:T(8,128)(2,1)S(1)} %get-tuple-element.64.up_grad.right), custom_call_target="tpu_custom_call" | custom-call | flops 3758096384 | bytes 14680064 | tf_op jit(solution)/shard_map/up_grad/pallas_call | solution.py:393
  77.4 1.6 %collective-permute-start.8 = (bf16[128,1024]{1,0:T(8,128)(2,1)S(1)}, bf16[128,1024]{1,0:T(8,128)(2,1)S(1)}, u32[]{:S(2)}, u32[]{:S(2)}) collective-permute-start(bf16[128,1024]{1,0:T(8,128)(2,1)S(1)} %combine.1.refs_0_), channel_id=1, source_target_pairs={{0,2},{2,0},{1,3},{3,1},{4,6},{6,4},{5,7},{7,5},{8,10},{10,8},{9,1... | collective-permute-start | bytes 786440 | tf_op jit(solution)/shard_map/ppermute | solution.py:57
  79.0 5.5 %collective-permute-done.17.refs_2_ = bf16[48,1152]{1,0:T(8,128)(2,1)S(1)} collective-permute-done((bf16[48,1152]{1,0:T(8,128)(2,1)S(1)}, bf16[48,1152]{1,0:T(8,128)(2,1)S(1)}, u32[]{:S(2)}, u32[]{:S(2)}) %collective-permute-start.17) | collective-permute-done | bytes 110624 | tf_op jit(solution)/shard_map/ppermute | solution.py:57
  84.5 0.6 combine_router.1.refs_0_
  85.2 1.6 %collective-permute-start.19 = (bf16[128,1152]{1,0:T(8,128)(2,1)S(1)}, bf16[128,1152]{1,0:T(8,128)(2,1)S(1)}, u32[]{:S(2)}, u32[]{:S(2)}) collective-permute-start(bf16[128,1152]{1,0:T(8,128)(2,1)S(1)} %combine_router.1.refs_0_), channel_id=1, source_target_pairs={{0,2},{2,0},{1,3},{3,1},{4,6},{6,4},{5,7},{7,5},{8,10},{10,8},{9,1... | collective-permute-start | bytes 884744 | tf_op jit(solution)/shard_map/ppermute | solution.py:57
  86.7 6.0 %gate_grad.1 = bf16[2048,3584]{1,0:T(8,128)(2,1)} custom-call(bf16[256,2048]{1,0:T(8,128)(2,1)S(1)} %get-tuple-element.72.left, bf16[256,3584]{1,0:T(8,128)(2,1)S(1)} %get-tuple-element.63.gate_grad.right), custom_call_target="tpu_custom_call" | custom-call | flops 3758096384 | bytes 14680064 | tf_op jit(solution)/shard_map/gate_grad/pallas_call | solution.py:393
  93.4 0.6 collective-permute-done.19.refs_1_
  94.0 7.1 %down_grad.1 = bf16[3584,2048]{1,0:T(8,128)(2,1)} custom-call(bf16[256,3584]{1,0:T(8,128)(2,1)S(1)} %get-tuple-element.52.hidden.after.left, bf16[256,2048]{1,0:T(8,128)(2,1)S(1)} %get-tuple-element.73.right), custom_call_target="tpu_custom_call" | custom-call | flops 3758096384 | bytes 14680064 | tf_op jit(solution)/shard_map/down_grad/pallas_call | solution.py:393
  101.1 0.9 finish.2
  102.0 1.1 %finish.3 = (bf16[128,2048]{1,0:T(8,128)(2,1)}, f32[128,2]{1,0:T(8,128)S(1)}) custom-call(bf16[128,1152]{1,0:T(8,128)(2,1)S(1)} %combine_router.1.refs_0_, bf16[128,1152]{1,0:T(8,128)(2,1)S(1)} %collective-permute-done.19.refs_1_, bf16[128,1152]{1,0:T(8,128)(2,1)S(1)} %collective-permute-done.20.refs_2_, bf16[128,1152]{1,0:T(8,128)(2,1)S(1)} %collective-permute-done.21.refs_3_), custom_call_target="tpu_custom_call" | custom-call | bytes 589824 | tf_op jit(solution)/shard_map/finish/pallas_call | solution.py:528
  103.2 0.6 copy.13
  (45 shorter events, 2.3 us)
Async XLA Ops:
  2.6 19.0 %collective-permute-start = (bf16[48,1024]{1,0:T(8,128)(2,1)S(1)}, bf16[48,1024]{1,0:T(8,128)(2,1)S(1)}, u32[]{:S(2)}, u32[]{:S(2)}) collective-permute-start(bf16[48,1024]{1,0:T(8,128)(2,1)S(1)} %get-tuple-element.47), channel_id=1, source_target_pairs={{0,4},{4,8},{8,12},{12,0},{1,5},{5,9},{9,13},{13,1},{2,6},{6,10},{... | collective-permute-start | bytes 294920 | tf_op jit(solution)/shard_map/ppermute | solution.py:57
  5.6 15.9 %collective-permute-start.1 = (bf16[48,1024]{1,0:T(8,128)(2,1)S(1)}, bf16[48,1024]{1,0:T(8,128)(2,1)S(1)}, u32[]{:S(2)}, u32[]{:S(2)}) collective-permute-start(bf16[48,1024]{1,0:T(8,128)(2,1)S(1)} %get-tuple-element.48), channel_id=1, source_target_pairs={{0,8},{4,12},{8,0},{12,4},{1,9},{5,13},{9,1},{13,5},{2,10},{6,14},... | collective-permute-start | bytes 294920 | tf_op jit(solution)/shard_map/ppermute | solution.py:57
  8.2 13.3 %collective-permute-start.2 = (bf16[48,1024]{1,0:T(8,128)(2,1)S(1)}, bf16[48,1024]{1,0:T(8,128)(2,1)S(1)}, u32[]{:S(2)}, u32[]{:S(2)}) collective-permute-start(bf16[48,1024]{1,0:T(8,128)(2,1)S(1)} %get-tuple-element.49), channel_id=1, source_target_pairs={{0,12},{4,0},{8,4},{12,8},{1,13},{5,1},{9,5},{13,9},{2,14},{6,2},{... | collective-permute-start | bytes 294920 | tf_op jit(solution)/shard_map/ppermute | solution.py:57
  21.5 10.4 %copy-start = (bf16[2048,3584]{1,0:T(8,128)(2,1)}, bf16[2048,3584]{1,0:T(8,128)(2,1)S(1)}, u32[]{:S(2)}) copy-start(bf16[2048,3584]{1,0:T(8,128)(2,1)S(1)} %get-tuple-element.51.up_w) | copy-start | bytes 44040196
  21.6 4.0 %collective-permute-start.3 = (bf16[144,1024]{1,0:T(8,128)(2,1)S(1)}, bf16[144,1024]{1,0:T(8,128)(2,1)S(1)}, u32[]{:S(2)}, u32[]{:S(2)}) collective-permute-start(bf16[144,1024]{1,0:T(8,128)(2,1)S(1)} %stack.2.direct), channel_id=1, source_target_pairs={{0,1},{1,0},{2,3},{3,2},{4,5},{5,4},{6,7},{7,6},{8,9},{9,8},{10,11... | collective-permute-start | bytes 884744 | tf_op jit(solution)/shard_map/ppermute | solution.py:57
  21.7 14.4 %collective-permute-start.11 = (bf16[48,1152]{1,0:T(8,128)(2,1)S(1)}, bf16[48,1152]{1,0:T(8,128)(2,1)S(1)}, u32[]{:S(2)}, u32[]{:S(2)}) collective-permute-start(bf16[48,1152]{1,0:T(8,128)(2,1)S(1)} %get-tuple-element.58), channel_id=1, source_target_pairs={{0,4},{4,8},{8,12},{12,0},{1,5},{5,9},{9,13},{13,1},{2,6},{6,10},{... | collective-permute-start | bytes 331784 | tf_op jit(solution)/shard_map/ppermute | solution.py:57
  22.4 13.7 %collective-permute-start.12 = (bf16[48,1152]{1,0:T(8,128)(2,1)S(1)}, bf16[48,1152]{1,0:T(8,128)(2,1)S(1)}, u32[]{:S(2)}, u32[]{:S(2)}) collective-permute-start(bf16[48,1152]{1,0:T(8,128)(2,1)S(1)} %get-tuple-element.59), channel_id=1, source_target_pairs={{0,8},{4,12},{8,0},{12,4},{1,9},{5,13},{9,1},{13,5},{2,10},{6,14},... | collective-permute-start | bytes 331784 | tf_op jit(solution)/shard_map/ppermute | solution.py:57
  22.7 13.4 %collective-permute-start.13 = (bf16[48,1152]{1,0:T(8,128)(2,1)S(1)}, bf16[48,1152]{1,0:T(8,128)(2,1)S(1)}, u32[]{:S(2)}, u32[]{:S(2)}) collective-permute-start(bf16[48,1152]{1,0:T(8,128)(2,1)S(1)} %get-tuple-element.60), channel_id=1, source_target_pairs={{0,12},{4,0},{8,4},{12,8},{1,13},{5,1},{9,5},{13,9},{2,14},{6,2},{... | collective-permute-start | bytes 331784 | tf_op jit(solution)/shard_map/ppermute | solution.py:57
  36.0 5.5 %collective-permute-start.4 = (bf16[192,1024]{1,0:T(8,128)(2,1)S(1)}, bf16[192,1024]{1,0:T(8,128)(2,1)S(1)}, u32[]{:S(2)}, u32[]{:S(2)}) collective-permute-start(bf16[192,1024]{1,0:T(8,128)(2,1)S(1)} %out_send.1), channel_id=1, source_target_pairs={{0,1},{1,0},{2,3},{3,2},{4,5},{5,4},{6,7},{7,6},{8,9},{9,8},{10,11... | collective-permute-start | bytes 1179656 | tf_op jit(solution)/shard_map/ppermute | solution.py:57
  36.2 5.5 %collective-permute-start.14 = (bf16[144,1152]{1,0:T(8,128)(2,1)S(1)}, bf16[144,1152]{1,0:T(8,128)(2,1)S(1)}, u32[]{:S(2)}, u32[]{:S(2)}) collective-permute-start(bf16[144,1152]{1,0:T(8,128)(2,1)S(1)} %stack.3.direct), channel_id=1, source_target_pairs={{0,1},{1,0},{2,3},{3,2},{4,5},{5,4},{6,7},{7,6},{8,9},{9,8},{10,11... | collective-permute-start | bytes 995336 | tf_op jit(solution)/shard_map/ppermute | solution.py:57
  36.7 17.8 %slice-start = ((s8[14680064]{0:T(1024)(128)(4,1)}), s8[4194304]{0:T(1024)(128)(4,1)S(1)}, s32[]{:S(2)}) async-start(s8[14680064]{0:T(1024)(128)(4,1)} %bitcast.2), calls=%async_computation | async-start | bytes 8388608
  36.7 17.8 %slice-start.1 = ((s8[14680064]{0:T(1024)(128)(4,1)}), s8[4194304]{0:T(1024)(128)(4,1)S(1)}, s32[]{:S(2)}) async-start(s8[14680064]{0:T(1024)(128)(4,1)} %bitcast.2), calls=%async_computation.1 | async-start | bytes 8388608
  41.6 12.9 %slice-start.2 = ((s8[14680064]{0:T(1024)(128)(4,1)}), s8[4194304]{0:T(1024)(128)(4,1)S(1)}, s32[]{:S(2)}) async-start(s8[14680064]{0:T(1024)(128)(4,1)} %bitcast.2), calls=%async_computation.2 | async-start | bytes 8388608
  41.7 12.9 %slice-start.3 = ((s8[14680064]{0:T(1024)(128)(4,1)}), s8[2097152]{0:T(1024)(128)(4,1)S(1)}, s32[]{:S(2)}) async-start(s8[14680064]{0:T(1024)(128)(4,1)} %bitcast.2), calls=%async_computation.3 | async-start | bytes 4194304
  59.1 8.8 %collective-permute-start.15 = (bf16[192,1024]{1,0:T(8,128)(2,1)S(1)}, bf16[192,1024]{1,0:T(8,128)(2,1)S(1)}, u32[]{:S(2)}, u32[]{:S(2)}) collective-permute-start(bf16[192,1024]{1,0:T(8,128)(2,1)S(1)} %input_send.1), channel_id=1, source_target_pairs={{0,1},{1,0},{2,3},{3,2},{4,5},{5,4},{6,7},{7,6},{8,9},{9,8},{10,11... | collective-permute-start | bytes 1179656 | tf_op jit(solution)/shard_map/ppermute | solution.py:57
  59.2 11.0 %collective-permute-start.5 = (bf16[48,1024]{1,0:T(8,128)(2,1)S(1)}, bf16[48,1024]{1,0:T(8,128)(2,1)S(1)}, u32[]{:S(2)}, u32[]{:S(2)}) collective-permute-start(bf16[48,1024]{1,0:T(8,128)(2,1)S(1)} %get-tuple-element.54), channel_id=1, source_target_pairs={{0,12},{4,0},{8,4},{12,8},{1,13},{5,1},{9,5},{13,9},{2,14},{6,2},{... | collective-permute-start | bytes 294920 | tf_op jit(solution)/shard_map/ppermute | solution.py:57
  65.0 12.0 %collective-permute-start.6 = (bf16[48,1024]{1,0:T(8,128)(2,1)S(1)}, bf16[48,1024]{1,0:T(8,128)(2,1)S(1)}, u32[]{:S(2)}, u32[]{:S(2)}) collective-permute-start(bf16[48,1024]{1,0:T(8,128)(2,1)S(1)} %get-tuple-element.55), channel_id=1, source_target_pairs={{0,8},{4,12},{8,0},{12,4},{1,9},{5,13},{9,1},{13,5},{2,10},{6,14},... | collective-permute-start | bytes 294920 | tf_op jit(solution)/shard_map/ppermute | solution.py:57
  65.9 11.1 %collective-permute-start.7 = (bf16[48,1024]{1,0:T(8,128)(2,1)S(1)}, bf16[48,1024]{1,0:T(8,128)(2,1)S(1)}, u32[]{:S(2)}, u32[]{:S(2)}) collective-permute-start(bf16[48,1024]{1,0:T(8,128)(2,1)S(1)} %get-tuple-element.56), channel_id=1, source_target_pairs={{0,4},{4,8},{8,12},{12,0},{1,5},{5,9},{9,13},{13,1},{2,6},{6,10},{... | collective-permute-start | bytes 294920 | tf_op jit(solution)/shard_map/ppermute | solution.py:57
  68.0 11.0 %collective-permute-start.16 = (bf16[48,1152]{1,0:T(8,128)(2,1)S(1)}, bf16[48,1152]{1,0:T(8,128)(2,1)S(1)}, u32[]{:S(2)}, u32[]{:S(2)}) collective-permute-start(bf16[48,1152]{1,0:T(8,128)(2,1)S(1)} %get-tuple-element.67), channel_id=1, source_target_pairs={{0,12},{4,0},{8,4},{12,8},{1,13},{5,1},{9,5},{13,9},{2,14},{6,2},{... | collective-permute-start | bytes 331784 | tf_op jit(solution)/shard_map/ppermute | solution.py:57
  69.9 14.6 %collective-permute-start.17 = (bf16[48,1152]{1,0:T(8,128)(2,1)S(1)}, bf16[48,1152]{1,0:T(8,128)(2,1)S(1)}, u32[]{:S(2)}, u32[]{:S(2)}) collective-permute-start(bf16[48,1152]{1,0:T(8,128)(2,1)S(1)} %get-tuple-element.68), channel_id=1, source_target_pairs={{0,8},{4,12},{8,0},{12,4},{1,9},{5,13},{9,1},{13,5},{2,10},{6,14},... | collective-permute-start | bytes 331784 | tf_op jit(solution)/shard_map/ppermute | solution.py:57
  70.2 14.3 %collective-permute-start.18 = (bf16[48,1152]{1,0:T(8,128)(2,1)S(1)}, bf16[48,1152]{1,0:T(8,128)(2,1)S(1)}, u32[]{:S(2)}, u32[]{:S(2)}) collective-permute-start(bf16[48,1152]{1,0:T(8,128)(2,1)S(1)} %get-tuple-element.69), channel_id=1, source_target_pairs={{0,4},{4,8},{8,12},{12,0},{1,5},{5,9},{9,13},{13,1},{2,6},{6,10},{... | collective-permute-start | bytes 331784 | tf_op jit(solution)/shard_map/ppermute | solution.py:57
  77.4 15.4 %collective-permute-start.8 = (bf16[128,1024]{1,0:T(8,128)(2,1)S(1)}, bf16[128,1024]{1,0:T(8,128)(2,1)S(1)}, u32[]{:S(2)}, u32[]{:S(2)}) collective-permute-start(bf16[128,1024]{1,0:T(8,128)(2,1)S(1)} %combine.1.refs_0_), channel_id=1, source_target_pairs={{0,2},{2,0},{1,3},{3,1},{4,6},{6,4},{5,7},{7,5},{8,10},{10,8},{9,1... | collective-permute-start | bytes 786440 | tf_op jit(solution)/shard_map/ppermute | solution.py:57
  85.2 8.8 %collective-permute-start.19 = (bf16[128,1152]{1,0:T(8,128)(2,1)S(1)}, bf16[128,1152]{1,0:T(8,128)(2,1)S(1)}, u32[]{:S(2)}, u32[]{:S(2)}) collective-permute-start(bf16[128,1152]{1,0:T(8,128)(2,1)S(1)} %combine_router.1.refs_0_), channel_id=1, source_target_pairs={{0,2},{2,0},{1,3},{3,1},{4,6},{6,4},{5,7},{7,5},{8,10},{10,8},{9,1... | collective-permute-start | bytes 884744 | tf_op jit(solution)/shard_map/ppermute | solution.py:57
  92.7 8.4 %collective-permute-start.9 = (bf16[128,1024]{1,0:T(8,128)(2,1)S(1)}, bf16[128,1024]{1,0:T(8,128)(2,1)S(1)}, u32[]{:S(2)}, u32[]{:S(2)}) collective-permute-start(bf16[128,1024]{1,0:T(8,128)(2,1)S(1)} %combine.1.refs_0_), channel_id=1, source_target_pairs={{0,1},{1,0},{2,3},{3,2},{4,5},{5,4},{6,7},{7,6},{8,9},{9,8},{10,11... | collective-permute-start | bytes 786440 | tf_op jit(solution)/shard_map/ppermute | solution.py:57
  92.8 8.3 %collective-permute-start.10 = (bf16[128,1024]{1,0:T(8,128)(2,1)S(1)}, bf16[128,1024]{1,0:T(8,128)(2,1)S(1)}, u32[]{:S(2)}, u32[]{:S(2)}) collective-permute-start(bf16[128,1024]{1,0:T(8,128)(2,1)S(1)} %collective-permute-done.8.refs_1_), channel_id=1, source_target_pairs={{0,1},{1,0},{2,3},{3,2},{4,5},{5,4},{6,7},{7,6},{8,9},{9,8},{10,11... | collective-permute-start | bytes 786440 | tf_op jit(solution)/shard_map/ppermute | solution.py:57
  93.3 8.7 %collective-permute-start.20 = (bf16[128,1152]{1,0:T(8,128)(2,1)S(1)}, bf16[128,1152]{1,0:T(8,128)(2,1)S(1)}, u32[]{:S(2)}, u32[]{:S(2)}) collective-permute-start(bf16[128,1152]{1,0:T(8,128)(2,1)S(1)} %combine_router.1.refs_0_), channel_id=1, source_target_pairs={{0,1},{1,0},{2,3},{3,2},{4,5},{5,4},{6,7},{7,6},{8,9},{9,8},{10,11... | collective-permute-start | bytes 884744 | tf_op jit(solution)/shard_map/ppermute | solution.py:57
  93.9 8.1 %collective-permute-start.21 = (bf16[128,1152]{1,0:T(8,128)(2,1)S(1)}, bf16[128,1152]{1,0:T(8,128)(2,1)S(1)}, u32[]{:S(2)}, u32[]{:S(2)}) collective-permute-start(bf16[128,1152]{1,0:T(8,128)(2,1)S(1)} %collective-permute-done.19.refs_1_), channel_id=1, source_target_pairs={{0,1},{1,0},{2,3},{3,2},{4,5},{5,4},{6,7},{7,6},{8,9},{9,8},{10,11... | collective-permute-start | bytes 884744 | tf_op jit(solution)/shard_map/ppermute | solution.py:57

commit v3 on v2

v3 whole, which is shorter than its diff:
```python
import functools

import jax
import jax.numpy as jnp
from jax import lax
from jax.experimental import pallas as pl
from jax.experimental.pallas import tpu as pltpu
from jax.sharding import PartitionSpec as P

FF = 7168
CAP = 48
LANES = 128
F32 = jnp.float32
BF16 = jnp.bfloat16


def dot(left, right, left_dim=1, right_dim=0):
    return lax.dot_general(
        left, right, (((left_dim,), (right_dim,)), ((), ())), preferred_element_type=F32
    )


def params(megabytes=6, slots=0):
    scale = 1 if slots <= 256 else 4
    return pltpu.CompilerParams(vmem_limit_bytes=megabytes * scale * 1024 * 1024)


def tile_of(size, most):
    for tile in (1024, 512, 256):
        if tile <= most and size % tile == 0:
            return tile
    return size


def padded(slots):
    return -(-slots // 256) * 256


IN_VMEM = pl.BlockSpec(memory_space=pltpu.VMEM)
ANYWHERE = pl.BlockSpec(memory_space=pl.ANY)


def own_half(half):
    return pl.multiple_of(lax.axis_index("tp") * half, half)


def other_half(half):
    return pl.multiple_of((1 - lax.axis_index("tp")) * half, half)


def cost(flops, nbytes):
    return pl.CostEstimate(flops=int(flops), bytes_accessed=int(nbytes), transcendentals=0)


def shift(value, axis, step):
    count = lax.axis_size(axis)
    return lax.ppermute(value, axis, [(j, (j + step) % count) for j in range(count)])


def pick_body(n, hid, reps, ids, gates, tokens, grads, *outs):
    own_tok, own_grad, own_coef = outs[0:3]
    first, second, weighted = outs[n + 2:]
    rows, width = tokens.shape
    half = width // 2
    upper = (
        lax.broadcasted_iota(jnp.int32, (rows, rows), 0)
        <= lax.broadcasted_iota(jnp.int32, (rows, rows), 1)
    ).astype(BF16)
    me, rep = lax.axis_index("ed"), lax.axis_index("dp") * 2 + lax.axis_index("tp")
    slot_index = lax.broadcasted_iota(jnp.int32, (CAP, rows), 0).astype(F32)
    gate0, gate1 = gates[0:1, :].astype(F32), gates[1:2, :].astype(F32)
    ids0, ids1 = ids[0:1, :], ids[1:2, :]
    for s in range(n):
        owner = lax.rem(me + s, n)
        expert = ((owner * reps + rep) * hid) // FF
        hit0 = jnp.where(ids0 == expert, 1.0, 0.0)
        hit1 = jnp.where(ids1 == expert, 1.0, 0.0)
        chosen = jnp.broadcast_to(hit0 + hit1, (8, rows)).astype(BF16)
        place = dot(chosen, upper)[0:1] - 1.0
        here = jnp.where(place == slot_index, 1.0, 0.0)
        placed0, placed1 = here * hit0, here * hit1
        placed = (placed0 + placed1).astype(BF16)
        weight = placed0 * gate0 + placed1 * gate1
        span = pl.ds(s * CAP, CAP)
        first[span, :] = placed0.astype(BF16)
        second[span, :] = placed1.astype(BF16)
        weighted[span, :] = weight.astype(BF16)
        coef = jnp.broadcast_to(jnp.sum(weight, axis=1, keepdims=True), (CAP, LANES)).astype(BF16)
        if s == 0:
            own_tok[...] = dot(placed, tokens[...]).astype(BF16)
            own_grad[...] = dot(placed, grads[...]).astype(BF16)
            own_coef[...] = coef
        else:
            mine = pl.ds(own_half(half), half)
            out = outs[2 + s]
            out[:, 0:half] = dot(placed, tokens[:, mine]).astype(BF16)
            out[:, half:width] = dot(placed, grads[:, mine]).astype(BF16)
            out[:, width:] = coef


def pick(n, hid, ids, gates, tokens, grads):
    rows, width = tokens.shape
    slots = n * CAP
    out = (
        [jax.ShapeDtypeStruct((CAP, width), BF16)] * 2
        + [jax.ShapeDtypeStruct((CAP, LANES), BF16)]
        + [jax.ShapeDtypeStruct((CAP, width + LANES), BF16)] * (n - 1)
        + [jax.ShapeDtypeStruct((slots, rows), BF16)] * 3
    )
    got = pl.pallas_call(
        functools.partial(pick_body, n, hid, lax.axis_size(("dp", "tp"))),
        out_shape=out,
        compiler_params=params(),
        cost_estimate=cost(4 * slots * rows * width, 8 * rows * width),
        name="pick",
    )(ids, gates, tokens, grads)
    return got[0:3], got[3:n + 2], got[n + 2:]


def load_body(after, weight, held, done, sems):
    rows = weight.shape[0] // sems.shape[0]
    copies = [
        pltpu.make_async_copy(weight.at[pl.ds(j * rows, rows)], held.at[pl.ds(j * rows, rows)], sems.at[j])
        for j in range(sems.shape[0])
    ]
    for copy in copies:
        copy.start()
    done[...] = jnp.zeros_like(done)
    for copy in copies:
        copy.wait()


def load(after, weight):
    return pl.pallas_call(
        load_body,
        out_shape=[pltpu.VMEM(weight.shape, BF16), jax.ShapeDtypeStruct((8, LANES), F32)],
        in_specs=[ANYWHERE] * 2,
        out_specs=[IN_VMEM] * 2,
        scratch_shapes=[pltpu.SemaphoreType.DMA((4,))],
        compiler_params=params(19),
        cost_estimate=cost(0, 2 * LANES),
        name="load",
    )(after, weight)


def stack_body(after, *refs):
    pieces, out = refs[:-1], refs[-1]
    for s, piece in enumerate(pieces):
        out[s * CAP:(s + 1) * CAP, :] = piece[...]


def stack(after, pieces):
    wide = pieces[0].shape[1]
    return pl.pallas_call(
        stack_body,
        out_shape=jax.ShapeDtypeStruct((len(pieces) * CAP, wide), BF16),
        in_specs=[ANYWHERE] + [IN_VMEM] * len(pieces),
        out_specs=IN_VMEM,
        compiler_params=params(),
        cost_estimate=cost(0, 4 * len(pieces) * CAP * wide),
        name="stack",
    )(after, *pieces)


def gather_rows(half, at, own, direct, other, held):
    held[0:CAP, :] = own[...]
    held[CAP:held.shape[0], pl.ds(own_half(half), half)] = direct[:, at:at + half]
    held[CAP:held.shape[0], pl.ds(other_half(half), half)] = other[:, at:at + half]


def clear_padding(slots, ref):
    if ref.shape[0] > slots:
        ref[slots:, :] = jnp.zeros((ref.shape[0] - slots, ref.shape[1]), ref.dtype)


def forward_body(slots, own, direct, other, gate_w, up_w, rows_out, hidden, act, slope):
    width, hid = gate_w.shape
    gather_rows(width // 2, 0, own, direct, other, rows_out.at[pl.ds(0, slots)])
    clear_padding(slots, rows_out)
    clear_padding(slots, hidden)
    rows = rows_out[0:slots, :]
    tile = tile_of(hid, 512)
    for at in range(0, hid, tile):
        span = slice(at, at + tile)
        pre_gate = dot(rows, gate_w[:, span])
        pre_up = dot(rows, up_w[:, span])
        logistic = jax.nn.sigmoid(pre_gate)
        silu = pre_gate * logistic
        hidden[0:slots, span] = (silu * pre_up).astype(BF16)
        act[:, span] = silu.astype(BF16)
        slope[:, span] = (pre_up * logistic * (1.0 + pre_gate * (1.0 - logistic))).astype(BF16)


def forward(n, own, direct, other, gate_w, up_w):
    width, hid = gate_w.shape
    slots = n * CAP
    return pl.pallas_call(
        functools.partial(forward_body, slots),
        out_shape=[
            pltpu.VMEM((padded(slots), width), BF16),
            pltpu.VMEM((padded(slots), hid), BF16),
            pltpu.VMEM((slots, hid), BF16),
            pltpu.VMEM((slots, hid), BF16),
        ],
        in_specs=[IN_VMEM] * 5,
        out_specs=[IN_VMEM] * 4,
        compiler_params=params(6, slots),
        cost_estimate=cost(0, 2 * slots * width),
        name="forward",
    )(own, direct, other, gate_w, up_w)


def streamed(down, buffers, sems, tile, columns):
    def copy(step):
        return pltpu.make_async_copy(
            down.at[pl.ds(step * tile, tile), columns],
            buffers.at[step % buffers.shape[0]],
            sems.at[step % buffers.shape[0]],
        )

    return copy


def middle_body(own, coef_own, direct, other, hidden, act, slope, down, scaled, gate_grad,
                up_grad, router, send, keep, held, total, coef, buffers, sems):
    hid, width = down.shape
    half = width // 2
    slots = held.shape[0]
    depth, tile = buffers.shape[0:2]
    steps = hid // tile
    copy = streamed(down, buffers, sems, tile, slice(None))
    for step in range(min(depth, steps)):
        copy(step).start()
    gather_rows(half, half, own, direct, other, held)
    coef[0:CAP, :] = coef_own[...].astype(F32)
    coef[CAP:, :] = direct[:, width:].astype(F32)
    scale = coef[:, 0:1]
    for ref in (scaled, gate_grad, up_grad):
        clear_padding(slots, ref)
    scaled[0:slots, :] = (scale * held[...].astype(F32)).astype(BF16)
    score = jnp.zeros((slots, LANES), F32)
    for step in range(steps):
        span = slice(step * tile, (step + 1) * tile)
        copy(step).wait()
        weight = buffers[step % depth]
        rows = hidden[0:slots, span]
        back = dot(held[...], weight, 1, 1)
        for at in range(0, width, half):
            part = dot(rows, buffers[step % depth, :, at:at + half])
            if step:
                total[:, at:at + half] += part
            else:
                total[:, at:at + half] = part
        if step + depth < steps:
            copy(step + depth).start()
        product = rows.astype(F32) * back
        for lane in range(0, tile // LANES * LANES, LANES):
            score += product[:, lane:lane + LANES]
        if tile % LANES:
            rest = jnp.sum(product[:, tile // LANES * LANES:], axis=1, keepdims=True)
            score += jnp.where(lax.broadcasted_iota(jnp.int32, score.shape, 1) == 0, rest, 0.0)
        grad = scale * back
        gate_grad[0:slots, span] = (grad * slope[:, span].astype(F32)).astype(BF16)
        up_grad[0:slots, span] = (grad * act[:, span].astype(F32)).astype(BF16)
    send[...] = total[:, pl.ds(other_half(half), half)].astype(BF16)
    keep[...] = total[:, pl.ds(own_half(half), half)]
    router[...] = jnp.broadcast_to(jnp.sum(score, axis=1, keepdims=True), router.shape)


def middle(n, own, coef_own, direct, other, hidden, act, slope, down):
    hid, width = down.shape
    half = width // 2
    slots = n * CAP
    tile = tile_of(hid, 256)
    return pl.pallas_call(
        middle_body,
        out_shape=[
            pltpu.VMEM((padded(slots), width), BF16),
            pltpu.VMEM((padded(slots), hid), BF16),
            pltpu.VMEM((padded(slots), hid), BF16),
            jax.ShapeDtypeStruct((slots, LANES), F32),
            jax.ShapeDtypeStruct((slots, half), BF16),
            jax.ShapeDtypeStruct((slots, half), F32),
        ],
        in_specs=[IN_VMEM] * 7 + [ANYWHERE],
        out_specs=[IN_VMEM] * 6,
        scratch_shapes=[
            pltpu.VMEM((slots, width), BF16),
            pltpu.VMEM((slots, width), F32),
            pltpu.VMEM((slots, LANES), F32),
            pltpu.VMEM((2, tile, width), BF16),
            pltpu.SemaphoreType.DMA((2,)),
        ],
        compiler_params=params(7, slots),
        cost_estimate=cost(4 * slots * width * hid, 2 * width * hid),
        name="middle",
    )(own, coef_own, direct, other, hidden, act, slope, down)


def input_body(mine, gate_grad, up_grad, gate_w, up_w, out):
    slots, half = out.shape
    start = own_half(half) if mine else other_half(half)
    tile = tile_of(half, 256)
    for at in range(0, half, tile):
        span = pl.ds(start + at, tile)
        value = dot(gate_grad[0:slots, :], gate_w[span, :], 1, 1)
        value += dot(up_grad[0:slots, :], up_w[span, :], 1, 1)
        out[:, at:at + tile] = value.astype(out.dtype)


def input_part(mine, kind, slots, gate_grad, up_grad, gate_w, up_w):
    width, hid = gate_w.shape
    return pl.pallas_call(
        functools.partial(input_body, mine),
        out_shape=jax.ShapeDtypeStruct((slots, width // 2), kind),
        in_specs=[IN_VMEM] * 4,
        out_specs=IN_VMEM,
        compiler_params=params(6, slots),
        cost_estimate=cost(2 * slots * width * hid, 2 * slots * width),
        name="input_keep" if mine else "input_send",
    )(gate_grad, up_grad, gate_w, up_w)


def weight_grad_body(after, left, right, out, done, buffers, sems):
    done[...] = jnp.zeros_like(done)
    depth, tile, columns = buffers.shape
    steps = out.shape[0] // tile
    piece = tile_of(columns, 512)

    def copy(step):
        slot = step % depth
        return pltpu.make_async_copy(
            buffers.at[slot], out.at[pl.ds(step * tile, tile), :], sems.at[slot]
        )

    for step in range(steps):
        flipped = left[:, step * tile:(step + 1) * tile].T
        if step >= depth:
            copy(step - depth).wait()
        for at in range(0, columns, piece):
            value = dot(flipped, right[:, at:at + piece])
            buffers[step % depth, :, at:at + piece] = value.astype(BF16)
        copy(step).start()
    for step in range(max(0, steps - depth), steps):
        copy(step).wait()


def weight_grad(after, left, right, name):
    slots, rows = left.shape
    columns = right.shape[1]
    tile = tile_of(rows, 256 if columns > 2048 else 512)
    return pl.pallas_call(
        weight_grad_body,
        out_shape=[pltpu.HBM((rows, columns), BF16), jax.ShapeDtypeStruct((8, LANES), F32)],
        in_specs=[ANYWHERE] + [IN_VMEM] * 2,
        out_specs=[ANYWHERE, IN_VMEM],
        scratch_shapes=[pltpu.VMEM((4, tile, columns), BF16), pltpu.SemaphoreType.DMA((4,))],
        compiler_params=params(12, slots),
        cost_estimate=cost(0, 2 * LANES),
        name=name,
    )(after, left, right)


def three_parts(value):
    high = value.astype(BF16)
    rest = value - high.astype(F32)
    mid = rest.astype(BF16)
    return high, mid, (rest - mid.astype(F32)).astype(BF16)


def write_chunks(n, total, got, router, outs):
    half = total.shape[1]
    for s in range(n):
        span = slice(s * CAP, (s + 1) * CAP)
        outs[s][:, 0:half] = (total[span, :] + got[span, :].astype(F32)).astype(BF16)
        if router is not None:
            high, mid, low = three_parts(router[span, :])
            lane = lax.broadcasted_iota(jnp.int32, (CAP, LANES), 1)
            outs[s][:, half:] = jnp.where(
                lane == 0, high, jnp.where(lane == 1, mid, jnp.where(lane == 2, low, jnp.zeros_like(low)))
            )


def merge_body(n, after, keep, got, *refs):
    write_chunks(n, keep[...], got, refs[0] if len(refs) > n else None, refs[-n:])


def merge(after, n, keep, got, *router):
    wide = keep.shape[1] + LANES * len(router)
    return pl.pallas_call(
        functools.partial(merge_body, n),
        out_shape=[jax.ShapeDtypeStruct((CAP, wide), BF16)] * n,
        in_specs=[ANYWHERE] + [IN_VMEM] * (2 + len(router)),
        out_specs=[IN_VMEM] * n,
        compiler_params=params(),
        cost_estimate=cost(0, 8 * keep.size),
        name="merge",
    )(after, keep, got, *router)


def combine_body(n, after, weights, *refs):
    chunks, out = refs[:n], refs[-1]
    total = dot(weights[0:CAP, :], chunks[0][...], 0, 0)
    for s in range(1, n):
        total += dot(weights[s * CAP:(s + 1) * CAP, :], chunks[s][...], 0, 0)
    out[...] = total.astype(BF16)


def combine(after, n, weights, chunks):
    half = chunks[0].shape[1]
    return pl.pallas_call(
        functools.partial(combine_body, n),
        out_shape=jax.ShapeDtypeStruct((weights.shape[1], half), BF16),
        in_specs=[ANYWHERE] + [IN_VMEM] * (n + 1),
        out_specs=IN_VMEM,
        compiler_params=params(),
        cost_estimate=cost(2 * weights.size * half, 2 * n * CAP * half),
        name="combine",
    )(after, weights, *chunks)


def combine_router_body(n, half, after, first, second, *refs):
    chunks, out = refs[:n], refs[-1]
    rows = first.shape[1]
    total = jnp.zeros((rows, half), F32)
    score0 = jnp.zeros((rows, LANES), F32)
    score1 = jnp.zeros((rows, LANES), F32)
    for s in range(n):
        span = pl.ds(s * CAP, CAP)
        placed0, placed1 = first[span, :], second[span, :]
        total += dot(placed0 + placed1, chunks[s][:, 0:half], 0, 0)
        score0 += dot(placed0, chunks[s][:, half:], 0, 0)
        score1 += dot(placed1, chunks[s][:, half:], 0, 0)
    out[:, 0:half] = total.astype(BF16)
    out[:, half:] = spread_scores(
        jnp.sum(score0, axis=1, keepdims=True), jnp.sum(score1, axis=1, keepdims=True)
    )


def combine_router(after, n, first, second, chunks):
    wide = chunks[0].shape[1]
    rows = first.shape[1]
    return pl.pallas_call(
        functools.partial(combine_router_body, n, wide - LANES),
        out_shape=jax.ShapeDtypeStruct((rows, wide), BF16),
        in_specs=[ANYWHERE] + [IN_VMEM] * (n + 2),
        out_specs=IN_VMEM,
        compiler_params=params(),
        cost_estimate=cost(2 * first.size * wide, 2 * n * CAP * wide),
        name="combine_router",
    )(after, first, second, *chunks)


def spread_scores(score0, score1):
    rows = score0.shape[0]
    lane = lax.broadcasted_iota(jnp.int32, (rows, LANES), 1)
    out = jnp.zeros((rows, LANES), F32)
    for k, score in enumerate((score0, score1)):
        for p, part in enumerate(three_parts(score)):
            out = jnp.where(lane == 3 * k + p, part.astype(F32), out)
    return out.astype(BF16)


def joined_scores(packed):
    values = packed.astype(F32)
    score0 = values[:, 0:1] + values[:, 1:2] + values[:, 2:3]
    score1 = values[:, 3:4] + values[:, 4:5] + values[:, 5:6]
    return score0, score1


def add_body(after, *refs):
    total = refs[0][...].astype(F32)
    for piece in refs[1:-1]:
        total += piece[...].astype(F32)
    refs[-1][...] = total.astype(BF16)


def add_pieces(after, pieces):
    return pl.pallas_call(
        add_body,
        out_shape=jax.ShapeDtypeStruct(pieces[0].shape, BF16),
        in_specs=[ANYWHERE] + [IN_VMEM] * len(pieces),
        out_specs=IN_VMEM,
        compiler_params=params(),
        cost_estimate=cost(0, 6 * pieces[0].size),
        name="add_pieces",
    )(after, *pieces)


def finish_body(half, count, layer_own, layer_other, *refs):
    own, other = refs[:count], refs[count:2 * count]
    layer, total, score = refs[2 * count:]
    rows = layer.shape[0]
    layer[:, pl.ds(own_half(half), half)] = layer_own[...]
    layer[:, pl.ds(other_half(half), half)] = layer_other[...]
    for pieces, start in ((own, own_half(half)), (other, other_half(half))):
        value = pieces[0][:, 0:half].astype(F32)
        for piece in pieces[1:]:
            value += piece[:, 0:half].astype(F32)
        total[:, pl.ds(start, half)] = value.astype(BF16)
    scores = [[joined_scores(piece[:, half:]) for piece in pieces] for pieces in (own, other)]
    sums = [[sum(part[k] for part in parts) for k in range(2)] for parts in scores]
    lane = lax.broadcasted_iota(jnp.int32, (rows, LANES), 1)
    score[...] = jnp.where(lane == 0, sums[0][0] + sums[1][0], sums[0][1] + sums[1][1]).T[0:2, :]


def finish(half, layer_own, layer_other, own, other):
    rows = own[0].shape[0]
    return pl.pallas_call(
        functools.partial(finish_body, half, len(own)),
        out_shape=[jax.ShapeDtypeStruct((rows, 2 * half), BF16)] * 2
        + [jax.ShapeDtypeStruct((2, rows), F32)],
        in_specs=[IN_VMEM] * (2 + 2 * len(own)),
        out_specs=[IN_VMEM] * 3,
        compiler_params=params(),
        cost_estimate=cost(0, 8 * rows * half),
        name="finish",
    )(layer_own, layer_other, *own, *other)


def from_chips(value):
    count = lax.axis_size("dp")
    if count == 2:
        return [value, shift(value, "dp", 1)]
    gathered = lax.all_gather(value, "dp", axis=0, tiled=False)
    return [gathered[j] for j in range(count)]


def on_device(tokens, expert_ids, gates, out_grad, gate_weight, up_weight, down_weight):
    ids, gates, tokens, out_grad, gate_weight, up_weight, down_weight = (
        pltpu.with_memory_space_constraint(v, pltpu.HBM)
        for v in (expert_ids.T, gates.T, tokens, out_grad, gate_weight, up_weight, down_weight)
    )
    n = lax.axis_size("ed")
    slots = n * CAP
    half = tokens.shape[1] // 2
    hid = gate_weight.shape[1]

    (own_tok, own_grad, own_coef), sent, placing = pick(n, hid, ids, gates, tokens, out_grad)
    arrived = [shift(sent[s - 1], "ed", s) for s in range(1, n)]
    gate_held, gate_done = load(own_coef, gate_weight)
    up_held, up_done = load(gate_done, up_weight)
    direct = stack(up_done, arrived)
    other = shift(direct, "tp", 1)
    rows, hidden, act, slope = forward(n, own_tok, direct, other, gate_held, up_held)
    scaled, gate_pre, up_pre, router, out_part, out_keep = middle(
        n, own_grad, own_coef, direct, other, hidden, act, slope, down_weight
    )
    out_got = shift(out_part, "tp", 1)
    in_part = input_part(False, BF16, slots, gate_pre, up_pre, gate_held, up_held)
    in_got = shift(in_part, "tp", 1)
    out_chunks = merge(router, n, out_keep, out_got)
    out_back = [out_chunks[0]] + [shift(out_chunks[s], "ed", -s) for s in range(1, n)]
    in_keep = input_part(True, F32, slots, gate_pre, up_pre, gate_held, up_held)
    in_chunks = merge(out_back[1], n, in_keep, in_got, router)
    in_back = [in_chunks[0]] + [shift(in_chunks[s], "ed", -s) for s in range(1, n)]
    first, second, weighted = placing
    up_w_grad, done = weight_grad(in_chunks[0], rows, up_pre, "up_grad")
    in_mine = combine_router(done, n, first, second, in_back)
    gate_w_grad, done = weight_grad(in_mine, rows, gate_pre, "gate_grad")
    out_mine = combine(done, n, weighted, out_back)
    down_grad, done = weight_grad(out_mine, hidden, scaled, "down_grad")
    in_own = from_chips(in_mine)
    out_half = add_pieces(done, from_chips(out_mine))
    layer_out, token_grad, gate_grad = finish(
        half, out_half, shift(out_half, "tp", 1),
        in_own, [shift(piece, "tp", 1) for piece in in_own],
    )
    return layer_out, token_grad, gate_grad.T, gate_w_grad, up_w_grad, down_grad


def solution(mesh):
    token_spec = P(("groups", "ed"), None)
    in_specs = (
        token_spec,
        token_spec,
        token_spec,
        token_spec,
        P(None, ("ed", "dp", "tp")),
        P(None, ("ed", "dp", "tp")),
        P(("ed", "dp", "tp"), None),
    )
    out_specs = (
        token_spec,
        token_spec,
        token_spec,
        P("groups", ("ed", "dp", "tp")),
        P("groups", ("ed", "dp", "tp")),
        P(("groups", "ed", "dp", "tp"), None),
    )
    return jax.shard_map(
        on_device, mesh=mesh, in_specs=in_specs, out_specs=out_specs, check_vma=False
    )
```

time: 104 us -> 97.4 us (0.937)
  Pallas kernels: 73.4 us -> 63.8 us
  waiting for transfers between devices: 6.18 us -> 9.45 us
    pallas_call x8 -> x6, Pallas kernels: 44 us -> 35 us  [the longest x3 17.9 us: weight_grad(): pl.pallas_call(weight_grad_body, out_shape=[pltpu.HBM((rows, columns), BF...]
    ppermute x22 -> x17, waiting for transfers between devices: 6.18 us -> 9.45 us  [shift(): lax.ppermute(value, axis, [(j, (j + step) % count) for j in range(count)])]
    ppermute x22 -> x17, starting transfers between devices: 22.6 us -> 22.9 us  [shift(): lax.ppermute(value, axis, [(j, (j + step) % count) for j in range(count)])]
  transfers between devices with their start and end apart: 22 -> 17, of which waited for: 2 -> 5; matrix products, arithmetic and copies ran while one was open for 0% -> 0% of each run, Pallas kernels for 51% -> 40%
where the time goes in v3:
time: 97.4 us; the launch traced here: 97 us
  Pallas kernels  63.8 us (66%)
  starting transfers between devices  22.9 us (24%)
  waiting for transfers between devices  9.45 us (10%)
    ppermute x17, starting transfers between devices, shift(): lax.ppermute(value, axis, [(j, (j + step) % count) for j in range(count)])  22.9 us
    pallas_call x3, Pallas kernels, weight_grad(): pl.pallas_call(weight_grad_body, out_shape=[pltpu.HBM((rows, columns), BF...  17.9 us
    pallas_call x1, Pallas kernels, middle(): pl.pallas_call(middle_body, out_shape=[pltpu.VMEM((padded(slots), width),...  14.8 us
    pallas_call x2, Pallas kernels, load(): pl.pallas_call(load_body, out_shape=[pltpu.VMEM(weight.shape, BF16), jax....  10.6 us
    ppermute x17, waiting for transfers between devices, shift(): lax.ppermute(value, axis, [(j, (j + step) % count) for j in range(count)])  9.45 us
    pallas_call x2, Pallas kernels, input_part(): pl.pallas_call(functools.partial(input_body, mine), out_shape=jax.ShapeDt...  9.24 us
    pallas_call x1, Pallas kernels, forward(): pl.pallas_call(functools.partial(forward_body, slots), out_shape=[pltpu.V...  6.36 us
    pallas_call x1, Pallas kernels, pick(): pl.pallas_call(functools.partial(pick_body, n, hid, lax.axis_size(('dp',...  2.28 us
  transfers between devices with their start and end apart: 17, of which 5 were waited for; matrix products, arithmetic and copies ran while one was open for 0% of the time, Pallas kernels for 40%

profile of v3, /device:TPU:0, one launch (start us, length us, event | category | flops | bytes accessed | tf_op | source)
XLA Modules:
  0.0 97.0 jit_solution(14231204918964238241)
XLA Ops:
  0.6 2.3 %pick.1 = (bf16[48,2048]{1,0:T(8,128)(2,1)S(1)}, bf16[48,2048]{1,0:T(8,128)(2,1)S(1)}, bf16[48,128]{1,0:T(8,128)(2,1)S(1)}, bf16[48,2176]{1,0:T(8,128)(2,1)S(1)}...) custom-call(s32[2,128]{1,0:T(2,128)} %bitcast.3, ...), custom_call_target="tpu_custom_call" | custom-call | flops 201326592 | bytes 2097152 | tf_op jit(solution)/shard_map/pick/pallas_call | solution.py:110
  2.9 3.1 %collective-permute-start = (bf16[48,2176]{1,0:T(8,128)(2,1)S(1)}, bf16[48,2176]{1,0:T(8,128)(2,1)S(1)}, u32[]{:S(2)}, u32[]{:S(2)}) collective-permute-start(bf16[48,2176]{1,0:T(8,128)(2,1)S(1)} %get-tuple-element.50), channel_id=1, source_target_pairs={{0,4},{4,8},{8,12},{12,0},{1,5},{5,9},{9,13},{13,1},{2,6},{6,10},{... | collective-permute-start | bytes 626696 | tf_op jit(solution)/shard_map/ppermute | solution.py:57
  6.0 2.6 %collective-permute-start.1 = (bf16[48,2176]{1,0:T(8,128)(2,1)S(1)}, bf16[48,2176]{1,0:T(8,128)(2,1)S(1)}, u32[]{:S(2)}, u32[]{:S(2)}) collective-permute-start(bf16[48,2176]{1,0:T(8,128)(2,1)S(1)} %get-tuple-element.51), channel_id=1, source_target_pairs={{0,8},{4,12},{8,0},{12,4},{1,9},{5,13},{9,1},{13,5},{2,10},{6,14},... | collective-permute-start | bytes 626696 | tf_op jit(solution)/shard_map/ppermute | solution.py:57
  8.6 1.3 %collective-permute-start.2 = (bf16[48,2176]{1,0:T(8,128)(2,1)S(1)}, bf16[48,2176]{1,0:T(8,128)(2,1)S(1)}, u32[]{:S(2)}, u32[]{:S(2)}) collective-permute-start(bf16[48,2176]{1,0:T(8,128)(2,1)S(1)} %get-tuple-element.52), channel_id=1, source_target_pairs={{0,12},{4,0},{8,4},{12,8},{1,13},{5,1},{9,5},{13,9},{2,14},{6,2},{... | collective-permute-start | bytes 626696 | tf_op jit(solution)/shard_map/ppermute | solution.py:57
  9.9 5.3 %load.2 = (bf16[2048,3584]{1,0:T(8,128)(2,1)S(1)}, f32[8,128]{1,0:T(8,128)S(1)}) custom-call(bf16[48,128]{1,0:T(8,128)(2,1)S(1)} %get-tuple-element.47.after.coef_own, bf16[2048,3584]{1,0:T(8,128)(2,1)} %weight.2), custom_call_target="tpu_custom_call" | custom-call | bytes 256 | tf_op jit(solution)/shard_map/load/pallas_call | solution.py:134
  15.2 5.3 %load.3 = (bf16[2048,3584]{1,0:T(8,128)(2,1)S(1)}, f32[8,128]{1,0:T(8,128)S(1)}) custom-call(f32[8,128]{1,0:T(8,128)S(1)} %get-tuple-element.48.after, bf16[2048,3584]{1,0:T(8,128)(2,1)} %weight.3), custom_call_target="tpu_custom_call" | custom-call | bytes 256 | tf_op jit(solution)/shard_map/load/pallas_call | solution.py:134
  20.5 1.7 %collective-permute-done.1.refs_1_ = bf16[48,2176]{1,0:T(8,128)(2,1)S(1)} collective-permute-done((bf16[48,2176]{1,0:T(8,128)(2,1)S(1)}, bf16[48,2176]{1,0:T(8,128)(2,1)S(1)}, u32[]{:S(2)}, u32[]{:S(2)}) %collective-permute-start.1) | collective-permute-done | bytes 208928 | tf_op jit(solution)/shard_map/ppermute | solution.py:57
  22.4 2.0 %collective-permute-done.3.other = bf16[144,2176]{1,0:T(8,128)(2,1)S(1)} collective-permute-done((bf16[144,2176]{1,0:T(8,128)(2,1)S(1)}, bf16[144,2176]{1,0:T(8,128)(2,1)S(1)}, u32[]{:S(2)}, u32[]{:S(2)}) %collective-permute-start.3) | collective-permute-done | bytes 626720 | tf_op jit(solution)/shard_map/ppermute | solution.py:57
  24.4 6.4 %forward.1 = (bf16[256,2048]{1,0:T(8,128)(2,1)S(1)}, bf16[256,3584]{1,0:T(8,128)(2,1)S(1)}, bf16[192,3584]{1,0:T(8,128)(2,1)S(1)}, bf16[192,3584]{1,0:T(8,128)(2,1)S(1)}) custom-call(bf16[48,2048]{1,0:T(8,128)(2,1)S(1)} %get-tuple-element.53.own, bf16[144,2176]{1,0:T(8,128)(2,1)S(1)} %stack.1.direct, bf16[144,2176]{1,0:T(8,128)(2,1)S(1)} %collective-permute-done.3.other, ...), custom_call_target="tpu_custom_call" | custom-call | bytes 786432 | tf_op jit(solution)/shard_map/forward/pallas_call | solution.py:197
  30.8 14.8 %middle.1 = (bf16[256,2048]{1,0:T(8,128)(2,1)S(1)}, bf16[256,3584]{1,0:T(8,128)(2,1)S(1)}, bf16[256,3584]{1,0:T(8,128)(2,1)S(1)}, f32[192,128]{1,0:T(8,128)S(1)}...) custom-call(bf16[48,2048]{1,0:T(8,128)(2,1)S(1)} %get-tuple-element.46.own, ...), custom_call_target="tpu_custom_call" | custom-call | flops 5637144576 | bytes 14680064 | tf_op jit(solution)/shard_map/middle/pallas_call | solution.py:275
  45.6 0.2 collective-permute-start.4
  45.8 4.6 %input_send.1 = bf16[192,1024]{1,0:T(8,128)(2,1)S(1)} custom-call(bf16[256,3584]{1,0:T(8,128)(2,1)S(1)} %get-tuple-element.63.gate_grad.right, bf16[256,3584]{1,0:T(8,128)(2,1)S(1)} %get-tuple-element.64.up_grad.right, bf16[2048,3584]{1,0:T(8,128)(2,1)S(1)} %get-tuple-element.54.gate_w, bf16[2048,3584]{1,0:T(8,128)(2,1)S(1)} %get-tuple-element.55.up_w), custom_call_target="tpu_custom_call" | custom-call | flops 2818572288 | bytes 786432 | tf_op jit(solution)/shard_map/input_send/pallas_call | solution.py:313
  50.4 0.4 collective-permute-start.6
  51.0 6.0 %collective-permute-start.5 = (bf16[48,1024]{1,0:T(8,128)(2,1)S(1)}, bf16[48,1024]{1,0:T(8,128)(2,1)S(1)}, u32[]{:S(2)}, u32[]{:S(2)}) collective-permute-start(bf16[48,1024]{1,0:T(8,128)(2,1)S(1)} %get-tuple-element.62), channel_id=1, source_target_pairs={{0,12},{4,0},{8,4},{12,8},{1,13},{5,1},{9,5},{13,9},{2,14},{6,2},{... | collective-permute-start | bytes 294920 | tf_op jit(solution)/shard_map/ppermute | solution.py:57
  57.0 4.6 %input_keep.1.keep = f32[192,1024]{1,0:T(8,128)S(1)} custom-call(bf16[256,3584]{1,0:T(8,128)(2,1)S(1)} %get-tuple-element.63.gate_grad.right, bf16[256,3584]{1,0:T(8,128)(2,1)S(1)} %get-tuple-element.64.up_grad.right, bf16[2048,3584]{1,0:T(8,128)(2,1)S(1)} %get-tuple-element.54.gate_w, bf16[2048,3584]{1,0:T(8,128)(2,1)S(1)} %get-tuple-element.55.up_w), custom_call_target="tpu_custom_call" | custom-call | flops 2818572288 | bytes 786432 | tf_op jit(solution)/shard_map/input_keep/pallas_call | solution.py:313
  61.6 0.1 merge.3
  61.8 2.0 %collective-permute-start.7 = (bf16[48,1152]{1,0:T(8,128)(2,1)S(1)}, bf16[48,1152]{1,0:T(8,128)(2,1)S(1)}, u32[]{:S(2)}, u32[]{:S(2)}) collective-permute-start(bf16[48,1152]{1,0:T(8,128)(2,1)S(1)} %get-tuple-element.70), channel_id=1, source_target_pairs={{0,12},{4,0},{8,4},{12,8},{1,13},{5,1},{9,5},{13,9},{2,14},{6,2},{... | collective-permute-start | bytes 331784 | tf_op jit(solution)/shard_map/ppermute | solution.py:57
  63.8 0.6 collective-permute-start.9
  64.4 2.3 %collective-permute-start.10 = (bf16[48,1024]{1,0:T(8,128)(2,1)S(1)}, bf16[48,1024]{1,0:T(8,128)(2,1)S(1)}, u32[]{:S(2)}, u32[]{:S(2)}) collective-permute-start(bf16[48,1024]{1,0:T(8,128)(2,1)S(1)} %get-tuple-element.76), channel_id=1, source_target_pairs={{0,8},{4,12},{8,0},{12,4},{1,9},{5,13},{9,1},{13,5},{2,10},{6,14},... | collective-permute-start | bytes 294920 | tf_op jit(solution)/shard_map/ppermute | solution.py:57
  66.8 1.4 %collective-permute-start.11 = (bf16[48,1024]{1,0:T(8,128)(2,1)S(1)}, bf16[48,1024]{1,0:T(8,128)(2,1)S(1)}, u32[]{:S(2)}, u32[]{:S(2)}) collective-permute-start(bf16[48,1024]{1,0:T(8,128)(2,1)S(1)} %get-tuple-element.77), channel_id=1, source_target_pairs={{0,4},{4,8},{8,12},{12,0},{1,5},{5,9},{9,13},{13,1},{2,6},{6,10},{... | collective-permute-start | bytes 294920 | tf_op jit(solution)/shard_map/ppermute | solution.py:57
  68.2 5.9 %up_grad.1 = (bf16[2048,3584]{1,0:T(8,128)(2,1)}, f32[8,128]{1,0:T(8,128)S(1)}) custom-call(bf16[48,1152]{1,0:T(8,128)(2,1)S(1)} %get-tuple-element.65.after.refs_0_, bf16[256,2048]{1,0:T(8,128)(2,1)S(1)} %get-tuple-element.66.left, bf16[256,3584]{1,0:T(8,128)(2,1)S(1)} %get-tuple-element.64.up_grad.right), custom_call_target="tpu_custom_call" | custom-call | bytes 256 | tf_op jit(solution)/shard_map/up_grad/pallas_call | solution.py:352
  74.1 3.8 %collective-permute-done.8.refs_2_ = bf16[48,1152]{1,0:T(8,128)(2,1)S(1)} collective-permute-done((bf16[48,1152]{1,0:T(8,128)(2,1)S(1)}, bf16[48,1152]{1,0:T(8,128)(2,1)S(1)}, u32[]{:S(2)}, u32[]{:S(2)}) %collective-permute-start.8) | collective-permute-done | bytes 110624 | tf_op jit(solution)/shard_map/ppermute | solution.py:57
  77.9 0.6 combine_router.1.after.refs_0_
  78.6 1.6 %collective-permute-start.14 = (bf16[128,1152]{1,0:T(8,128)(2,1)S(1)}, bf16[128,1152]{1,0:T(8,128)(2,1)S(1)}, u32[]{:S(2)}, u32[]{:S(2)}) collective-permute-start(bf16[128,1152]{1,0:T(8,128)(2,1)S(1)} %combine_router.1.after.refs_0_), channel_id=1, source_target_pairs={{0,2},{2,0},{1,3},{3,1},{4,6},{6,4},{5,7},{7,5},{8,10},{10,8},{9,1... | collective-permute-start | bytes 884744 | tf_op jit(solution)/shard_map/ppermute | solution.py:57
  80.1 6.0 %gate_grad.1 = (bf16[2048,3584]{1,0:T(8,128)(2,1)}, f32[8,128]{1,0:T(8,128)S(1)}) custom-call(bf16[128,1152]{1,0:T(8,128)(2,1)S(1)} %combine_router.1.after.refs_0_, bf16[256,2048]{1,0:T(8,128)(2,1)S(1)} %get-tuple-element.66.left, bf16[256,3584]{1,0:T(8,128)(2,1)S(1)} %get-tuple-element.63.gate_grad.right), custom_call_target="tpu_custom_call" | custom-call | bytes 256 | tf_op jit(solution)/shard_map/gate_grad/pallas_call | solution.py:352
  86.1 0.5 combine.1.after.refs_0_
  86.6 0.6 collective-permute-start.12
  87.2 0.5 collective-permute-start.16
  87.7 6.0 %down_grad.1 = (bf16[3584,2048]{1,0:T(8,128)(2,1)}, f32[8,128]{1,0:T(8,128)S(1)}) custom-call(bf16[128,1024]{1,0:T(8,128)(2,1)S(1)} %combine.1.after.refs_0_, bf16[256,3584]{1,0:T(8,128)(2,1)S(1)} %get-tuple-element.56.hidden.left, bf16[256,2048]{1,0:T(8,128)(2,1)S(1)} %get-tuple-element.78.right), custom_call_target="tpu_custom_call" | custom-call | bytes 256 | tf_op jit(solution)/shard_map/down_grad/pallas_call | solution.py:352
  93.7 0.3 collective-permute-done.12.refs_1_
  94.2 1.5 %collective-permute-done.13.layer_other = bf16[128,1024]{1,0:T(8,128)(2,1)S(1)} collective-permute-done((bf16[128,1024]{1,0:T(8,128)(2,1)S(1)}, bf16[128,1024]{1,0:T(8,128)(2,1)S(1)}, u32[]{:S(2)}, u32[]{:S(2)}) %collective-permute-start.13) | collective-permute-done | bytes 262176 | tf_op jit(solution)/shard_map/ppermute | solution.py:57
  95.7 1.3 %finish.1 = (bf16[128,2048]{1,0:T(8,128)(2,1)}, bf16[128,2048]{1,0:T(8,128)(2,1)}, f32[2,128]{1,0:T(2,128)}) custom-call(bf16[128,1024]{1,0:T(8,128)(2,1)S(1)} %add_pieces.1.layer_own, bf16[128,1024]{1,0:T(8,128)(2,1)S(1)} %collective-permute-done.13.layer_other, bf16[128,1152]{1,0:T(8,128)(2,1)S(1)} %combine_router.1.after.refs_0_, ...), custom_call_target="tpu_custom_call" | custom-call | bytes 1048576 | tf_op jit(solution)/shard_map/finish/pallas_call | solution.py:509
  (19 shorter events, 0.4 us)
Async XLA Ops:
  2.9 17.6 %collective-permute-start = (bf16[48,2176]{1,0:T(8,128)(2,1)S(1)}, bf16[48,2176]{1,0:T(8,128)(2,1)S(1)}, u32[]{:S(2)}, u32[]{:S(2)}) collective-permute-start(bf16[48,2176]{1,0:T(8,128)(2,1)S(1)} %get-tuple-element.50), channel_id=1, source_target_pairs={{0,4},{4,8},{8,12},{12,0},{1,5},{5,9},{9,13},{13,1},{2,6},{6,10},{... | collective-permute-start | bytes 626696 | tf_op jit(solution)/shard_map/ppermute | solution.py:57
  6.0 16.3 %collective-permute-start.1 = (bf16[48,2176]{1,0:T(8,128)(2,1)S(1)}, bf16[48,2176]{1,0:T(8,128)(2,1)S(1)}, u32[]{:S(2)}, u32[]{:S(2)}) collective-permute-start(bf16[48,2176]{1,0:T(8,128)(2,1)S(1)} %get-tuple-element.51), channel_id=1, source_target_pairs={{0,8},{4,12},{8,0},{12,4},{1,9},{5,13},{9,1},{13,5},{2,10},{6,14},... | collective-permute-start | bytes 626696 | tf_op jit(solution)/shard_map/ppermute | solution.py:57
  8.6 13.7 %collective-permute-start.2 = (bf16[48,2176]{1,0:T(8,128)(2,1)S(1)}, bf16[48,2176]{1,0:T(8,128)(2,1)S(1)}, u32[]{:S(2)}, u32[]{:S(2)}) collective-permute-start(bf16[48,2176]{1,0:T(8,128)(2,1)S(1)} %get-tuple-element.52), channel_id=1, source_target_pairs={{0,12},{4,0},{8,4},{12,8},{1,13},{5,1},{9,5},{13,9},{2,14},{6,2},{... | collective-permute-start | bytes 626696 | tf_op jit(solution)/shard_map/ppermute | solution.py:57
  22.3 2.1 %collective-permute-start.3 = (bf16[144,2176]{1,0:T(8,128)(2,1)S(1)}, bf16[144,2176]{1,0:T(8,128)(2,1)S(1)}, u32[]{:S(2)}, u32[]{:S(2)}) collective-permute-start(bf16[144,2176]{1,0:T(8,128)(2,1)S(1)} %stack.1.direct), channel_id=1, source_target_pairs={{0,1},{1,0},{2,3},{3,2},{4,5},{5,4},{6,7},{7,6},{8,9},{9,8},{10,11... | collective-permute-start | bytes 1880072 | tf_op jit(solution)/shard_map/ppermute | solution.py:57
  45.6 5.3 %collective-permute-start.4 = (bf16[192,1024]{1,0:T(8,128)(2,1)S(1)}, bf16[192,1024]{1,0:T(8,128)(2,1)S(1)}, u32[]{:S(2)}, u32[]{:S(2)}) collective-permute-start(bf16[192,1024]{1,0:T(8,128)(2,1)S(1)} %get-tuple-element.61), channel_id=1, source_target_pairs={{0,1},{1,0},{2,3},{3,2},{4,5},{5,4},{6,7},{7,6},{8,9},{9,8},{10,11... | collective-permute-start | bytes 1179656 | tf_op jit(solution)/shard_map/ppermute | solution.py:57
  50.4 11.2 %collective-permute-start.6 = (bf16[192,1024]{1,0:T(8,128)(2,1)S(1)}, bf16[192,1024]{1,0:T(8,128)(2,1)S(1)}, u32[]{:S(2)}, u32[]{:S(2)}) collective-permute-start(bf16[192,1024]{1,0:T(8,128)(2,1)S(1)} %input_send.1), channel_id=1, source_target_pairs={{0,1},{1,0},{2,3},{3,2},{4,5},{5,4},{6,7},{7,6},{8,9},{9,8},{10,11... | collective-permute-start | bytes 1179656 | tf_op jit(solution)/shard_map/ppermute | solution.py:57
  51.0 10.7 %collective-permute-start.5 = (bf16[48,1024]{1,0:T(8,128)(2,1)S(1)}, bf16[48,1024]{1,0:T(8,128)(2,1)S(1)}, u32[]{:S(2)}, u32[]{:S(2)}) collective-permute-start(bf16[48,1024]{1,0:T(8,128)(2,1)S(1)} %get-tuple-element.62), channel_id=1, source_target_pairs={{0,12},{4,0},{8,4},{12,8},{1,13},{5,1},{9,5},{13,9},{2,14},{6,2},{... | collective-permute-start | bytes 294920 | tf_op jit(solution)/shard_map/ppermute | solution.py:57
  61.8 12.4 %collective-permute-start.7 = (bf16[48,1152]{1,0:T(8,128)(2,1)S(1)}, bf16[48,1152]{1,0:T(8,128)(2,1)S(1)}, u32[]{:S(2)}, u32[]{:S(2)}) collective-permute-start(bf16[48,1152]{1,0:T(8,128)(2,1)S(1)} %get-tuple-element.70), channel_id=1, source_target_pairs={{0,12},{4,0},{8,4},{12,8},{1,13},{5,1},{9,5},{13,9},{2,14},{6,2},{... | collective-permute-start | bytes 331784 | tf_op jit(solution)/shard_map/ppermute | solution.py:57
  63.8 14.1 %collective-permute-start.8 = (bf16[48,1152]{1,0:T(8,128)(2,1)S(1)}, bf16[48,1152]{1,0:T(8,128)(2,1)S(1)}, u32[]{:S(2)}, u32[]{:S(2)}) collective-permute-start(bf16[48,1152]{1,0:T(8,128)(2,1)S(1)} %get-tuple-element.71), channel_id=1, source_target_pairs={{0,8},{4,12},{8,0},{12,4},{1,9},{5,13},{9,1},{13,5},{2,10},{6,14},... | collective-permute-start | bytes 331784 | tf_op jit(solution)/shard_map/ppermute | solution.py:57
  63.8 14.1 %collective-permute-start.9 = (bf16[48,1152]{1,0:T(8,128)(2,1)S(1)}, bf16[48,1152]{1,0:T(8,128)(2,1)S(1)}, u32[]{:S(2)}, u32[]{:S(2)}) collective-permute-start(bf16[48,1152]{1,0:T(8,128)(2,1)S(1)} %get-tuple-element.72), channel_id=1, source_target_pairs={{0,4},{4,8},{8,12},{12,0},{1,5},{5,9},{9,13},{13,1},{2,6},{6,10},{... | collective-permute-start | bytes 331784 | tf_op jit(solution)/shard_map/ppermute | solution.py:57
  64.4 21.7 %collective-permute-start.10 = (bf16[48,1024]{1,0:T(8,128)(2,1)S(1)}, bf16[48,1024]{1,0:T(8,128)(2,1)S(1)}, u32[]{:S(2)}, u32[]{:S(2)}) collective-permute-start(bf16[48,1024]{1,0:T(8,128)(2,1)S(1)} %get-tuple-element.76), channel_id=1, source_target_pairs={{0,8},{4,12},{8,0},{12,4},{1,9},{5,13},{9,1},{13,5},{2,10},{6,14},... | collective-permute-start | bytes 294920 | tf_op jit(solution)/shard_map/ppermute | solution.py:57
  66.8 19.3 %collective-permute-start.11 = (bf16[48,1024]{1,0:T(8,128)(2,1)S(1)}, bf16[48,1024]{1,0:T(8,128)(2,1)S(1)}, u32[]{:S(2)}, u32[]{:S(2)}) collective-permute-start(bf16[48,1024]{1,0:T(8,128)(2,1)S(1)} %get-tuple-element.77), channel_id=1, source_target_pairs={{0,4},{4,8},{8,12},{12,0},{1,5},{5,9},{9,13},{13,1},{2,6},{6,10},{... | collective-permute-start | bytes 294920 | tf_op jit(solution)/shard_map/ppermute | solution.py:57
  78.6 8.6 %collective-permute-start.14 = (bf16[128,1152]{1,0:T(8,128)(2,1)S(1)}, bf16[128,1152]{1,0:T(8,128)(2,1)S(1)}, u32[]{:S(2)}, u32[]{:S(2)}) collective-permute-start(bf16[128,1152]{1,0:T(8,128)(2,1)S(1)} %combine_router.1.after.refs_0_), channel_id=1, source_target_pairs={{0,2},{2,0},{1,3},{3,1},{4,6},{6,4},{5,7},{7,5},{8,10},{10,8},{9,1... | collective-permute-start | bytes 884744 | tf_op jit(solution)/shard_map/ppermute | solution.py:57
  86.6 7.4 %collective-permute-start.12 = (bf16[128,1024]{1,0:T(8,128)(2,1)S(1)}, bf16[128,1024]{1,0:T(8,128)(2,1)S(1)}, u32[]{:S(2)}, u32[]{:S(2)}) collective-permute-start(bf16[128,1024]{1,0:T(8,128)(2,1)S(1)} %combine.1.after.refs_0_), channel_id=1, source_target_pairs={{0,2},{2,0},{1,3},{3,1},{4,6},{6,4},{5,7},{7,5},{8,10},{10,8},{9,1... | collective-permute-start | bytes 786440 | tf_op jit(solution)/shard_map/ppermute | solution.py:57
  87.2 7.0 %collective-permute-start.15 = (bf16[128,1152]{1,0:T(8,128)(2,1)S(1)}, bf16[128,1152]{1,0:T(8,128)(2,1)S(1)}, u32[]{:S(2)}, u32[]{:S(2)}) collective-permute-start(bf16[128,1152]{1,0:T(8,128)(2,1)S(1)} %combine_router.1.after.refs_0_), channel_id=1, source_target_pairs={{0,1},{1,0},{2,3},{3,2},{4,5},{5,4},{6,7},{7,6},{8,9},{9,8},{10,11... | collective-permute-start | bytes 884744 | tf_op jit(solution)/shard_map/ppermute | solution.py:57
  87.2 8.5 %collective-permute-start.16 = (bf16[128,1152]{1,0:T(8,128)(2,1)S(1)}, bf16[128,1152]{1,0:T(8,128)(2,1)S(1)}, u32[]{:S(2)}, u32[]{:S(2)}) collective-permute-start(bf16[128,1152]{1,0:T(8,128)(2,1)S(1)} %collective-permute-done.14.refs_1_), channel_id=1, source_target_pairs={{0,1},{1,0},{2,3},{3,2},{4,5},{5,4},{6,7},{7,6},{8,9},{9,8},{10,11... | collective-permute-start | bytes 884744 | tf_op jit(solution)/shard_map/ppermute | solution.py:57
  94.1 1.6 %collective-permute-start.13 = (bf16[128,1024]{1,0:T(8,128)(2,1)S(1)}, bf16[128,1024]{1,0:T(8,128)(2,1)S(1)}, u32[]{:S(2)}, u32[]{:S(2)}) collective-permute-start(bf16[128,1024]{1,0:T(8,128)(2,1)S(1)} %add_pieces.1.layer_own), channel_id=1, source_target_pairs={{0,1},{1,0},{2,3},{3,2},{4,5},{5,4},{6,7},{7,6},{8,9},{9,8},{10,11... | collective-permute-start | bytes 786440 | tf_op jit(solution)/shard_map/ppermute | solution.py:57

commit v4 on v3

--- a/solution.py
+++ b/solution.py
@@ -177,7 +177,8 @@
     width, hid = gate_w.shape
     gather_rows(width // 2, 0, own, direct, other, rows_out.at[pl.ds(0, slots)])
     clear_padding(slots, rows_out)
-    clear_padding(slots, hidden)
+    for ref in (hidden, act, slope):
+        clear_padding(slots, ref)
     rows = rows_out[0:slots, :]
     tile = tile_of(hid, 512)
     for at in range(0, hid, tile):
@@ -187,8 +188,8 @@
         logistic = jax.nn.sigmoid(pre_gate)
         silu = pre_gate * logistic
         hidden[0:slots, span] = (silu * pre_up).astype(BF16)
-        act[:, span] = silu.astype(BF16)
-        slope[:, span] = (pre_up * logistic * (1.0 + pre_gate * (1.0 - logistic))).astype(BF16)
+        act[0:slots, span] = silu.astype(BF16)
+        slope[0:slots, span] = (pre_up * logistic * (1.0 + pre_gate * (1.0 - logistic))).astype(BF16)
 
 
 def forward(n, own, direct, other, gate_w, up_w):
@@ -199,8 +200,8 @@
         out_shape=[
             pltpu.VMEM((padded(slots), width), BF16),
             pltpu.VMEM((padded(slots), hid), BF16),
-            pltpu.VMEM((slots, hid), BF16),
-            pltpu.VMEM((slots, hid), BF16),
+            pltpu.VMEM((padded(slots), hid), BF16),
+            pltpu.VMEM((padded(slots), hid), BF16),
         ],
         in_specs=[IN_VMEM] * 5,
         out_specs=[IN_VMEM] * 4,
@@ -235,7 +236,8 @@
     coef[0:CAP, :] = coef_own[...].astype(F32)
     coef[CAP:, :] = direct[:, width:].astype(F32)
     scale = coef[:, 0:1]
-    for ref in (scaled, gate_grad, up_grad):
+    clear_padding(slots, scaled)
+    for ref in (gate_grad, up_grad):
         clear_padding(slots, ref)
     scaled[0:slots, :] = (scale * held[...].astype(F32)).astype(BF16)
     score = jnp.zeros((slots, LANES), F32)
@@ -260,8 +262,8 @@
             rest = jnp.sum(product[:, tile // LANES * LANES:], axis=1, keepdims=True)
             score += jnp.where(lax.broadcasted_iota(jnp.int32, score.shape, 1) == 0, rest, 0.0)
         grad = scale * back
-        gate_grad[0:slots, span] = (grad * slope[:, span].astype(F32)).astype(BF16)
-        up_grad[0:slots, span] = (grad * act[:, span].astype(F32)).astype(BF16)
+        gate_grad[0:slots, span] = (grad * slope[0:slots, span].astype(F32)).astype(BF16)
+        up_grad[0:slots, span] = (grad * act[0:slots, span].astype(F32)).astype(BF16)
     send[...] = total[:, pl.ds(other_half(half), half)].astype(BF16)
     keep[...] = total[:, pl.ds(own_half(half), half)]
     router[...] = jnp.broadcast_to(jnp.sum(score, axis=1, keepdims=True), router.shape)
@@ -288,10 +290,11 @@
             pltpu.VMEM((slots, width), BF16),
             pltpu.VMEM((slots, width), F32),
             pltpu.VMEM((slots, LANES), F32),
-            pltpu.VMEM((2, tile, width), BF16),
-            pltpu.SemaphoreType.DMA((2,)),
+            pltpu.VMEM((4, tile, width), BF16),
+            pltpu.SemaphoreType.DMA((4,)),
         ],
-        compiler_params=params(7, slots),
+        input_output_aliases={5: 2, 6: 1},
+        compiler_params=params(9, slots),
         cost_estimate=cost(4 * slots * width * hid, 2 * width * hid),
         name="middle",
     )(own, coef_own, direct, other, hidden, act, slope, down)
@@ -368,30 +371,31 @@
     return high, mid, (rest - mid.astype(F32)).astype(BF16)
 
 
-def write_chunks(n, total, got, router, outs):
+def write_chunks(chosen, total, got, router, outs):
     half = total.shape[1]
-    for s in range(n):
+    for j, s in enumerate(chosen):
         span = slice(s * CAP, (s + 1) * CAP)
-        outs[s][:, 0:half] = (total[span, :] + got[span, :].astype(F32)).astype(BF16)
+        outs[j][:, 0:half] = (total[span, :] + got[span, :].astype(F32)).astype(BF16)
         if router is not None:
             high, mid, low = three_parts(router[span, :])
             lane = lax.broadcasted_iota(jnp.int32, (CAP, LANES), 1)
-            outs[s][:, half:] = jnp.where(
+            outs[j][:, half:] = jnp.where(
                 lane == 0, high, jnp.where(lane == 1, mid, jnp.where(lane == 2, low, jnp.zeros_like(low)))
             )
 
 
-def merge_body(n, after, keep, got, *refs):
-    write_chunks(n, keep[...], got, refs[0] if len(refs) > n else None, refs[-n:])
-
-
-def merge(after, n, keep, got, *router):
+def merge_body(chosen, after, keep, got, *refs):
+    count = len(chosen)
+    write_chunks(chosen, keep, got, refs[0] if len(refs) > count else None, refs[-count:])
+
+
+def merge(after, chosen, keep, got, *router):
     wide = keep.shape[1] + LANES * len(router)
     return pl.pallas_call(
-        functools.partial(merge_body, n),
-        out_shape=[jax.ShapeDtypeStruct((CAP, wide), BF16)] * n,
+        functools.partial(merge_body, chosen),
+        out_shape=[jax.ShapeDtypeStruct((CAP, wide), BF16)] * len(chosen),
         in_specs=[ANYWHERE] + [IN_VMEM] * (2 + len(router)),
-        out_specs=[IN_VMEM] * n,
+        out_specs=[IN_VMEM] * len(chosen),
         compiler_params=params(),
         cost_estimate=cost(0, 8 * keep.size),
         name="merge",
@@ -549,13 +553,13 @@
     out_got = shift(out_part, "tp", 1)
     in_part = input_part(False, BF16, slots, gate_pre, up_pre, gate_held, up_held)
     in_got = shift(in_part, "tp", 1)
-    out_chunks = merge(router, n, out_keep, out_got)
-    out_back = [out_chunks[0]] + [shift(out_chunks[s], "ed", -s) for s in range(1, n)]
     in_keep = input_part(True, F32, slots, gate_pre, up_pre, gate_held, up_held)
-    in_chunks = merge(out_back[1], n, in_keep, in_got, router)
+    in_chunks = merge(router, range(n), in_keep, in_got, router)
     in_back = [in_chunks[0]] + [shift(in_chunks[s], "ed", -s) for s in range(1, n)]
     first, second, weighted = placing
     up_w_grad, done = weight_grad(in_chunks[0], rows, up_pre, "up_grad")
+    out_chunks = merge(done, range(n), out_keep, out_got)
+    out_back = [out_chunks[0]] + [shift(out_chunks[s], "ed", -s) for s in range(1, n)]
     in_mine = combine_router(done, n, first, second, in_back)
     gate_w_grad, done = weight_grad(in_mine, rows, gate_pre, "gate_grad")
     out_mine = combine(done, n, weighted, out_back)

time: 97.4 us -> 91.7 us (0.941)
  waiting for transfers between devices: 9.45 us -> 5.34 us
  Pallas kernels: 63.8 us -> 62.1 us
    ppermute x17, waiting for transfers between devices: 9.45 us -> 5.34 us  [shift(): lax.ppermute(value, axis, [(j, (j + step) % count) for j in range(count)])]
    pallas_call x1, Pallas kernels: 14.8 us -> 13 us  [middle(): pl.pallas_call(middle_body, out_shape=[pltpu.VMEM((padded(slots), width),...]
  transfers between devices with their start and end apart: 17 -> 17, of which waited for: 5 -> 3; matrix products, arithmetic and copies ran while one was open for 0% -> 0% of each run, Pallas kernels for 40% -> 38%
where the time goes in v4:
time: 91.7 us; the launch traced here: 91.5 us
  Pallas kernels  62.1 us (68%)
  starting transfers between devices  23.2 us (25%)
  waiting for transfers between devices  5.34 us (6%)
    ppermute x17, starting transfers between devices, shift(): lax.ppermute(value, axis, [(j, (j + step) % count) for j in range(count)])  23.2 us
    pallas_call x3, Pallas kernels, weight_grad(): pl.pallas_call(weight_grad_body, out_shape=[pltpu.HBM((rows, columns), BF...  17.9 us
    pallas_call x1, Pallas kernels, middle(): pl.pallas_call(middle_body, out_shape=[pltpu.VMEM((padded(slots), width),...  13 us
    pallas_call x2, Pallas kernels, load(): pl.pallas_call(load_body, out_shape=[pltpu.VMEM(weight.shape, BF16), jax....  10.6 us
    pallas_call x2, Pallas kernels, input_part(): pl.pallas_call(functools.partial(input_body, mine), out_shape=jax.ShapeDt...  9.25 us
    pallas_call x1, Pallas kernels, forward(): pl.pallas_call(functools.partial(forward_body, slots), out_shape=[pltpu.V...  6.43 us
    ppermute x17, waiting for transfers between devices, shift(): lax.ppermute(value, axis, [(j, (j + step) % count) for j in range(count)])  5.34 us
    pallas_call x1, Pallas kernels, pick(): pl.pallas_call(functools.partial(pick_body, n, hid, lax.axis_size(('dp',...  2.28 us
  transfers between devices with their start and end apart: 17, of which 3 were waited for; matrix products, arithmetic and copies ran while one was open for 0% of the time, Pallas kernels for 38%

profile of v4, /device:TPU:0, one launch (start us, length us, event | category | flops | bytes accessed | tf_op | source)
XLA Modules:
  0.0 91.5 jit_solution(14705830685205594618)
XLA Ops:
  0.6 2.3 %pick.1 = (bf16[48,2048]{1,0:T(8,128)(2,1)S(1)}, bf16[48,2048]{1,0:T(8,128)(2,1)S(1)}, bf16[48,128]{1,0:T(8,128)(2,1)S(1)}, bf16[48,2176]{1,0:T(8,128)(2,1)S(1)}...) custom-call(s32[2,128]{1,0:T(2,128)} %bitcast.3, ...), custom_call_target="tpu_custom_call" | custom-call | flops 201326592 | bytes 2097152 | tf_op jit(solution)/shard_map/pick/pallas_call | solution.py:110
  2.9 3.1 %collective-permute-start = (bf16[48,2176]{1,0:T(8,128)(2,1)S(1)}, bf16[48,2176]{1,0:T(8,128)(2,1)S(1)}, u32[]{:S(2)}, u32[]{:S(2)}) collective-permute-start(bf16[48,2176]{1,0:T(8,128)(2,1)S(1)} %get-tuple-element.50), channel_id=1, source_target_pairs={{0,4},{4,8},{8,12},{12,0},{1,5},{5,9},{9,13},{13,1},{2,6},{6,10},{... | collective-permute-start | bytes 626696 | tf_op jit(solution)/shard_map/ppermute | solution.py:57
  6.0 2.6 %collective-permute-start.1 = (bf16[48,2176]{1,0:T(8,128)(2,1)S(1)}, bf16[48,2176]{1,0:T(8,128)(2,1)S(1)}, u32[]{:S(2)}, u32[]{:S(2)}) collective-permute-start(bf16[48,2176]{1,0:T(8,128)(2,1)S(1)} %get-tuple-element.51), channel_id=1, source_target_pairs={{0,8},{4,12},{8,0},{12,4},{1,9},{5,13},{9,1},{13,5},{2,10},{6,14},... | collective-permute-start | bytes 626696 | tf_op jit(solution)/shard_map/ppermute | solution.py:57
  8.6 1.3 %collective-permute-start.2 = (bf16[48,2176]{1,0:T(8,128)(2,1)S(1)}, bf16[48,2176]{1,0:T(8,128)(2,1)S(1)}, u32[]{:S(2)}, u32[]{:S(2)}) collective-permute-start(bf16[48,2176]{1,0:T(8,128)(2,1)S(1)} %get-tuple-element.52), channel_id=1, source_target_pairs={{0,12},{4,0},{8,4},{12,8},{1,13},{5,1},{9,5},{13,9},{2,14},{6,2},{... | collective-permute-start | bytes 626696 | tf_op jit(solution)/shard_map/ppermute | solution.py:57
  9.9 5.3 %load.2 = (bf16[2048,3584]{1,0:T(8,128)(2,1)S(1)}, f32[8,128]{1,0:T(8,128)S(1)}) custom-call(bf16[48,128]{1,0:T(8,128)(2,1)S(1)} %get-tuple-element.47.after.coef_own, bf16[2048,3584]{1,0:T(8,128)(2,1)} %weight.2), custom_call_target="tpu_custom_call" | custom-call | bytes 256 | tf_op jit(solution)/shard_map/load/pallas_call | solution.py:134
  15.2 5.3 %load.3 = (bf16[2048,3584]{1,0:T(8,128)(2,1)S(1)}, f32[8,128]{1,0:T(8,128)S(1)}) custom-call(f32[8,128]{1,0:T(8,128)S(1)} %get-tuple-element.48.after, bf16[2048,3584]{1,0:T(8,128)(2,1)} %weight.3), custom_call_target="tpu_custom_call" | custom-call | bytes 256 | tf_op jit(solution)/shard_map/load/pallas_call | solution.py:134
  20.5 1.7 %collective-permute-done.1.refs_1_ = bf16[48,2176]{1,0:T(8,128)(2,1)S(1)} collective-permute-done((bf16[48,2176]{1,0:T(8,128)(2,1)S(1)}, bf16[48,2176]{1,0:T(8,128)(2,1)S(1)}, u32[]{:S(2)}, u32[]{:S(2)}) %collective-permute-start.1) | collective-permute-done | bytes 208928 | tf_op jit(solution)/shard_map/ppermute | solution.py:57
  22.3 0.1 collective-permute-start.3
  22.4 2.0 %collective-permute-done.3.other = bf16[144,2176]{1,0:T(8,128)(2,1)S(1)} collective-permute-done((bf16[144,2176]{1,0:T(8,128)(2,1)S(1)}, bf16[144,2176]{1,0:T(8,128)(2,1)S(1)}, u32[]{:S(2)}, u32[]{:S(2)}) %collective-permute-start.3) | collective-permute-done | bytes 626720 | tf_op jit(solution)/shard_map/ppermute | solution.py:57
  24.4 6.4 %forward.1 = (bf16[256,2048]{1,0:T(8,128)(2,1)S(1)}, bf16[256,3584]{1,0:T(8,128)(2,1)S(1)}, bf16[256,3584]{1,0:T(8,128)(2,1)S(1)}, bf16[256,3584]{1,0:T(8,128)(2,1)S(1)}) custom-call(bf16[48,2048]{1,0:T(8,128)(2,1)S(1)} %get-tuple-element.53.own, bf16[144,2176]{1,0:T(8,128)(2,1)S(1)} %stack.1.direct, bf16[144,2176]{1,0:T(8,128)(2,1)S(1)} %collective-permute-done.3.other, ...), custom_call_target="tpu_custom_call" | custom-call | bytes 786432 | tf_op jit(solution)/shard_map/forward/pallas_call | solution.py:198
  30.9 13.0 %middle.1 = (bf16[256,2048]{1,0:T(8,128)(2,1)S(1)}, bf16[256,3584]{1,0:T(8,128)(2,1)S(1)}, bf16[256,3584]{1,0:T(8,128)(2,1)S(1)}, f32[192,128]{1,0:T(8,128)S(1)}...) custom-call(bf16[48,2048]{1,0:T(8,128)(2,1)S(1)} %get-tuple-element.46.own,, ...), custom_call_target="tpu_custom_call", output_to_operand_aliasing={{2}: (5, {}), {1}: (6, {})} | custom-call | flops 5637144576 | bytes 14680064 | tf_op jit(solution)/shard_map/middle/pallas_call | solution.py:277
  43.9 4.6 %input_send.1 = bf16[192,1024]{1,0:T(8,128)(2,1)S(1)} custom-call(bf16[256,3584]{1,0:T(8,128)(2,1)S(1)} %get-tuple-element.60.gate_grad.right, bf16[256,3584]{1,0:T(8,128)(2,1)S(1)} %get-tuple-element.61.up_grad.right, bf16[2048,3584]{1,0:T(8,128)(2,1)S(1)} %get-tuple-element.54.gate_w, bf16[2048,3584]{1,0:T(8,128)(2,1)S(1)} %get-tuple-element.55.up_w), custom_call_target="tpu_custom_call" | custom-call | flops 2818572288 | bytes 786432 | tf_op jit(solution)/shard_map/input_send/pallas_call | solution.py:316
  48.5 0.2 collective-permute-start.4
  48.7 0.4 collective-permute-start.8
  49.1 4.6 %input_keep.1.keep = f32[192,1024]{1,0:T(8,128)S(1)} custom-call(bf16[256,3584]{1,0:T(8,128)(2,1)S(1)} %get-tuple-element.60.gate_grad.right, bf16[256,3584]{1,0:T(8,128)(2,1)S(1)} %get-tuple-element.61.up_grad.right, bf16[2048,3584]{1,0:T(8,128)(2,1)S(1)} %get-tuple-element.54.gate_w, bf16[2048,3584]{1,0:T(8,128)(2,1)S(1)} %get-tuple-element.55.up_w), custom_call_target="tpu_custom_call" | custom-call | flops 2818572288 | bytes 786432 | tf_op jit(solution)/shard_map/input_keep/pallas_call | solution.py:316
  53.7 0.1 merge.2
  53.8 6.0 %collective-permute-start.5 = (bf16[48,1152]{1,0:T(8,128)(2,1)S(1)}, bf16[48,1152]{1,0:T(8,128)(2,1)S(1)}, u32[]{:S(2)}, u32[]{:S(2)}) collective-permute-start(bf16[48,1152]{1,0:T(8,128)(2,1)S(1)} %get-tuple-element.67), channel_id=1, source_target_pairs={{0,12},{4,0},{8,4},{12,8},{1,13},{5,1},{9,5},{13,9},{2,14},{6,2},{... | collective-permute-start | bytes 331784 | tf_op jit(solution)/shard_map/ppermute | solution.py:57
  59.9 0.4 collective-permute-start.6
  60.3 0.2 collective-permute-start.7
  60.5 6.0 %up_grad.1 = (bf16[2048,3584]{1,0:T(8,128)(2,1)}, f32[8,128]{1,0:T(8,128)S(1)}) custom-call(bf16[48,1152]{1,0:T(8,128)(2,1)S(1)} %get-tuple-element.62.after.refs_0_, bf16[256,2048]{1,0:T(8,128)(2,1)S(1)} %get-tuple-element.63.left, bf16[256,3584]{1,0:T(8,128)(2,1)S(1)} %get-tuple-element.61.up_grad.right), custom_call_target="tpu_custom_call" | custom-call | bytes 256 | tf_op jit(solution)/shard_map/up_grad/pallas_call | solution.py:355
  66.6 2.4 %collective-permute-start.10 = (bf16[48,1024]{1,0:T(8,128)(2,1)S(1)}, bf16[48,1024]{1,0:T(8,128)(2,1)S(1)}, u32[]{:S(2)}, u32[]{:S(2)}) collective-permute-start(bf16[48,1024]{1,0:T(8,128)(2,1)S(1)} %get-tuple-element.76), channel_id=1, source_target_pairs={{0,8},{4,12},{8,0},{12,4},{1,9},{5,13},{9,1},{13,5},{2,10},{6,14},... | collective-permute-start | bytes 294920 | tf_op jit(solution)/shard_map/ppermute | solution.py:57
  68.9 1.9 %collective-permute-start.11 = (bf16[48,1024]{1,0:T(8,128)(2,1)S(1)}, bf16[48,1024]{1,0:T(8,128)(2,1)S(1)}, u32[]{:S(2)}, u32[]{:S(2)}) collective-permute-start(bf16[48,1024]{1,0:T(8,128)(2,1)S(1)} %get-tuple-element.77), channel_id=1, source_target_pairs={{0,4},{4,8},{8,12},{12,0},{1,5},{5,9},{9,13},{13,1},{2,6},{6,10},{... | collective-permute-start | bytes 294920 | tf_op jit(solution)/shard_map/ppermute | solution.py:57
  70.8 1.9 %collective-permute-start.9 = (bf16[48,1024]{1,0:T(8,128)(2,1)S(1)}, bf16[48,1024]{1,0:T(8,128)(2,1)S(1)}, u32[]{:S(2)}, u32[]{:S(2)}) collective-permute-start(bf16[48,1024]{1,0:T(8,128)(2,1)S(1)} %get-tuple-element.75), channel_id=1, source_target_pairs={{0,12},{4,0},{8,4},{12,8},{1,13},{5,1},{9,5},{13,9},{2,14},{6,2},{... | collective-permute-start | bytes 294920 | tf_op jit(solution)/shard_map/ppermute | solution.py:57
  72.7 0.6 combine_router.1.after.refs_0_
  73.4 1.6 %collective-permute-start.14 = (bf16[128,1152]{1,0:T(8,128)(2,1)S(1)}, bf16[128,1152]{1,0:T(8,128)(2,1)S(1)}, u32[]{:S(2)}, u32[]{:S(2)}) collective-permute-start(bf16[128,1152]{1,0:T(8,128)(2,1)S(1)} %combine_router.1.after.refs_0_), channel_id=1, source_target_pairs={{0,2},{2,0},{1,3},{3,1},{4,6},{6,4},{5,7},{7,5},{8,10},{10,8},{9,1... | collective-permute-start | bytes 884744 | tf_op jit(solution)/shard_map/ppermute | solution.py:57
  74.9 6.0 %gate_grad.1 = (bf16[2048,3584]{1,0:T(8,128)(2,1)}, f32[8,128]{1,0:T(8,128)S(1)}) custom-call(bf16[128,1152]{1,0:T(8,128)(2,1)S(1)} %combine_router.1.after.refs_0_, bf16[256,2048]{1,0:T(8,128)(2,1)S(1)} %get-tuple-element.63.left, bf16[256,3584]{1,0:T(8,128)(2,1)S(1)} %get-tuple-element.60.gate_grad.right), custom_call_target="tpu_custom_call" | custom-call | bytes 256 | tf_op jit(solution)/shard_map/gate_grad/pallas_call | solution.py:355
  80.9 0.5 combine.1.after.refs_0_
  81.4 0.6 collective-permute-start.12
  82.0 0.5 collective-permute-start.16
  82.5 6.0 %down_grad.1 = (bf16[3584,2048]{1,0:T(8,128)(2,1)}, f32[8,128]{1,0:T(8,128)S(1)}) custom-call(bf16[128,1024]{1,0:T(8,128)(2,1)S(1)} %combine.1.after.refs_0_, bf16[256,3584]{1,0:T(8,128)(2,1)S(1)} %get-tuple-element.56.hidden.left, bf16[256,2048]{1,0:T(8,128)(2,1)S(1)} %get-tuple-element.78.right), custom_call_target="tpu_custom_call" | custom-call | bytes 256 | tf_op jit(solution)/shard_map/down_grad/pallas_call | solution.py:355
  88.7 1.5 %collective-permute-done.13.layer_other = bf16[128,1024]{1,0:T(8,128)(2,1)S(1)} collective-permute-done((bf16[128,1024]{1,0:T(8,128)(2,1)S(1)}, bf16[128,1024]{1,0:T(8,128)(2,1)S(1)}, u32[]{:S(2)}, u32[]{:S(2)}) %collective-permute-start.13) | collective-permute-done | bytes 262176 | tf_op jit(solution)/shard_map/ppermute | solution.py:57
  90.2 1.3 %finish.1 = (bf16[128,2048]{1,0:T(8,128)(2,1)}, bf16[128,2048]{1,0:T(8,128)(2,1)}, f32[2,128]{1,0:T(2,128)}) custom-call(bf16[128,1024]{1,0:T(8,128)(2,1)S(1)} %add_pieces.1.layer_own, bf16[128,1024]{1,0:T(8,128)(2,1)S(1)} %collective-permute-done.13.layer_other, bf16[128,1152]{1,0:T(8,128)(2,1)S(1)} %combine_router.1.after.refs_0_, ...), custom_call_target="tpu_custom_call" | custom-call | bytes 1048576 | tf_op jit(solution)/shard_map/finish/pallas_call | solution.py:513
  (19 shorter events, 0.3 us)
Async XLA Ops:
  2.9 17.6 %collective-permute-start = (bf16[48,2176]{1,0:T(8,128)(2,1)S(1)}, bf16[48,2176]{1,0:T(8,128)(2,1)S(1)}, u32[]{:S(2)}, u32[]{:S(2)}) collective-permute-start(bf16[48,2176]{1,0:T(8,128)(2,1)S(1)} %get-tuple-element.50), channel_id=1, source_target_pairs={{0,4},{4,8},{8,12},{12,0},{1,5},{5,9},{9,13},{13,1},{2,6},{6,10},{... | collective-permute-start | bytes 626696 | tf_op jit(solution)/shard_map/ppermute | solution.py:57
  6.0 16.3 %collective-permute-start.1 = (bf16[48,2176]{1,0:T(8,128)(2,1)S(1)}, bf16[48,2176]{1,0:T(8,128)(2,1)S(1)}, u32[]{:S(2)}, u32[]{:S(2)}) collective-permute-start(bf16[48,2176]{1,0:T(8,128)(2,1)S(1)} %get-tuple-element.51), channel_id=1, source_target_pairs={{0,8},{4,12},{8,0},{12,4},{1,9},{5,13},{9,1},{13,5},{2,10},{6,14},... | collective-permute-start | bytes 626696 | tf_op jit(solution)/shard_map/ppermute | solution.py:57
  8.6 13.7 %collective-permute-start.2 = (bf16[48,2176]{1,0:T(8,128)(2,1)S(1)}, bf16[48,2176]{1,0:T(8,128)(2,1)S(1)}, u32[]{:S(2)}, u32[]{:S(2)}) collective-permute-start(bf16[48,2176]{1,0:T(8,128)(2,1)S(1)} %get-tuple-element.52), channel_id=1, source_target_pairs={{0,12},{4,0},{8,4},{12,8},{1,13},{5,1},{9,5},{13,9},{2,14},{6,2},{... | collective-permute-start | bytes 626696 | tf_op jit(solution)/shard_map/ppermute | solution.py:57
  22.3 2.1 %collective-permute-start.3 = (bf16[144,2176]{1,0:T(8,128)(2,1)S(1)}, bf16[144,2176]{1,0:T(8,128)(2,1)S(1)}, u32[]{:S(2)}, u32[]{:S(2)}) collective-permute-start(bf16[144,2176]{1,0:T(8,128)(2,1)S(1)} %stack.1.direct), channel_id=1, source_target_pairs={{0,1},{1,0},{2,3},{3,2},{4,5},{5,4},{6,7},{7,6},{8,9},{9,8},{10,11... | collective-permute-start | bytes 1880072 | tf_op jit(solution)/shard_map/ppermute | solution.py:57
  48.5 5.2 %collective-permute-start.4 = (bf16[192,1024]{1,0:T(8,128)(2,1)S(1)}, bf16[192,1024]{1,0:T(8,128)(2,1)S(1)}, u32[]{:S(2)}, u32[]{:S(2)}) collective-permute-start(bf16[192,1024]{1,0:T(8,128)(2,1)S(1)} %input_send.1), channel_id=1, source_target_pairs={{0,1},{1,0},{2,3},{3,2},{4,5},{5,4},{6,7},{7,6},{8,9},{9,8},{10,11... | collective-permute-start | bytes 1179656 | tf_op jit(solution)/shard_map/ppermute | solution.py:57
  48.7 17.8 %collective-permute-start.8 = (bf16[192,1024]{1,0:T(8,128)(2,1)S(1)}, bf16[192,1024]{1,0:T(8,128)(2,1)S(1)}, u32[]{:S(2)}, u32[]{:S(2)}) collective-permute-start(bf16[192,1024]{1,0:T(8,128)(2,1)S(1)} %get-tuple-element.73), channel_id=1, source_target_pairs={{0,1},{1,0},{2,3},{3,2},{4,5},{5,4},{6,7},{7,6},{8,9},{9,8},{10,11... | collective-permute-start | bytes 1179656 | tf_op jit(solution)/shard_map/ppermute | solution.py:57
  53.8 17.0 %collective-permute-start.5 = (bf16[48,1152]{1,0:T(8,128)(2,1)S(1)}, bf16[48,1152]{1,0:T(8,128)(2,1)S(1)}, u32[]{:S(2)}, u32[]{:S(2)}) collective-permute-start(bf16[48,1152]{1,0:T(8,128)(2,1)S(1)} %get-tuple-element.67), channel_id=1, source_target_pairs={{0,12},{4,0},{8,4},{12,8},{1,13},{5,1},{9,5},{13,9},{2,14},{6,2},{... | collective-permute-start | bytes 331784 | tf_op jit(solution)/shard_map/ppermute | solution.py:57
  59.9 12.9 %collective-permute-start.6 = (bf16[48,1152]{1,0:T(8,128)(2,1)S(1)}, bf16[48,1152]{1,0:T(8,128)(2,1)S(1)}, u32[]{:S(2)}, u32[]{:S(2)}) collective-permute-start(bf16[48,1152]{1,0:T(8,128)(2,1)S(1)} %get-tuple-element.68), channel_id=1, source_target_pairs={{0,8},{4,12},{8,0},{12,4},{1,9},{5,13},{9,1},{13,5},{2,10},{6,14},... | collective-permute-start | bytes 331784 | tf_op jit(solution)/shard_map/ppermute | solution.py:57
  60.3 12.4 %collective-permute-start.7 = (bf16[48,1152]{1,0:T(8,128)(2,1)S(1)}, bf16[48,1152]{1,0:T(8,128)(2,1)S(1)}, u32[]{:S(2)}, u32[]{:S(2)}) collective-permute-start(bf16[48,1152]{1,0:T(8,128)(2,1)S(1)} %get-tuple-element.69), channel_id=1, source_target_pairs={{0,4},{4,8},{8,12},{12,0},{1,5},{5,9},{9,13},{13,1},{2,6},{6,10},{... | collective-permute-start | bytes 331784 | tf_op jit(solution)/shard_map/ppermute | solution.py:57
  66.6 14.3 %collective-permute-start.10 = (bf16[48,1024]{1,0:T(8,128)(2,1)S(1)}, bf16[48,1024]{1,0:T(8,128)(2,1)S(1)}, u32[]{:S(2)}, u32[]{:S(2)}) collective-permute-start(bf16[48,1024]{1,0:T(8,128)(2,1)S(1)} %get-tuple-element.76), channel_id=1, source_target_pairs={{0,8},{4,12},{8,0},{12,4},{1,9},{5,13},{9,1},{13,5},{2,10},{6,14},... | collective-permute-start | bytes 294920 | tf_op jit(solution)/shard_map/ppermute | solution.py:57
  68.9 12.0 %collective-permute-start.11 = (bf16[48,1024]{1,0:T(8,128)(2,1)S(1)}, bf16[48,1024]{1,0:T(8,128)(2,1)S(1)}, u32[]{:S(2)}, u32[]{:S(2)}) collective-permute-start(bf16[48,1024]{1,0:T(8,128)(2,1)S(1)} %get-tuple-element.77), channel_id=1, source_target_pairs={{0,4},{4,8},{8,12},{12,0},{1,5},{5,9},{9,13},{13,1},{2,6},{6,10},{... | collective-permute-start | bytes 294920 | tf_op jit(solution)/shard_map/ppermute | solution.py:57
  70.8 10.1 %collective-permute-start.9 = (bf16[48,1024]{1,0:T(8,128)(2,1)S(1)}, bf16[48,1024]{1,0:T(8,128)(2,1)S(1)}, u32[]{:S(2)}, u32[]{:S(2)}) collective-permute-start(bf16[48,1024]{1,0:T(8,128)(2,1)S(1)} %get-tuple-element.75), channel_id=1, source_target_pairs={{0,12},{4,0},{8,4},{12,8},{1,13},{5,1},{9,5},{13,9},{2,14},{6,2},{... | collective-permute-start | bytes 294920 | tf_op jit(solution)/shard_map/ppermute | solution.py:57
  73.4 8.6 %collective-permute-start.14 = (bf16[128,1152]{1,0:T(8,128)(2,1)S(1)}, bf16[128,1152]{1,0:T(8,128)(2,1)S(1)}, u32[]{:S(2)}, u32[]{:S(2)}) collective-permute-start(bf16[128,1152]{1,0:T(8,128)(2,1)S(1)} %combine_router.1.after.refs_0_), channel_id=1, source_target_pairs={{0,2},{2,0},{1,3},{3,1},{4,6},{6,4},{5,7},{7,5},{8,10},{10,8},{9,1... | collective-permute-start | bytes 884744 | tf_op jit(solution)/shard_map/ppermute | solution.py:57
  81.4 7.1 %collective-permute-start.12 = (bf16[128,1024]{1,0:T(8,128)(2,1)S(1)}, bf16[128,1024]{1,0:T(8,128)(2,1)S(1)}, u32[]{:S(2)}, u32[]{:S(2)}) collective-permute-start(bf16[128,1024]{1,0:T(8,128)(2,1)S(1)} %combine.1.after.refs_0_), channel_id=1, source_target_pairs={{0,2},{2,0},{1,3},{3,1},{4,6},{6,4},{5,7},{7,5},{8,10},{10,8},{9,1... | collective-permute-start | bytes 786440 | tf_op jit(solution)/shard_map/ppermute | solution.py:57
  82.0 6.7 %collective-permute-start.15 = (bf16[128,1152]{1,0:T(8,128)(2,1)S(1)}, bf16[128,1152]{1,0:T(8,128)(2,1)S(1)}, u32[]{:S(2)}, u32[]{:S(2)}) collective-permute-start(bf16[128,1152]{1,0:T(8,128)(2,1)S(1)} %combine_router.1.after.refs_0_), channel_id=1, source_target_pairs={{0,1},{1,0},{2,3},{3,2},{4,5},{5,4},{6,7},{7,6},{8,9},{9,8},{10,11... | collective-permute-start | bytes 884744 | tf_op jit(solution)/shard_map/ppermute | solution.py:57
  82.0 8.2 %collective-permute-start.16 = (bf16[128,1152]{1,0:T(8,128)(2,1)S(1)}, bf16[128,1152]{1,0:T(8,128)(2,1)S(1)}, u32[]{:S(2)}, u32[]{:S(2)}) collective-permute-start(bf16[128,1152]{1,0:T(8,128)(2,1)S(1)} %collective-permute-done.14.refs_1_), channel_id=1, source_target_pairs={{0,1},{1,0},{2,3},{3,2},{4,5},{5,4},{6,7},{7,6},{8,9},{9,8},{10,11... | collective-permute-start | bytes 884744 | tf_op jit(solution)/shard_map/ppermute | solution.py:57
  88.6 1.6 %collective-permute-start.13 = (bf16[128,1024]{1,0:T(8,128)(2,1)S(1)}, bf16[128,1024]{1,0:T(8,128)(2,1)S(1)}, u32[]{:S(2)}, u32[]{:S(2)}) collective-permute-start(bf16[128,1024]{1,0:T(8,128)(2,1)S(1)} %add_pieces.1.layer_own), channel_id=1, source_target_pairs={{0,1},{1,0},{2,3},{3,2},{4,5},{5,4},{6,7},{7,6},{8,9},{9,8},{10,11... | collective-permute-start | bytes 786440 | tf_op jit(solution)/shard_map/ppermute | solution.py:57

commit v5 on v4

--- a/solution.py
+++ b/solution.py
@@ -273,7 +273,7 @@
     hid, width = down.shape
     half = width // 2
     slots = n * CAP
-    tile = tile_of(hid, 256)
+    tile = tile_of(hid, 512)
     return pl.pallas_call(
         middle_body,
         out_shape=[
@@ -290,8 +290,8 @@
             pltpu.VMEM((slots, width), BF16),
             pltpu.VMEM((slots, width), F32),
             pltpu.VMEM((slots, LANES), F32),
-            pltpu.VMEM((4, tile, width), BF16),
-            pltpu.SemaphoreType.DMA((4,)),
+            pltpu.VMEM((2, tile, width), BF16),
+            pltpu.SemaphoreType.DMA((2,)),
         ],
         input_output_aliases={5: 2, 6: 1},
         compiler_params=params(9, slots),

time: 91.7 us -> 90.4 us (0.986)
  Pallas kernels: 62.1 us -> 60.7 us
    pallas_call x1, Pallas kernels: 13 us -> 11.6 us  [middle(): pl.pallas_call(middle_body, out_shape=[pltpu.VMEM((padded(slots), width),...]
where the time goes in v5:
time: 90.4 us; the launch traced here: 90.1 us
  Pallas kernels  60.7 us (67%)
  starting transfers between devices  23.2 us (26%)
  waiting for transfers between devices  5.34 us (6%)
    ppermute x17, starting transfers between devices, shift(): lax.ppermute(value, axis, [(j, (j + step) % count) for j in range(count)])  23.2 us
    pallas_call x3, Pallas kernels, weight_grad(): pl.pallas_call(weight_grad_body, out_shape=[pltpu.HBM((rows, columns), BF...  17.9 us
    pallas_call x1, Pallas kernels, middle(): pl.pallas_call(middle_body, out_shape=[pltpu.VMEM((padded(slots), width),...  11.6 us
    pallas_call x2, Pallas kernels, load(): pl.pallas_call(load_body, out_shape=[pltpu.VMEM(weight.shape, BF16), jax....  10.6 us
    pallas_call x2, Pallas kernels, input_part(): pl.pallas_call(functools.partial(input_body, mine), out_shape=jax.ShapeDt...  9.25 us
    pallas_call x1, Pallas kernels, forward(): pl.pallas_call(functools.partial(forward_body, slots), out_shape=[pltpu.V...  6.43 us
    ppermute x17, waiting for transfers between devices, shift(): lax.ppermute(value, axis, [(j, (j + step) % count) for j in range(count)])  5.34 us
    pallas_call x1, Pallas kernels, pick(): pl.pallas_call(functools.partial(pick_body, n, hid, lax.axis_size(('dp',...  2.28 us
  transfers between devices with their start and end apart: 17, of which 3 were waited for; matrix products, arithmetic and copies ran while one was open for 0% of the time, Pallas kernels for 38%

profile of v5, /device:TPU:0, one launch (start us, length us, event | category | flops | bytes accessed | tf_op | source)
XLA Modules:
  0.0 90.1 jit_solution(7422124537711739280)
XLA Ops:
  0.6 2.3 %pick.1 = (bf16[48,2048]{1,0:T(8,128)(2,1)S(1)}, bf16[48,2048]{1,0:T(8,128)(2,1)S(1)}, bf16[48,128]{1,0:T(8,128)(2,1)S(1)}, bf16[48,2176]{1,0:T(8,128)(2,1)S(1)}...) custom-call(s32[2,128]{1,0:T(2,128)} %bitcast.3, ...), custom_call_target="tpu_custom_call" | custom-call | flops 201326592 | bytes 2097152 | tf_op jit(solution)/shard_map/pick/pallas_call | solution.py:110
  2.9 3.1 %collective-permute-start = (bf16[48,2176]{1,0:T(8,128)(2,1)S(1)}, bf16[48,2176]{1,0:T(8,128)(2,1)S(1)}, u32[]{:S(2)}, u32[]{:S(2)}) collective-permute-start(bf16[48,2176]{1,0:T(8,128)(2,1)S(1)} %get-tuple-element.50), channel_id=1, source_target_pairs={{0,4},{4,8},{8,12},{12,0},{1,5},{5,9},{9,13},{13,1},{2,6},{6,10},{... | collective-permute-start | bytes 626696 | tf_op jit(solution)/shard_map/ppermute | solution.py:57
  6.0 2.6 %collective-permute-start.1 = (bf16[48,2176]{1,0:T(8,128)(2,1)S(1)}, bf16[48,2176]{1,0:T(8,128)(2,1)S(1)}, u32[]{:S(2)}, u32[]{:S(2)}) collective-permute-start(bf16[48,2176]{1,0:T(8,128)(2,1)S(1)} %get-tuple-element.51), channel_id=1, source_target_pairs={{0,8},{4,12},{8,0},{12,4},{1,9},{5,13},{9,1},{13,5},{2,10},{6,14},... | collective-permute-start | bytes 626696 | tf_op jit(solution)/shard_map/ppermute | solution.py:57
  8.6 1.3 %collective-permute-start.2 = (bf16[48,2176]{1,0:T(8,128)(2,1)S(1)}, bf16[48,2176]{1,0:T(8,128)(2,1)S(1)}, u32[]{:S(2)}, u32[]{:S(2)}) collective-permute-start(bf16[48,2176]{1,0:T(8,128)(2,1)S(1)} %get-tuple-element.52), channel_id=1, source_target_pairs={{0,12},{4,0},{8,4},{12,8},{1,13},{5,1},{9,5},{13,9},{2,14},{6,2},{... | collective-permute-start | bytes 626696 | tf_op jit(solution)/shard_map/ppermute | solution.py:57
  9.9 5.3 %load.2 = (bf16[2048,3584]{1,0:T(8,128)(2,1)S(1)}, f32[8,128]{1,0:T(8,128)S(1)}) custom-call(bf16[48,128]{1,0:T(8,128)(2,1)S(1)} %get-tuple-element.47.after.coef_own, bf16[2048,3584]{1,0:T(8,128)(2,1)} %weight.2), custom_call_target="tpu_custom_call" | custom-call | bytes 256 | tf_op jit(solution)/shard_map/load/pallas_call | solution.py:134
  15.2 5.3 %load.3 = (bf16[2048,3584]{1,0:T(8,128)(2,1)S(1)}, f32[8,128]{1,0:T(8,128)S(1)}) custom-call(f32[8,128]{1,0:T(8,128)S(1)} %get-tuple-element.48.after, bf16[2048,3584]{1,0:T(8,128)(2,1)} %weight.3), custom_call_target="tpu_custom_call" | custom-call | bytes 256 | tf_op jit(solution)/shard_map/load/pallas_call | solution.py:134
  20.5 1.7 %collective-permute-done.1.refs_1_ = bf16[48,2176]{1,0:T(8,128)(2,1)S(1)} collective-permute-done((bf16[48,2176]{1,0:T(8,128)(2,1)S(1)}, bf16[48,2176]{1,0:T(8,128)(2,1)S(1)}, u32[]{:S(2)}, u32[]{:S(2)}) %collective-permute-start.1) | collective-permute-done | bytes 208928 | tf_op jit(solution)/shard_map/ppermute | solution.py:57
  22.3 0.1 collective-permute-start.3
  22.4 2.0 %collective-permute-done.3.other = bf16[144,2176]{1,0:T(8,128)(2,1)S(1)} collective-permute-done((bf16[144,2176]{1,0:T(8,128)(2,1)S(1)}, bf16[144,2176]{1,0:T(8,128)(2,1)S(1)}, u32[]{:S(2)}, u32[]{:S(2)}) %collective-permute-start.3) | collective-permute-done | bytes 626720 | tf_op jit(solution)/shard_map/ppermute | solution.py:57
  24.4 6.4 %forward.1 = (bf16[256,2048]{1,0:T(8,128)(2,1)S(1)}, bf16[256,3584]{1,0:T(8,128)(2,1)S(1)}, bf16[256,3584]{1,0:T(8,128)(2,1)S(1)}, bf16[256,3584]{1,0:T(8,128)(2,1)S(1)}) custom-call(bf16[48,2048]{1,0:T(8,128)(2,1)S(1)} %get-tuple-element.53.own, bf16[144,2176]{1,0:T(8,128)(2,1)S(1)} %stack.1.direct, bf16[144,2176]{1,0:T(8,128)(2,1)S(1)} %collective-permute-done.3.other, ...), custom_call_target="tpu_custom_call" | custom-call | bytes 786432 | tf_op jit(solution)/shard_map/forward/pallas_call | solution.py:198
  30.9 11.6 %middle.1 = (bf16[256,2048]{1,0:T(8,128)(2,1)S(1)}, bf16[256,3584]{1,0:T(8,128)(2,1)S(1)}, bf16[256,3584]{1,0:T(8,128)(2,1)S(1)}, f32[192,128]{1,0:T(8,128)S(1)}...) custom-call(bf16[48,2048]{1,0:T(8,128)(2,1)S(1)} %get-tuple-element.46.own,, ...), custom_call_target="tpu_custom_call", output_to_operand_aliasing={{2}: (5, {}), {1}: (6, {})} | custom-call | flops 5637144576 | bytes 14680064 | tf_op jit(solution)/shard_map/middle/pallas_call | solution.py:277
  42.5 4.6 %input_send.1 = bf16[192,1024]{1,0:T(8,128)(2,1)S(1)} custom-call(bf16[256,3584]{1,0:T(8,128)(2,1)S(1)} %get-tuple-element.60.gate_grad.right, bf16[256,3584]{1,0:T(8,128)(2,1)S(1)} %get-tuple-element.61.up_grad.right, bf16[2048,3584]{1,0:T(8,128)(2,1)S(1)} %get-tuple-element.54.gate_w, bf16[2048,3584]{1,0:T(8,128)(2,1)S(1)} %get-tuple-element.55.up_w), custom_call_target="tpu_custom_call" | custom-call | flops 2818572288 | bytes 786432 | tf_op jit(solution)/shard_map/input_send/pallas_call | solution.py:316
  47.1 0.2 collective-permute-start.4
  47.3 0.4 collective-permute-start.8
  47.7 4.6 %input_keep.1.keep = f32[192,1024]{1,0:T(8,128)S(1)} custom-call(bf16[256,3584]{1,0:T(8,128)(2,1)S(1)} %get-tuple-element.60.gate_grad.right, bf16[256,3584]{1,0:T(8,128)(2,1)S(1)} %get-tuple-element.61.up_grad.right, bf16[2048,3584]{1,0:T(8,128)(2,1)S(1)} %get-tuple-element.54.gate_w, bf16[2048,3584]{1,0:T(8,128)(2,1)S(1)} %get-tuple-element.55.up_w), custom_call_target="tpu_custom_call" | custom-call | flops 2818572288 | bytes 786432 | tf_op jit(solution)/shard_map/input_keep/pallas_call | solution.py:316
  52.3 0.1 merge.2
  52.4 6.0 %collective-permute-start.5 = (bf16[48,1152]{1,0:T(8,128)(2,1)S(1)}, bf16[48,1152]{1,0:T(8,128)(2,1)S(1)}, u32[]{:S(2)}, u32[]{:S(2)}) collective-permute-start(bf16[48,1152]{1,0:T(8,128)(2,1)S(1)} %get-tuple-element.67), channel_id=1, source_target_pairs={{0,12},{4,0},{8,4},{12,8},{1,13},{5,1},{9,5},{13,9},{2,14},{6,2},{... | collective-permute-start | bytes 331784 | tf_op jit(solution)/shard_map/ppermute | solution.py:57
  58.5 0.4 collective-permute-start.6
  58.9 0.2 collective-permute-start.7
  59.1 6.0 %up_grad.1 = (bf16[2048,3584]{1,0:T(8,128)(2,1)}, f32[8,128]{1,0:T(8,128)S(1)}) custom-call(bf16[48,1152]{1,0:T(8,128)(2,1)S(1)} %get-tuple-element.62.after.refs_0_, bf16[256,2048]{1,0:T(8,128)(2,1)S(1)} %get-tuple-element.63.left, bf16[256,3584]{1,0:T(8,128)(2,1)S(1)} %get-tuple-element.61.up_grad.right), custom_call_target="tpu_custom_call" | custom-call | bytes 256 | tf_op jit(solution)/shard_map/up_grad/pallas_call | solution.py:355
  65.2 2.4 %collective-permute-start.10 = (bf16[48,1024]{1,0:T(8,128)(2,1)S(1)}, bf16[48,1024]{1,0:T(8,128)(2,1)S(1)}, u32[]{:S(2)}, u32[]{:S(2)}) collective-permute-start(bf16[48,1024]{1,0:T(8,128)(2,1)S(1)} %get-tuple-element.76), channel_id=1, source_target_pairs={{0,8},{4,12},{8,0},{12,4},{1,9},{5,13},{9,1},{13,5},{2,10},{6,14},... | collective-permute-start | bytes 294920 | tf_op jit(solution)/shard_map/ppermute | solution.py:57
  67.5 1.9 %collective-permute-start.11 = (bf16[48,1024]{1,0:T(8,128)(2,1)S(1)}, bf16[48,1024]{1,0:T(8,128)(2,1)S(1)}, u32[]{:S(2)}, u32[]{:S(2)}) collective-permute-start(bf16[48,1024]{1,0:T(8,128)(2,1)S(1)} %get-tuple-element.77), channel_id=1, source_target_pairs={{0,4},{4,8},{8,12},{12,0},{1,5},{5,9},{9,13},{13,1},{2,6},{6,10},{... | collective-permute-start | bytes 294920 | tf_op jit(solution)/shard_map/ppermute | solution.py:57
  69.4 1.9 %collective-permute-start.9 = (bf16[48,1024]{1,0:T(8,128)(2,1)S(1)}, bf16[48,1024]{1,0:T(8,128)(2,1)S(1)}, u32[]{:S(2)}, u32[]{:S(2)}) collective-permute-start(bf16[48,1024]{1,0:T(8,128)(2,1)S(1)} %get-tuple-element.75), channel_id=1, source_target_pairs={{0,12},{4,0},{8,4},{12,8},{1,13},{5,1},{9,5},{13,9},{2,14},{6,2},{... | collective-permute-start | bytes 294920 | tf_op jit(solution)/shard_map/ppermute | solution.py:57
  71.3 0.6 combine_router.1.after.refs_0_
  72.0 1.6 %collective-permute-start.14 = (bf16[128,1152]{1,0:T(8,128)(2,1)S(1)}, bf16[128,1152]{1,0:T(8,128)(2,1)S(1)}, u32[]{:S(2)}, u32[]{:S(2)}) collective-permute-start(bf16[128,1152]{1,0:T(8,128)(2,1)S(1)} %combine_router.1.after.refs_0_), channel_id=1, source_target_pairs={{0,2},{2,0},{1,3},{3,1},{4,6},{6,4},{5,7},{7,5},{8,10},{10,8},{9,1... | collective-permute-start | bytes 884744 | tf_op jit(solution)/shard_map/ppermute | solution.py:57
  73.5 6.0 %gate_grad.1 = (bf16[2048,3584]{1,0:T(8,128)(2,1)}, f32[8,128]{1,0:T(8,128)S(1)}) custom-call(bf16[128,1152]{1,0:T(8,128)(2,1)S(1)} %combine_router.1.after.refs_0_, bf16[256,2048]{1,0:T(8,128)(2,1)S(1)} %get-tuple-element.63.left, bf16[256,3584]{1,0:T(8,128)(2,1)S(1)} %get-tuple-element.60.gate_grad.right), custom_call_target="tpu_custom_call" | custom-call | bytes 256 | tf_op jit(solution)/shard_map/gate_grad/pallas_call | solution.py:355
  79.5 0.5 combine.1.after.refs_0_
  80.0 0.6 collective-permute-start.12
  80.6 0.5 collective-permute-start.16
  81.1 6.0 %down_grad.1 = (bf16[3584,2048]{1,0:T(8,128)(2,1)}, f32[8,128]{1,0:T(8,128)S(1)}) custom-call(bf16[128,1024]{1,0:T(8,128)(2,1)S(1)} %combine.1.after.refs_0_, bf16[256,3584]{1,0:T(8,128)(2,1)S(1)} %get-tuple-element.56.hidden.left, bf16[256,2048]{1,0:T(8,128)(2,1)S(1)} %get-tuple-element.78.right), custom_call_target="tpu_custom_call" | custom-call | bytes 256 | tf_op jit(solution)/shard_map/down_grad/pallas_call | solution.py:355
  87.3 1.5 %collective-permute-done.13.layer_other = bf16[128,1024]{1,0:T(8,128)(2,1)S(1)} collective-permute-done((bf16[128,1024]{1,0:T(8,128)(2,1)S(1)}, bf16[128,1024]{1,0:T(8,128)(2,1)S(1)}, u32[]{:S(2)}, u32[]{:S(2)}) %collective-permute-start.13) | collective-permute-done | bytes 262176 | tf_op jit(solution)/shard_map/ppermute | solution.py:57
  88.8 1.3 %finish.1 = (bf16[128,2048]{1,0:T(8,128)(2,1)}, bf16[128,2048]{1,0:T(8,128)(2,1)}, f32[2,128]{1,0:T(2,128)}) custom-call(bf16[128,1024]{1,0:T(8,128)(2,1)S(1)} %add_pieces.1.layer_own, bf16[128,1024]{1,0:T(8,128)(2,1)S(1)} %collective-permute-done.13.layer_other, bf16[128,1152]{1,0:T(8,128)(2,1)S(1)} %combine_router.1.after.refs_0_, ...), custom_call_target="tpu_custom_call" | custom-call | bytes 1048576 | tf_op jit(solution)/shard_map/finish/pallas_call | solution.py:513
  (19 shorter events, 0.3 us)
Async XLA Ops:
  2.9 17.6 %collective-permute-start = (bf16[48,2176]{1,0:T(8,128)(2,1)S(1)}, bf16[48,2176]{1,0:T(8,128)(2,1)S(1)}, u32[]{:S(2)}, u32[]{:S(2)}) collective-permute-start(bf16[48,2176]{1,0:T(8,128)(2,1)S(1)} %get-tuple-element.50), channel_id=1, source_target_pairs={{0,4},{4,8},{8,12},{12,0},{1,5},{5,9},{9,13},{13,1},{2,6},{6,10},{... | collective-permute-start | bytes 626696 | tf_op jit(solution)/shard_map/ppermute | solution.py:57
  6.0 16.3 %collective-permute-start.1 = (bf16[48,2176]{1,0:T(8,128)(2,1)S(1)}, bf16[48,2176]{1,0:T(8,128)(2,1)S(1)}, u32[]{:S(2)}, u32[]{:S(2)}) collective-permute-start(bf16[48,2176]{1,0:T(8,128)(2,1)S(1)} %get-tuple-element.51), channel_id=1, source_target_pairs={{0,8},{4,12},{8,0},{12,4},{1,9},{5,13},{9,1},{13,5},{2,10},{6,14},... | collective-permute-start | bytes 626696 | tf_op jit(solution)/shard_map/ppermute | solution.py:57
  8.6 13.7 %collective-permute-start.2 = (bf16[48,2176]{1,0:T(8,128)(2,1)S(1)}, bf16[48,2176]{1,0:T(8,128)(2,1)S(1)}, u32[]{:S(2)}, u32[]{:S(2)}) collective-permute-start(bf16[48,2176]{1,0:T(8,128)(2,1)S(1)} %get-tuple-element.52), channel_id=1, source_target_pairs={{0,12},{4,0},{8,4},{12,8},{1,13},{5,1},{9,5},{13,9},{2,14},{6,2},{... | collective-permute-start | bytes 626696 | tf_op jit(solution)/shard_map/ppermute | solution.py:57
  22.3 2.1 %collective-permute-start.3 = (bf16[144,2176]{1,0:T(8,128)(2,1)S(1)}, bf16[144,2176]{1,0:T(8,128)(2,1)S(1)}, u32[]{:S(2)}, u32[]{:S(2)}) collective-permute-start(bf16[144,2176]{1,0:T(8,128)(2,1)S(1)} %stack.1.direct), channel_id=1, source_target_pairs={{0,1},{1,0},{2,3},{3,2},{4,5},{5,4},{6,7},{7,6},{8,9},{9,8},{10,11... | collective-permute-start | bytes 1880072 | tf_op jit(solution)/shard_map/ppermute | solution.py:57
  47.1 5.2 %collective-permute-start.4 = (bf16[192,1024]{1,0:T(8,128)(2,1)S(1)}, bf16[192,1024]{1,0:T(8,128)(2,1)S(1)}, u32[]{:S(2)}, u32[]{:S(2)}) collective-permute-start(bf16[192,1024]{1,0:T(8,128)(2,1)S(1)} %input_send.1), channel_id=1, source_target_pairs={{0,1},{1,0},{2,3},{3,2},{4,5},{5,4},{6,7},{7,6},{8,9},{9,8},{10,11... | collective-permute-start | bytes 1179656 | tf_op jit(solution)/shard_map/ppermute | solution.py:57
  47.3 17.8 %collective-permute-start.8 = (bf16[192,1024]{1,0:T(8,128)(2,1)S(1)}, bf16[192,1024]{1,0:T(8,128)(2,1)S(1)}, u32[]{:S(2)}, u32[]{:S(2)}) collective-permute-start(bf16[192,1024]{1,0:T(8,128)(2,1)S(1)} %get-tuple-element.73), channel_id=1, source_target_pairs={{0,1},{1,0},{2,3},{3,2},{4,5},{5,4},{6,7},{7,6},{8,9},{9,8},{10,11... | collective-permute-start | bytes 1179656 | tf_op jit(solution)/shard_map/ppermute | solution.py:57
  52.4 17.0 %collective-permute-start.5 = (bf16[48,1152]{1,0:T(8,128)(2,1)S(1)}, bf16[48,1152]{1,0:T(8,128)(2,1)S(1)}, u32[]{:S(2)}, u32[]{:S(2)}) collective-permute-start(bf16[48,1152]{1,0:T(8,128)(2,1)S(1)} %get-tuple-element.67), channel_id=1, source_target_pairs={{0,12},{4,0},{8,4},{12,8},{1,13},{5,1},{9,5},{13,9},{2,14},{6,2},{... | collective-permute-start | bytes 331784 | tf_op jit(solution)/shard_map/ppermute | solution.py:57
  58.5 12.9 %collective-permute-start.6 = (bf16[48,1152]{1,0:T(8,128)(2,1)S(1)}, bf16[48,1152]{1,0:T(8,128)(2,1)S(1)}, u32[]{:S(2)}, u32[]{:S(2)}) collective-permute-start(bf16[48,1152]{1,0:T(8,128)(2,1)S(1)} %get-tuple-element.68), channel_id=1, source_target_pairs={{0,8},{4,12},{8,0},{12,4},{1,9},{5,13},{9,1},{13,5},{2,10},{6,14},... | collective-permute-start | bytes 331784 | tf_op jit(solution)/shard_map/ppermute | solution.py:57
  58.9 12.4 %collective-permute-start.7 = (bf16[48,1152]{1,0:T(8,128)(2,1)S(1)}, bf16[48,1152]{1,0:T(8,128)(2,1)S(1)}, u32[]{:S(2)}, u32[]{:S(2)}) collective-permute-start(bf16[48,1152]{1,0:T(8,128)(2,1)S(1)} %get-tuple-element.69), channel_id=1, source_target_pairs={{0,4},{4,8},{8,12},{12,0},{1,5},{5,9},{9,13},{13,1},{2,6},{6,10},{... | collective-permute-start | bytes 331784 | tf_op jit(solution)/shard_map/ppermute | solution.py:57
  65.2 14.3 %collective-permute-start.10 = (bf16[48,1024]{1,0:T(8,128)(2,1)S(1)}, bf16[48,1024]{1,0:T(8,128)(2,1)S(1)}, u32[]{:S(2)}, u32[]{:S(2)}) collective-permute-start(bf16[48,1024]{1,0:T(8,128)(2,1)S(1)} %get-tuple-element.76), channel_id=1, source_target_pairs={{0,8},{4,12},{8,0},{12,4},{1,9},{5,13},{9,1},{13,5},{2,10},{6,14},... | collective-permute-start | bytes 294920 | tf_op jit(solution)/shard_map/ppermute | solution.py:57
  67.5 12.0 %collective-permute-start.11 = (bf16[48,1024]{1,0:T(8,128)(2,1)S(1)}, bf16[48,1024]{1,0:T(8,128)(2,1)S(1)}, u32[]{:S(2)}, u32[]{:S(2)}) collective-permute-start(bf16[48,1024]{1,0:T(8,128)(2,1)S(1)} %get-tuple-element.77), channel_id=1, source_target_pairs={{0,4},{4,8},{8,12},{12,0},{1,5},{5,9},{9,13},{13,1},{2,6},{6,10},{... | collective-permute-start | bytes 294920 | tf_op jit(solution)/shard_map/ppermute | solution.py:57
  69.4 10.1 %collective-permute-start.9 = (bf16[48,1024]{1,0:T(8,128)(2,1)S(1)}, bf16[48,1024]{1,0:T(8,128)(2,1)S(1)}, u32[]{:S(2)}, u32[]{:S(2)}) collective-permute-start(bf16[48,1024]{1,0:T(8,128)(2,1)S(1)} %get-tuple-element.75), channel_id=1, source_target_pairs={{0,12},{4,0},{8,4},{12,8},{1,13},{5,1},{9,5},{13,9},{2,14},{6,2},{... | collective-permute-start | bytes 294920 | tf_op jit(solution)/shard_map/ppermute | solution.py:57
  72.0 8.6 %collective-permute-start.14 = (bf16[128,1152]{1,0:T(8,128)(2,1)S(1)}, bf16[128,1152]{1,0:T(8,128)(2,1)S(1)}, u32[]{:S(2)}, u32[]{:S(2)}) collective-permute-start(bf16[128,1152]{1,0:T(8,128)(2,1)S(1)} %combine_router.1.after.refs_0_), channel_id=1, source_target_pairs={{0,2},{2,0},{1,3},{3,1},{4,6},{6,4},{5,7},{7,5},{8,10},{10,8},{9,1... | collective-permute-start | bytes 884744 | tf_op jit(solution)/shard_map/ppermute | solution.py:57
  80.0 7.1 %collective-permute-start.12 = (bf16[128,1024]{1,0:T(8,128)(2,1)S(1)}, bf16[128,1024]{1,0:T(8,128)(2,1)S(1)}, u32[]{:S(2)}, u32[]{:S(2)}) collective-permute-start(bf16[128,1024]{1,0:T(8,128)(2,1)S(1)} %combine.1.after.refs_0_), channel_id=1, source_target_pairs={{0,2},{2,0},{1,3},{3,1},{4,6},{6,4},{5,7},{7,5},{8,10},{10,8},{9,1... | collective-permute-start | bytes 786440 | tf_op jit(solution)/shard_map/ppermute | solution.py:57
  80.6 6.7 %collective-permute-start.15 = (bf16[128,1152]{1,0:T(8,128)(2,1)S(1)}, bf16[128,1152]{1,0:T(8,128)(2,1)S(1)}, u32[]{:S(2)}, u32[]{:S(2)}) collective-permute-start(bf16[128,1152]{1,0:T(8,128)(2,1)S(1)} %combine_router.1.after.refs_0_), channel_id=1, source_target_pairs={{0,1},{1,0},{2,3},{3,2},{4,5},{5,4},{6,7},{7,6},{8,9},{9,8},{10,11... | collective-permute-start | bytes 884744 | tf_op jit(solution)/shard_map/ppermute | solution.py:57
  80.6 8.2 %collective-permute-start.16 = (bf16[128,1152]{1,0:T(8,128)(2,1)S(1)}, bf16[128,1152]{1,0:T(8,128)(2,1)S(1)}, u32[]{:S(2)}, u32[]{:S(2)}) collective-permute-start(bf16[128,1152]{1,0:T(8,128)(2,1)S(1)} %collective-permute-done.14.refs_1_), channel_id=1, source_target_pairs={{0,1},{1,0},{2,3},{3,2},{4,5},{5,4},{6,7},{7,6},{8,9},{9,8},{10,11... | collective-permute-start | bytes 884744 | tf_op jit(solution)/shard_map/ppermute | solution.py:57
  87.2 1.6 %collective-permute-start.13 = (bf16[128,1024]{1,0:T(8,128)(2,1)S(1)}, bf16[128,1024]{1,0:T(8,128)(2,1)S(1)}, u32[]{:S(2)}, u32[]{:S(2)}) collective-permute-start(bf16[128,1024]{1,0:T(8,128)(2,1)S(1)} %add_pieces.1.layer_own), channel_id=1, source_target_pairs={{0,1},{1,0},{2,3},{3,2},{4,5},{5,4},{6,7},{7,6},{8,9},{9,8},{10,11... | collective-permute-start | bytes 786440 | tf_op jit(solution)/shard_map/ppermute | solution.py:57
